TPU v7x, 32 devices: a whole 2x2x4 slice. The times are simulated.
32 devices in a mesh: sub: 8 (over z, x), site: 4 (over y, core).
Axes of the slice: x: 2, y: 2, z: 4, core: 2. Of those that a mesh axis runs over, the one named last changes fastest.
Arguments:
- sgt: bfloat16 [128, 2, 2, 6, 64, 128], P('sub', None, None, None, 'site'), may hold values from -6 to 6
- mechanism: float32 [128, 6], P('sub'), may hold values from -5 to 5
- slip: bfloat16 [128, 64, 2, 128], P('sub'), may hold values from -0.3125 to 0.3125
- point_list: int32 [128], replicated, may hold values from 0 to 127, as said below
- subfault_counts: int32 [8], replicated, may hold values from 1 to 16, 64 in all
Outputs:
- seismograms: bfloat16 [64, 2, 64, 2048], P('sub', None, 'site')
- psa: float32 [64, 2, 64, 40], P('sub', None, 'site')
Inputs may be any that keep to these rules, and one draw needn't show every extreme that they name: `point_list`: every SGT point is named by exactly one subfault slot. Of the 16 slots of each worker w (slots w * 16 to w * 16 + 15), exactly 2 name points of each reader block r (points r * 16 to r * 16 + 15). `subfault_counts`: the counts sum to 64, and the largest is 16. Slots of a worker past its count are not part of the rupture.
All inputs are finite; a program needn't handle non-finite values.
Results may differ from a plain program's by a relative error of at most 0.0049.
Values may be sent and summed in bfloat16 or wider, within the bound.
No kernel may reach another device: no remote copies, remote signals or barrier semaphores. Data moves between devices by JAX's collectives and lax.ppermute only.
A program may use at most 128 MiB of HBM per device.

v0:
```python
import math

import jax
import jax.numpy as jnp
from jax import lax
from jax.sharding import PartitionSpec as P

NT = 2048
PERIODS = 40


damping = 0.05
sample_step = 0.1


def synthesis_basis(freq_count, sample_count):
    freq_ids = jnp.arange(freq_count, dtype=jnp.int32)
    time_ids = jnp.arange(sample_count, dtype=jnp.int32)
    angles = (freq_ids[:, None] * time_ids[None, :] % sample_count).astype(jnp.float32) * (
        2.0 * math.pi / sample_count
    )
    norm_scale = 1.0 / math.sqrt(freq_count)
    return jnp.stack([norm_scale * jnp.cos(angles), -norm_scale * jnp.sin(angles)])


def oscillator_gains(period_count, freq_count, sample_count):
    period_ids = jnp.arange(period_count, dtype=jnp.float32)
    periods = 2.0 * jnp.exp(period_ids * (math.log(5.0) / max(period_count - 1, 1)))
    natural = 2.0 * math.pi / periods
    omega_bins = jnp.arange(freq_count, dtype=jnp.float32) * (
        2.0 * math.pi / (sample_count * sample_step)
    )
    squared_natural = (natural * natural)[:, None]
    real_part = squared_natural - (omega_bins * omega_bins)[None, :]
    imag_part = 2.0 * damping * natural[:, None] * omega_bins[None, :]
    magnitude = real_part * real_part + imag_part * imag_part
    return (-squared_natural * real_part / magnitude, squared_natural * imag_part / magnitude)


def rank_within_reader(readers, workers):
    onehot = (readers[:, :, None] == jnp.arange(workers, dtype=jnp.int32)[None, None, :]).astype(
        jnp.int32
    )
    return jnp.sum(onehot * jnp.cumsum(onehot, axis=1), axis=2) - 1


def project_strain(green_rows, moments):
    combined = moments[:, 0, None, None, None, None] * green_rows[:, :, :, 0].astype(jnp.float32)
    for strain in range(1, 6):
        combined = combined + moments[:, strain, None, None, None, None] * green_rows[
            :, :, :, strain
        ].astype(jnp.float32)
    return combined.astype(jnp.bfloat16)


def contract_slip(projected, slip_real, slip_imag):
    with_real = jnp.einsum(
        "jrcsf,jvf->rvcsf", projected, slip_real, preferred_element_type=jnp.float32
    )
    with_imag = jnp.einsum(
        "jrcsf,jvf->rvcsf", projected, slip_imag, preferred_element_type=jnp.float32
    )
    return jnp.stack([with_real[0] - with_imag[1], with_imag[0] + with_real[1]], axis=2)


def per_device(sgt, mechanism, slip, point_list, subfault_counts):
    workers = lax.axis_size("sub")
    worker = lax.axis_index("sub")
    slot_count = slip.shape[0]
    per_reader = sgt.shape[0]
    capacity = slot_count // workers
    freq_count = sgt.shape[-1]
    table_all = point_list.reshape(workers, slot_count)
    readers = table_all // per_reader
    local_rows = table_all % per_reader
    occurrence = rank_within_reader(readers, workers)
    rank_ids = jnp.arange(capacity, dtype=jnp.int32)
    held_here = readers == worker
    chosen = (held_here[:, None, :] & (occurrence[:, None, :] == rank_ids[None, :, None])).astype(
        jnp.int32
    )
    send_rows = jnp.sum(chosen * local_rows[:, None, :], axis=2).reshape(-1)
    own_readers = lax.dynamic_index_in_dim(readers, worker, 0, keepdims=False)
    own_occ = lax.dynamic_index_in_dim(occurrence, worker, 0, keepdims=False)
    reader_ids = jnp.arange(workers, dtype=jnp.int32)
    matched = (
        (own_readers[None, None, :] == reader_ids[:, None, None])
        & (own_occ[None, None, :] == rank_ids[None, :, None])
    ).astype(jnp.int32)
    slot_order = jnp.sum(
        matched * jnp.arange(slot_count, dtype=jnp.int32)[None, None, :], axis=2
    ).reshape(-1)
    own_count = lax.dynamic_index_in_dim(subfault_counts, worker, 0, keepdims=False)
    live_mask = (jnp.arange(slot_count, dtype=jnp.int32) < own_count).astype(slip.dtype)
    slip_live = slip * live_mask[:, None, None, None]
    slip_arranged = jnp.take(slip_live, slot_order, axis=0)
    slip_real = slip_arranged[:, :, 0]
    slip_imag = slip_arranged[:, :, 1]
    moments_arranged = jnp.take(mechanism, slot_order, axis=0)
    outgoing = jnp.take(sgt, send_rows, axis=0)
    partial_value = contract_slip(
        project_strain(
            lax.all_to_all(outgoing, "sub", split_axis=0, concat_axis=0, tiled=True),
            moments_arranged,
        ),
        slip_real,
        slip_imag,
    )
    basis = synthesis_basis(freq_count, NT)
    spectrum = lax.psum_scatter(partial_value, "sub", scatter_dimension=0, tiled=True)
    motion = jnp.einsum("vcrsf,rft->vcst", spectrum, basis, precision=lax.Precision.HIGHEST)
    gain_real, gain_imag = oscillator_gains(PERIODS, freq_count, NT)
    spec_real = spectrum[:, :, 0]
    spec_imag = spectrum[:, :, 1]
    gain_re = gain_real[:, None, None, None, :]
    gain_im = gain_imag[:, None, None, None, :]
    resp_real = gain_re * spec_real[None] - gain_im * spec_imag[None]
    resp_imag = gain_re * spec_imag[None] + gain_im * spec_real[None]
    response = jnp.stack([resp_real, resp_imag], axis=3).astype(jnp.bfloat16)
    basis_low = basis.astype(jnp.bfloat16)
    response_wave = jnp.einsum(
        "kvcrsf,rft->kvcst", response, basis_low, preferred_element_type=jnp.float32
    )
    peak_values = jnp.max(jnp.abs(response_wave), axis=4)
    return (motion.astype(jnp.bfloat16), jnp.transpose(peak_values, (1, 2, 3, 0)))


def solution(mesh):
    in_specs = (
        P("sub", None, None, None, "site", None),
        P("sub", None),
        P("sub", None, None, None),
        P(),
        P(),
    )
    out_specs = (P("sub", None, "site", None), P("sub", None, "site", None))
    return jax.shard_map(
        per_device, mesh=mesh, in_specs=in_specs, out_specs=out_specs, check_vma=False
    )
```

profile of v0, /device:TPU:0, one launch (start us, length us, event | category | flops | bytes accessed | tf_op | source)
XLA Modules:
  0.0 168.9 jit_solution(7281606898656251647)
XLA Ops:
  7.2 0.0 copy-start
  7.2 0.8 reshape.513
  8.1 0.1 copy.109
  8.1 0.4 fusion.39
  8.6 0.1 copy.110
  8.7 0.1 select_reduce_fusion
  8.8 0.1 copy.116
  8.9 0.1 reshape.517
  9.0 0.1 reshape.516
  9.1 0.1 select_reduce_fusion.1
  9.2 0.1 copy.111
  9.3 0.1 reshape.515
  9.4 0.0 copy-done
  9.4 0.9 gather_fusion.2
  10.3 0.0 copy-start.5
  10.3 0.0 copy-start.6
  10.3 1.4 broadcast_select_fusion
  11.7 7.3 %all-to-all-start = ((bf16[16,2,2,6,16,128]{5,4,3,2,1,0:T(8,128)(2,1)}), bf16[16,2,2,6,16,128]{5,4,3,2,1,0:T(8,128)(2,1)S(1)}, u32[]{:S(2)}, u32[]{:S(2)}) async-start(bf16[16,2,2,6,16,128]{5,4,3,2,1,0:T(8,128)(2,1)} %broadcast_select_fusion), calls=%async_computation | async-start | bytes 3145728 | tf_op jit(solution)/shard_map/all_to_all | solution.py:103
  18.9 0.0 reduce-scatter.2.cloned.1.call-start
  19.0 0.1 reshape.514
  19.1 0.0 copy-done.5
  19.1 0.1 copy.115
  19.2 0.0 copy-done.6
  19.2 0.6 dynamic_slice.16
  19.7 0.6 gather_fusion.1
  20.3 0.7 compare_convert_fusion
  21.0 1.9 %copy_multiply_fusion = bf16[16,64,2,128]{3,1,2,0:T(8,128)(2,1)} fusion(bf16[16,64,2,128]{3,2,1,0:T(2,128)(2,1)} %param.7, bf16[16]{0:T(256)(128)(2,1)S(1)} %compare_convert_fusion), kind=kLoop, calls=%fused_computation.53 | loop fusion | flops 262144 | bytes 1048608 | tf_op jit(solution)/shard_map/mul | solution.py:95
  22.9 2.5 %gather_fusion = bf16[16,64,2,128]{3,1,2,0:T(8,128)(2,1)} fusion(bf16[16,64,2,128]{3,1,2,0:T(8,128)(2,1)} %copy_multiply_fusion, s32[1024]{0:T(1024)S(1)} %pad_clamp_fusion.1), kind=kCustom, calls=%fused_computation | custom fusion | bytes 1048640 | tf_op jit(solution)/shard_map/jit(_take)/gather | solution.py:96
  25.4 2.7 %copy.114 = bf16[16,64,2,128]{1,0,3,2:T(8,128)(2,1)} copy(bf16[16,64,2,128]{3,1,2,0:T(8,128)(2,1)} %gather_fusion) | data formatting | bytes 1048576 | tf_op jit(solution)/shard_map/jit(_take)/gather | solution.py:96
  28.1 0.1 broadcast_select_fusion.2
  28.2 0.3 slice_reduce_fusion.5
  28.4 2.4 %broadcast_select_fusion.1 = bf16[16,64,2,128]{1,0,3,2:T(8,128)(2,1)} fusion(bf16[16,64,2,128]{1,0,3,2:T(8,128)(2,1)} %copy.114, pred[16]{0:T(512)(128)(4,1)S(1)} %compare_and_fusion.1), kind=kLoop, calls=%fused_computation.38 | loop fusion | flops 262144 | bytes 1048592 | tf_op jit(solution)/shard_map/jit(_take)/select_n | solution.py:96
  30.8 25.1 %all-to-all-done = bf16[16,2,2,6,16,128]{5,4,3,2,1,0:T(8,128)(2,1)S(1)} async-done(((bf16[16,2,2,6,16,128]{5,4,3,2,1,0:T(8,128)(2,1)}), bf16[16,2,2,6,16,128]{5,4,3,2,1,0:T(8,128)(2,1)S(1)}, u32[]{:S(2)}, u32[]{:S(2)}) %all-to-all-start) | async-done | bytes 1572896 | tf_op jit(solution)/shard_map/all_to_all | solution.py:103
  55.9 0.4 fusion.18
  56.3 0.0 copy-start.3
  56.3 3.9 %copy.132 = bf16[16,2,2,16,128]{0,3,2,4,1:T(8,128)(2,1)} copy(bf16[16,2,2,16,128]{4,3,2,1,0:T(8,128)(2,1)S(1)} %fusion.18) | data formatting | bytes 524288 | tf_op jit(solution)/shard_map/convert_element_type | solution.py:53
  60.3 3.8 %copy.123 = bf16[16,2,2,16,128]{0,3,2,1,4:T(8,128)(2,1)} copy(bf16[16,2,2,16,128]{4,3,2,1,0:T(8,128)(2,1)S(1)} %fusion.18) | data formatting | bytes 524288 | tf_op jit(solution)/shard_map/convert_element_type | solution.py:53
  64.1 0.0 copy-done.3
  64.1 0.0 copy-start.1
  64.1 2.4 %convolution_bitcast_fusion.1 = f32[2,64,2,16,128]{1,3,2,4,0:T(8,128)S(1)} fusion(bf16[16,2,2,16,128]{0,3,2,4,1:T(8,128)(2,1)} %copy.132, bf16[16,64,2,128]{1,0,3,2:T(8,128)(2,1)S(1)} %copy-done.3), kind=kOutput, calls=%fused_computation.13 | convolution fusion | flops 16777216 | bytes 2883584 | tf_op jit(solution)/shard_map/jrcsf,jvf->rvcsf/dot_general | solution.py:60
  66.5 0.0 copy-done.1
  66.5 0.7 convolution_bitcast_fusion.2
  67.2 0.5 fusion.6
  67.7 0.5 fusion.5
  68.2 2.4 %pad_maximum_fusion = f32[64,2,2,16,128]{0,3,1,4,2:T(8,128)} fusion(f32[64,2,1,16,128]{0,3,1,4,2:T(8,128)S(1)} %fusion.5, f32[64,2,1,16,128]{0,3,1,4,2:T(8,128)S(1)} %fusion.6), kind=kLoop, calls=%fused_computation.10 | loop fusion | flops 524288 | bytes 4194304 | tf_op jit(solution)/shard_map/stack | solution.py:63
  70.6 4.9 %copy.128 = f32[64,2,2,16,128]{4,3,2,1,0:T(8,128)} copy(f32[64,2,2,16,128]{0,3,1,4,2:T(8,128)} %pad_maximum_fusion) | data formatting | bytes 4194304 | tf_op jit(solution)/shard_map/stack | solution.py:63
  75.5 0.0 reduce-scatter.2.cloned.1.call-update
  75.6 0.1 fusion.25
  75.7 5.3 %sine_multiply_fusion = (f32[1,128,2048]{2,1,0:T(8,128)S(1)}, f32[1,128,2048]{2,1,0:T(8,128)}) fusion(), kind=kLoop, calls=%fused_computation.33 | loop fusion | flops 4194304 | bytes 2097152 | tf_op jit(solution)/shard_map/mul | solution.py:23
  81.0 61.4 %reduce-scatter.2.cloned.1.call-done = f32[8,2,2,16,128]{4,3,2,1,0:T(8,128)} async-done(((f32[64,2,2,16,128]{4,3,2,1,0:T(8,128)}), f32[8,2,2,16,128]{4,3,2,1,0:T(8,128)}) %reduce-scatter.2.cloned.1.call-update) | async-done | bytes 262160 | tf_op jit(solution)/shard_map/reduce_scatter | solution.py:110
  142.4 1.0 slice_bitcast_fusion.13
  143.4 0.0 copy-start.2
  143.4 1.5 subtract_convert_fusion
  144.9 0.0 copy-done.2
  144.9 0.0 copy-start.4
  144.9 12.1 %fusion = f32[40,8,2,16]{3,2,1,0:T(2,128)S(1)} fusion(bf16[40,8,2,1,16,128]{5,4,3,2,1,0:T(8,128)(2,1)S(1)} %get-tuple-element.19, bf16[40,8,2,1,16,128]{5,4,3,2,1,0:T(8,128)(2,1)S(1)} %get-tuple-element.18, f32[1,128,2048]{2,1,0:T(8,128)S(1)} %get-tuple-element.26, f32[1,128,2048]{2,1,0:T(8,128)S(1)} %copy-done.2), kind=kOutput, calls=%fused_computation.4 | convolution fusion | flops 10782496768 | bytes 7380992 | tf_op jit(solution)/shard_map/kvcrsf,rft->kvcst/dot_general | solution.py:121
  157.1 0.9 copy.129
  157.9 0.0 copy-done.4
  157.9 4.1 %fusion.4 = bf16[8,2,16,2048]{3,2,1,0:T(8,128)(2,1)} fusion(f32[8,2,2,16,128]{4,3,2,1,0:T(8,128)S(1)} %copy-done.4, f32[1,128,2048]{2,1,0:T(8,128)S(1)} %get-tuple-element.26, f32[1,128,2048]{2,1,0:T(8,128)} %get-tuple-element.27), kind=kOutput, calls=%fused_computation.12 | convolution fusion | flops 1611661312 | bytes 3407872 | tf_op jit(solution)/shard_map/vcrsf,rft->vcst/dot_general | solution.py:111
  (15 shorter events, 0.1 us)
Async XLA Ops:
  7.2 2.3 %copy-start = (bf16[16,2,2,6,16,128]{5,4,3,2,1,0:T(8,128)(2,1)S(1)}, bf16[16,2,2,6,16,128]{5,4,3,2,1,0:T(8,128)(2,1)}, u32[]{:S(2)}) copy-start(bf16[16,2,2,6,16,128]{5,4,3,2,1,0:T(8,128)(2,1)} %param.5) | copy-start | bytes 4718596
  10.3 8.8 %copy-start.5 = (f32[16,6]{0,1:T(8,128)S(1)}, f32[16,6]{0,1:T(8,128)}, u32[]{:S(2)}) copy-start(f32[16,6]{0,1:T(8,128)} %param.6) | copy-start | bytes 1156
  10.3 8.8 %copy-start.6 = (s32[8]{0:T(128)S(1)}, s32[8]{0:T(128)}, u32[]{:S(2)}) copy-start(s32[8]{0:T(128)} %param.9) | copy-start | bytes 100
  11.7 44.3 %all-to-all-start = ((bf16[16,2,2,6,16,128]{5,4,3,2,1,0:T(8,128)(2,1)}), bf16[16,2,2,6,16,128]{5,4,3,2,1,0:T(8,128)(2,1)S(1)}, u32[]{:S(2)}, u32[]{:S(2)}) async-start(bf16[16,2,2,6,16,128]{5,4,3,2,1,0:T(8,128)(2,1)} %broadcast_select_fusion), calls=%async_computation | async-start | bytes 3145728 | tf_op jit(solution)/shard_map/all_to_all | solution.py:103
  18.9 123.5 %reduce-scatter.2.cloned.1.call-start = ((), (), s32[]{:S(2)}) async-start(), calls=%async_computation.2 | async-start | bytes 2359296 | tf_op jit(solution)/shard_map/reduce_scatter | solution.py:110
  56.3 7.8 %copy-start.3 = (bf16[16,64,2,128]{1,0,3,2:T(8,128)(2,1)S(1)}, bf16[16,64,2,128]{1,0,3,2:T(8,128)(2,1)}, u32[]{:S(2)}) copy-start(bf16[16,64,2,128]{1,0,3,2:T(8,128)(2,1)} %broadcast_select_fusion.1) | copy-start | bytes 1572868
  64.1 2.4 %copy-start.1 = (bf16[16,2,2,16,128]{0,3,2,1,4:T(8,128)(2,1)S(1)}, bf16[16,2,2,16,128]{0,3,2,1,4:T(8,128)(2,1)}, u32[]{:S(2)}) copy-start(bf16[16,2,2,16,128]{0,3,2,1,4:T(8,128)(2,1)} %copy.123) | copy-start | bytes 786436
  143.4 1.5 copy-start.2
  144.9 13.0 %copy-start.4 = (f32[8,2,2,16,128]{4,3,2,1,0:T(8,128)S(1)}, f32[8,2,2,16,128]{4,3,2,1,0:T(8,128)}, u32[]{:S(2)}) copy-start(f32[8,2,2,16,128]{4,3,2,1,0:T(8,128)} %reduce-scatter.2.cloned.1.call-done) | copy-start | bytes 786436
Sparse Core Ops, SparseCore 0:
  75.7 66.6 reduce-scatter.1
where the time goes:
time: 169 us
  waiting for transfers between devices  86.5 us (51%)
  local copies, waits for them, and re-layouts  23.6 us (14%)
  matrix products  19.3 us (11%)
  other arithmetic  17.9 us (11%)
  between operations  14.3 us (8%)
  starting transfers between devices  7.29 us (4%)
    reduce_scatter x1, waiting for transfers between devices, per_device(): lax.psum_scatter(partial_value, 'sub', scatter_dimension=0, tiled=True)  61.4 us
    all_to_all x1, waiting for transfers between devices, per_device(): lax.all_to_all(outgoing, 'sub', split_axis=0, concat_axis=0, tiled=True)  25.1 us
    dot_general x1, matrix products, per_device(): jnp.einsum('kvcrsf,rft->kvcst', response, basis_low, preferred_element_ty...  12.1 us
    convert_element_type x2, local copies, waits for them, and re-layouts, project_strain(): return combined.astype(jnp.bfloat16)  7.75 us
    all_to_all x1, starting transfers between devices, per_device(): lax.all_to_all(outgoing, 'sub', split_axis=0, concat_axis=0, tiled=True)  7.25 us
    mul x1, other arithmetic, synthesis_basis(): -norm_scale * jnp.sin(angles)  5.33 us
    gather x2, local copies, waits for them, and re-layouts, per_device(): slip_arranged = jnp.take(slip_live, slot_order, axis=0)  5.19 us
    another operation x1, local copies, waits for them, and re-layouts, contract_slip(): jnp.stack([with_real[0] - with_imag[1], with_imag[0] + with_real[1]], axi...  4.93 us
  transfers between devices with their start and end apart: 2, of which 2 were waited for; matrix products, arithmetic and copies ran while one was open for 10% of the time, Pallas kernels for 0%

commit v1 on v0

v1 whole, which is shorter than its diff:
```python
import functools
import math

import jax
import jax.numpy as jnp
from jax import lax
from jax.experimental import pallas as pl
from jax.experimental.pallas import tpu as pltpu
from jax.sharding import PartitionSpec as P

NT = 2048
PERIODS = 40

damping = 0.05
sample_step = 0.1

LANES = 128
STRAINS = 6
BF16 = jnp.bfloat16
F32 = jnp.float32


def synthesis_basis(freq_count, sample_count):
    freq_ids = jnp.arange(freq_count, dtype=jnp.int32)
    time_ids = jnp.arange(sample_count, dtype=jnp.int32)
    angles = (time_ids[:, None] * freq_ids[None, :] % sample_count).astype(F32) * (
        2.0 * math.pi / sample_count
    )
    norm_scale = 1.0 / math.sqrt(freq_count)
    return jnp.concatenate([norm_scale * jnp.cos(angles), -norm_scale * jnp.sin(angles)], axis=1)


def oscillator_gains(period_count, freq_count, sample_count):
    period_ids = jnp.arange(period_count, dtype=F32)
    periods = 2.0 * jnp.exp(period_ids * (math.log(5.0) / max(period_count - 1, 1)))
    natural = 2.0 * math.pi / periods
    omega_bins = jnp.arange(freq_count, dtype=F32) * (2.0 * math.pi / (sample_count * sample_step))
    squared_natural = (natural * natural)[:, None]
    real_part = squared_natural - (omega_bins * omega_bins)[None, :]
    imag_part = 2.0 * damping * natural[:, None] * omega_bins[None, :]
    magnitude = real_part * real_part + imag_part * imag_part
    return (-squared_natural * real_part / magnitude, squared_natural * imag_part / magnitude)


def swap_blocks(parts):
    count = len(parts)
    width = LANES // count
    parts = list(parts)
    group = lax.broadcasted_iota(jnp.int32, parts[0].shape, 1) // width
    step = 1
    while step < count:
        low_lanes = (group & step) == 0
        for x in range(count):
            if x & step:
                continue
            low, high = parts[x], parts[x | step]
            parts[x] = jnp.where(low_lanes, low, pltpu.roll(high, width * step, 1))
            parts[x | step] = jnp.where(low_lanes, pltpu.roll(low, LANES - width * step, 1), high)
        step *= 2
    return parts


def spread_groups(packed, count):
    width = LANES // count
    group = lax.broadcasted_iota(jnp.int32, packed.shape, 1) // width
    arrays = [packed]
    step = count // 2
    while step:
        low_lanes = (group & step) == 0
        split = []
        for array in arrays:
            other = pltpu.roll(array, width * step, 1) if 2 * width * step == LANES else None
            if other is None:
                up = pltpu.roll(array, width * step, 1)
                down = pltpu.roll(array, LANES - width * step, 1)
            else:
                up = down = other
            split.append(jnp.where(low_lanes, array, up))
            split.append(jnp.where(low_lanes, down, array))
        arrays = split
        step //= 2
    return arrays


def pack_slip_kernel(workers, slip_ref, mech_ref, out_ref, wide, padded):
    core = lax.rem(lax.axis_index("site"), 2)
    stride = 2 * workers
    rows = slip_ref.shape[0] // stride
    chunk = 16
    wide[...] = slip_ref[...].astype(F32)
    for start in range(0, rows, chunk):
        parts = [
            wide[pl.ds(start * stride + 2 * x + core, chunk, stride=stride), :]
            for x in range(workers)
        ]
        for d, part in enumerate(swap_blocks(parts)):
            out_ref[d, start : start + chunk, :] = part.astype(BF16)
    padded[...] = jnp.zeros_like(padded)
    padded[:, :STRAINS] = mech_ref[...]
    moments = padded[...]
    first = moments.astype(BF16).astype(F32)
    second = (moments - first).astype(BF16).astype(F32)
    third = moments - first - second
    coded = (
        first + pltpu.roll(second, STRAINS, 1) + pltpu.roll(third, 2 * STRAINS, 1)
    ).astype(BF16)
    for d in range(workers):
        out_ref[d, rows:, :] = coded


def project_kernel(workers, point_ref, sgt_ref, recv_ref, out_ref, slot_of, moments, wide):
    me = lax.axis_index("sub")
    points = sgt_ref.shape[0]
    sites = sgt_ref.shape[4]
    total = point_ref.shape[0]
    slots = total // workers
    mech_start = recv_ref.shape[1] - slots

    def note_slot(j, carry):
        slot_of[point_ref[j]] = j
        return carry

    lax.fori_loop(0, total, note_slot, 0, unroll=8)
    for w in range(workers):
        coded = recv_ref[w, mech_start:, :].astype(F32)
        moments[w * slots : (w + 1) * slots, :] = (
            coded
            + pltpu.roll(coded, LANES - STRAINS, 1)
            + pltpu.roll(coded, LANES - 2 * STRAINS, 1)
        )
    height = 4 * sites

    def one_point(row, carry):
        moment = moments[pl.ds(slot_of[me * points + row], 1), :]
        weights = [
            jnp.broadcast_to(moment[:, m : m + 1], (sites, LANES)) for m in range(STRAINS)
        ]
        for p in range(2):
            for c in range(2):
                combined = weights[0] * sgt_ref[row, p, c, 0].astype(F32)
                for m in range(1, STRAINS):
                    combined = combined + weights[m] * sgt_ref[row, p, c, m].astype(F32)
                start = pl.multiple_of(row * height + (2 * p + c) * sites, sites)
                wide[pl.ds(start, sites), :] = combined.astype(BF16).astype(F32)
        return carry

    lax.fori_loop(0, points, one_point, 0, unroll=2)
    rows = out_ref.shape[1]
    chunk = 16
    for start in range(0, rows, chunk):
        parts = [
            wide[pl.ds(start * workers + x, chunk, stride=workers), :] for x in range(workers)
        ]
        for d, part in enumerate(swap_blocks(parts)):
            out_ref[d, start : start + chunk, :] = part.astype(BF16)


def contract_kernel(
    workers, point_ref, count_ref, own_ref, other_ref, proj_ref, out_ref, live, slip, proj, total
):
    core = lax.rem(lax.axis_index("site"), 2)
    slots = point_ref.shape[0] // workers
    slip_rows = own_ref.shape[1] - slots
    tall = slip_rows // slots
    proj_rows = proj_ref.shape[1]
    high = proj_rows // slots
    half = high // 2
    block = 4

    def note_worker(w, filled):
        def note_slot(k, carry):
            live[filled + k] = w * slots + k
            return carry

        count = count_ref[w]
        lax.fori_loop(0, count, note_slot, 0)
        return filled + count

    amount = lax.fori_loop(0, workers, note_worker, 0)
    for w in range(workers):
        slip[core, w * slip_rows : (w + 1) * slip_rows, :] = own_ref[w, :slip_rows, :].astype(F32)
        slip[1 - core, w * slip_rows : (w + 1) * slip_rows, :] = other_ref[
            w, :slip_rows, :
        ].astype(F32)
        proj[w * proj_rows : (w + 1) * proj_rows, :] = proj_ref[w].astype(F32)
    total[...] = jnp.zeros_like(total)
    lines = min(2, half)

    def add_slots(first, number):
        slots_here = [live[first + i] for i in range(number)]
        spread = [
            [
                spread_groups(slip[p, pl.ds(pl.multiple_of(j * tall, tall), tall), :], workers)
                for p in range(2)
            ]
            for j in slots_here
        ]
        starts = [point_ref[j] * high for j in slots_here]
        for line in range(0, half, lines):
            for x in range(workers):
                for y in range(line, line + lines):
                    where_real = (y * workers + x) * tall
                    where_imag = ((half + y) * workers + x) * tall
                    real = total[where_real : where_real + tall, :]
                    imag = total[where_imag : where_imag + tall, :]
                    for i in range(number):
                        green_real = proj[pl.ds(starts[i] + y, 1), :]
                        green_imag = proj[pl.ds(starts[i] + half + y, 1), :]
                        slip_real, slip_imag = spread[i][0][x], spread[i][1][x]
                        real = real + (green_real * slip_real - green_imag * slip_imag)
                        imag = imag + (green_real * slip_imag + green_imag * slip_real)
                    total[where_real : where_real + tall, :] = real
                    total[where_imag : where_imag + tall, :] = imag

    def add_block(i, carry):
        add_slots(i * block, block)
        return carry

    def add_one(i, carry):
        add_slots(i, 1)
        return carry

    lax.fori_loop(0, amount // block, add_block, 0)
    lax.fori_loop((amount // block) * block, amount, add_one, 0)
    variations = workers * tall
    for d in range(workers):
        for v in range(tall):
            y, x = divmod(d * tall + v, workers)
            out_ref[d, v * high : (v + 1) * high, :] = total[
                pl.ds(x * tall + y, high, stride=variations), :
            ]


def dot_rows(a, b):
    return lax.dot_general(a, b, (((1,), (1,)), ((), ())), preferred_element_type=F32)


def synthesis_kernel(
    workers,
    tall,
    recv_ref,
    gain_re_ref,
    gain_im_ref,
    basis_ref,
    rest_ref,
    motion_ref,
    peak_ref,
    natural,
    peaks,
):
    rows = recv_ref.shape[1]
    for x, part in enumerate(swap_blocks([recv_ref[w] for w in range(workers)])):
        natural[pl.ds(x, rows, stride=workers), :] = part
    freqs = natural.shape[1]
    width = natural.shape[0] // (2 * tall)
    real = jnp.concatenate(
        [natural[(2 * v) * width : (2 * v + 1) * width, :] for v in range(tall)], axis=0
    )
    imag = jnp.concatenate(
        [natural[(2 * v + 1) * width : (2 * v + 2) * width, :] for v in range(tall)], axis=0
    )
    real_main, imag_main = real.astype(BF16), imag.astype(BF16)
    main = jnp.concatenate([real_main, imag_main], axis=1)
    rest = jnp.concatenate(
        [
            (real - real_main.astype(F32)).astype(BF16),
            (imag - imag_main.astype(F32)).astype(BF16),
        ],
        axis=1,
    )
    samples = basis_ref.shape[0]
    tile = 256
    for t in range(0, samples, tile):
        motion = dot_rows(main, basis_ref[t : t + tile, :])
        motion = motion + dot_rows(rest, basis_ref[t : t + tile, :])
        motion = motion + dot_rows(main, rest_ref[t : t + tile, :])
        motion_ref[:, t : t + tile] = motion.astype(BF16)
    tile = 512

    def one_period(q):
        gain_re = gain_re_ref[pl.ds(q, 1), :]
        gain_im = gain_im_ref[pl.ds(q, 1), :]
        response = jnp.concatenate(
            [
                (gain_re * real - gain_im * imag).astype(BF16),
                (gain_re * imag + gain_im * real).astype(BF16),
            ],
            axis=1,
        )
        peak = None
        for t in range(0, samples, tile):
            wave = jnp.abs(dot_rows(basis_ref[t : t + tile, :], response))
            wave = jnp.max(wave.reshape(tile // 8, 8, wave.shape[1]), axis=0)
            peak = wave if peak is None else jnp.maximum(peak, wave)
        peaks[pl.ds(q, 1), :] = jnp.max(peak, axis=0, keepdims=True)

    periods = gain_re_ref.shape[0]
    group = 20

    def some_periods(i, carry):
        for u in range(group):
            one_period(i * group + u)
        return carry

    lax.fori_loop(0, periods // group, some_periods, 0)
    for q in range(periods - periods % group, periods):
        one_period(q)
    peak_ref[...] = peaks[...].T[:, :periods]


def vmem():
    return pl.BlockSpec(memory_space=pltpu.VMEM)


def smem():
    return pl.BlockSpec(memory_space=pltpu.SMEM)


def params(mebibytes):
    return pltpu.CompilerParams(vmem_limit_bytes=mebibytes * 2**20)


def per_device(sgt, mechanism, slip, point_list, subfault_counts):
    workers = lax.axis_size("sub")
    site_parts = lax.axis_size("site")
    slots, variations, _, freqs = slip.shape
    points, _, components, _, sites, _ = sgt.shape
    total = point_list.shape[0]
    tall = variations // workers
    high = 2 * components * sites // workers
    slip_rows = slots * tall
    proj_rows = points * high
    flat = slip.reshape(slots * variations * 2, freqs)
    packed = pl.pallas_call(
        functools.partial(pack_slip_kernel, workers),
        out_shape=jax.ShapeDtypeStruct((workers, slip_rows + slots, LANES), BF16),
        in_specs=[vmem(), vmem()],
        out_specs=vmem(),
        scratch_shapes=[pltpu.VMEM(flat.shape, F32), pltpu.VMEM((slots, LANES), F32)],
        compiler_params=params(16),
        name="pack_slip",
    )(flat, mechanism)
    own = lax.all_to_all(packed, "sub", split_axis=0, concat_axis=0, tiled=True)
    other = lax.ppermute(own, "site", [(i, i ^ 1) for i in range(site_parts)])
    projected = pl.pallas_call(
        functools.partial(project_kernel, workers),
        out_shape=jax.ShapeDtypeStruct((workers, proj_rows, LANES), BF16),
        in_specs=[smem(), vmem(), vmem()],
        out_specs=vmem(),
        scratch_shapes=[
            pltpu.SMEM((total,), jnp.int32),
            pltpu.VMEM((total, LANES), F32),
            pltpu.VMEM((proj_rows * workers, LANES), F32),
        ],
        compiler_params=params(24),
        name="project",
    )(point_list, sgt, own)
    chunks = lax.all_to_all(projected, "sub", split_axis=0, concat_axis=0, tiled=True)
    partial_rows = tall * high
    spectrum = pl.pallas_call(
        functools.partial(contract_kernel, workers),
        out_shape=jax.ShapeDtypeStruct((workers, partial_rows, LANES), F32),
        in_specs=[smem(), smem(), vmem(), vmem(), vmem()],
        out_specs=vmem(),
        scratch_shapes=[
            pltpu.SMEM((total,), jnp.int32),
            pltpu.VMEM((2, workers * slip_rows, LANES), F32),
            pltpu.VMEM((workers * proj_rows, LANES), F32),
            pltpu.VMEM((high * variations, LANES), F32),
        ],
        compiler_params=params(24),
        name="contract",
    )(point_list, subfault_counts, own, other, chunks)
    spectrum = lax.all_to_all(spectrum, "sub", split_axis=0, concat_axis=0, tiled=True)
    basis = synthesis_basis(freqs, NT)
    basis_low = basis.astype(BF16)
    basis_rest = (basis - lax.reduce_precision(basis, 8, 7)).astype(BF16)
    gain_re, gain_im = oscillator_gains(PERIODS, freqs, NT)
    width = tall * components * sites
    motion, peaks = pl.pallas_call(
        functools.partial(synthesis_kernel, workers, tall),
        out_shape=(
            jax.ShapeDtypeStruct((width, NT), BF16),
            jax.ShapeDtypeStruct((width, PERIODS), F32),
        ),
        in_specs=[vmem()] * 5,
        out_specs=(vmem(), vmem()),
        scratch_shapes=[
            pltpu.VMEM((2 * width, freqs), F32),
            pltpu.VMEM((LANES, width), F32),
        ],
        compiler_params=params(32),
        name="synthesis",
    )(spectrum, gain_re, gain_im, basis_low, basis_rest)
    return (
        motion.reshape(tall, components, sites, NT),
        peaks.reshape(tall, components, sites, PERIODS),
    )


def solution(mesh):
    in_specs = (
        P("sub", None, None, None, "site", None),
        P("sub", None),
        P("sub", None, None, None),
        P(),
        P(),
    )
    out_specs = (P("sub", None, "site", None), P("sub", None, "site", None))
    return jax.shard_map(
        per_device, mesh=mesh, in_specs=in_specs, out_specs=out_specs, check_vma=False
    )
```

time: 169 us -> 71.3 us (0.42)
  waiting for transfers between devices: 86.5 us -> 18.2 us
  Pallas kernels: 0 us -> 27.2 us
  local copies, waits for them, and re-layouts: 23.6 us -> 1.83 us
  matrix products: 19.3 us -> 0 us
  between operations: 14.3 us -> 0.69 us
  other arithmetic: 17.9 us -> 8.38 us
  starting transfers between devices: 7.29 us -> 14.5 us
    reduce_scatter x1 -> x0, waiting for transfers between devices: 61.4 us -> none  [per_device(): lax.psum_scatter(partial_value, 'sub', scatter_dimension=0, tiled=True)]
    pallas_call x0 -> x4, Pallas kernels: none -> 27.2 us  [the longest x1 14.2 us: per_device(): pl.pallas_call(functools.partial(synthesis_kernel, workers, tall), out_sh...]
    dot_general x4 -> x0, matrix products: 19.3 us -> none  [the longest x1 12.1 us: per_device(): jnp.einsum('kvcrsf,rft->kvcst', response, basis_low, preferred_element_ty...]
    convert_element_type x2 -> x0, local copies, waits for them, and re-layouts: 7.75 us -> none  [project_strain(): return combined.astype(jnp.bfloat16)]
    all_to_all x1 -> x3, starting transfers between devices: 7.25 us -> 14.4 us  [the longest x1 7.25 us: per_device(): own = lax.all_to_all(packed, 'sub', split_axis=0, concat_axis=0, tiled=True)]
    all_to_all x1 -> x3, waiting for transfers between devices: 25.1 us -> 18.2 us  [the longest x1 7.03 us: per_device(): lax.all_to_all(spectrum, 'sub', split_axis=0, concat_axis=0, tiled=True)]
    gather x4 -> x0, local copies, waits for them, and re-layouts: 6.6 us -> none  [the longest x2 5.19 us: per_device(): slip_arranged = jnp.take(slip_live, slot_order, axis=0)]
    another operation x1 -> x0, local copies, waits for them, and re-layouts: 4.93 us -> none  [contract_slip(): jnp.stack([with_real[0] - with_imag[1], with_imag[0] + with_real[1]], axi...]
  transfers between devices with their start and end apart: 2 -> 4, of which waited for: 2 -> 3; matrix products, arithmetic and copies ran while one was open for 10% -> 12% of each run, Pallas kernels for 0% -> 0%
where the time goes in v1:
time: 71.3 us; the launch traced here: 70.8 us
  Pallas kernels  27.2 us (38%)
  waiting for transfers between devices  18.2 us (26%)
  starting transfers between devices  14.5 us (20%)
  other arithmetic  8.38 us (12%)
  local copies, waits for them, and re-layouts  1.83 us (3%)
    pallas_call x1, Pallas kernels, per_device(): pl.pallas_call(functools.partial(synthesis_kernel, workers, tall), out_sh...  14.2 us
    pallas_call x1, Pallas kernels, per_device(): pl.pallas_call(functools.partial(contract_kernel, workers), out_shape=jax...  8.27 us
    all_to_all x1, starting transfers between devices, per_device(): own = lax.all_to_all(packed, 'sub', split_axis=0, concat_axis=0, tiled=True)  7.25 us
    all_to_all x1, waiting for transfers between devices, per_device(): lax.all_to_all(spectrum, 'sub', split_axis=0, concat_axis=0, tiled=True)  7.03 us
    all_to_all x1, waiting for transfers between devices, per_device(): lax.all_to_all(projected, 'sub', split_axis=0, concat_axis=0, tiled=True)  6.59 us
    mul x1, other arithmetic, synthesis_basis(): -norm_scale * jnp.sin(angles)  5.06 us
    all_to_all x1, waiting for transfers between devices, per_device(): own = lax.all_to_all(packed, 'sub', split_axis=0, concat_axis=0, tiled=True)  4.55 us
    all_to_all x1, starting transfers between devices, per_device(): lax.all_to_all(projected, 'sub', split_axis=0, concat_axis=0, tiled=True)  3.59 us
  transfers between devices with their start and end apart: 4, of which 3 were waited for; matrix products, arithmetic and copies ran while one was open for 12% of the time, Pallas kernels for 0%

profile of v1, /device:TPU:0, one launch (start us, length us, event | category | flops | bytes accessed | tf_op | source)
XLA Modules:
  0.0 70.8 jit_solution(15414741299598165019)
XLA Ops:
  0.6 0.8 %copy.7.mech_ref = f32[16,6]{1,0:T(8,128)S(1)} copy(f32[16,6]{0,1:T(8,128)} %param.6) | data formatting | bytes 768 | tf_op args[1]
  1.4 0.0 copy-start.1
  1.4 1.0 %copy-done.1 = bf16[16,64,2,128]{3,2,1,0:T(2,128)(2,1)S(1)} copy-done((bf16[16,64,2,128]{3,2,1,0:T(2,128)(2,1)S(1)}, bf16[16,64,2,128]{3,2,1,0:T(2,128)(2,1)}, u32[]{:S(2)}) %copy-start.1) | copy-done | bytes 524312
  2.4 0.0 copy-start
  2.4 0.0 copy-start.2
  2.4 1.4 %pack_slip.1 = bf16[8,144,128]{2,1,0:T(8,128)(2,1)} custom-call(bf16[2048,128]{1,0:T(8,128)(2,1)S(1)} %bitcast.3, f32[16,6]{1,0:T(8,128)S(1)} %copy.7.mech_ref), custom_call_target="tpu_custom_call" | custom-call | tf_op jit(solution)/shard_map/pack_slip/pallas_call | solution.py:334
  3.8 7.3 %all-to-all-start = ((bf16[8,144,128]{2,1,0:T(8,128)(2,1)}), bf16[8,144,128]{2,1,0:T(8,128)(2,1)S(1)}, u32[]{:S(2)}, u32[]{:S(2)}) async-start(bf16[8,144,128]{2,1,0:T(8,128)(2,1)} %pack_slip.1), calls=%async_computation | async-start | bytes 589824 | tf_op jit(solution)/shard_map/all_to_all | solution.py:343
  11.1 5.1 %sine_multiply_fusion = (f32[2048,128]{1,0:T(8,128)}, f32[2048,128]{1,0:T(8,128)}) fusion(), kind=kLoop, calls=%fused_computation.10 | loop fusion | flops 4194304 | bytes 2097152 | tf_op jit(solution)/shard_map/mul | solution.py:30
  16.1 4.5 %all-to-all-done.recv_ref.own_ref = bf16[8,144,128]{2,1,0:T(8,128)(2,1)S(1)} async-done(((bf16[8,144,128]{2,1,0:T(8,128)(2,1)}), bf16[8,144,128]{2,1,0:T(8,128)(2,1)S(1)}, u32[]{:S(2)}, u32[]{:S(2)}) %all-to-all-start) | async-done | bytes 294944 | tf_op jit(solution)/shard_map/all_to_all | solution.py:343
  20.7 0.0 copy-done
  20.7 0.0 copy-done.2
  20.7 3.4 %project.1 = bf16[8,128,128]{2,1,0:T(8,128)(2,1)} custom-call(s32[128]{0:T(128)S(1)} %copy-done.2, bf16[16,2,2,6,16,128]{5,4,3,2,1,0:T(8,128)(2,1)S(1)} %copy-done, bf16[8,144,128]{2,1,0:T(8,128)(2,1)S(1)} %all-to-all-done.recv_ref.own_ref), custom_call_target="tpu_custom_call" | custom-call | tf_op jit(solution)/shard_map/project/pallas_call | solution.py:345
  24.0 3.6 %all-to-all-start.1 = ((bf16[8,128,128]{2,1,0:T(8,128)(2,1)}), bf16[8,128,128]{2,1,0:T(8,128)(2,1)S(1)}, u32[]{:S(2)}, u32[]{:S(2)}) async-start(bf16[8,128,128]{2,1,0:T(8,128)(2,1)} %project.1), calls=%async_computation.1 | async-start | bytes 524288 | tf_op jit(solution)/shard_map/all_to_all | solution.py:358
  27.6 0.1 collective-permute-start
  27.7 0.0 copy-start.3
  27.8 1.8 %fusion.rest_ref = bf16[2048,256]{1,0:T(8,128)(2,1)S(1)} fusion(f32[2048,128]{1,0:T(8,128)} %get-tuple-element.12, f32[2048,128]{1,0:T(8,128)} %get-tuple-element.13), kind=kLoop, calls=%fused_computation.1 | loop fusion | flops 2097152 | bytes 3145728 | tf_op jit(solution)/shard_map/convert_element_type | solution.py:377
  29.6 0.0 copy-start.4
  29.6 0.0 collective-permute-done.other_ref
  29.6 6.6 %all-to-all-done.1.proj_ref = bf16[8,128,128]{2,1,0:T(8,128)(2,1)S(1)} async-done(((bf16[8,128,128]{2,1,0:T(8,128)(2,1)}), bf16[8,128,128]{2,1,0:T(8,128)(2,1)S(1)}, u32[]{:S(2)}, u32[]{:S(2)}) %all-to-all-start.1) | async-done | bytes 262176 | tf_op jit(solution)/shard_map/all_to_all | solution.py:358
  36.2 0.0 copy-done.3
  36.2 8.3 %contract.1 = f32[8,64,128]{2,1,0:T(8,128)} custom-call(s32[128]{0:T(128)S(1)} %copy-done.2, s32[8]{0:T(128)S(1)} %copy-done.3, bf16[8,144,128]{2,1,0:T(8,128)(2,1)S(1)} %all-to-all-done.recv_ref.own_ref, bf16[8,144,128]{2,1,0:T(8,128)(2,1)S(1)} %collective-permute-done.other_ref, bf16[8,128,128]{2,1,0:T(8,128)(2,1)S(1)} %all-to-all-done.1.proj_ref), custom_call_target="tpu_custom_call" | custom-call | tf_op jit(solution)/shard_map/contract/pallas_call | solution.py:360
  44.4 3.6 %all-to-all-start.2 = ((f32[8,64,128]{2,1,0:T(8,128)}), f32[8,64,128]{2,1,0:T(8,128)S(1)}, u32[]{:S(2)}, u32[]{:S(2)}) async-start(f32[8,64,128]{2,1,0:T(8,128)} %contract.1), calls=%async_computation.2 | async-start | bytes 524288 | tf_op jit(solution)/shard_map/all_to_all | solution.py:374
  48.0 0.1 fusion.10
  48.1 0.0 copy-done.4
  48.1 1.4 %fusion.1.basis_ref = bf16[2048,256]{1,0:T(8,128)(2,1)S(1)} fusion(f32[2048,128]{1,0:T(8,128)S(1)} %copy-done.4, f32[2048,128]{1,0:T(8,128)} %get-tuple-element.13), kind=kLoop, calls=%fused_computation.3 | loop fusion | flops 2097152 | bytes 3145728 | tf_op jit(solution)/shard_map/convert_element_type | solution.py:376
  49.5 7.0 %all-to-all-done.2.recv_ref = f32[8,64,128]{2,1,0:T(8,128)S(1)} async-done(((f32[8,64,128]{2,1,0:T(8,128)}), f32[8,64,128]{2,1,0:T(8,128)S(1)}, u32[]{:S(2)}, u32[]{:S(2)}) %all-to-all-start.2) | async-done | bytes 262176 | tf_op jit(solution)/shard_map/all_to_all | solution.py:374
  56.5 14.2 %synthesis.1 = (bf16[256,2048]{1,0:T(8,128)(2,1)}, f32[256,40]{1,0:T(8,128)}) custom-call(f32[8,64,128]{2,1,0:T(8,128)S(1)} %all-to-all-done.2.recv_ref, f32[40,128]{1,0:T(8,128)S(1)} %get-tuple-element.7.gain_re_ref, f32[40,128]{1,0:T(8,128)S(1)} %get-tuple-element.6.gain_im_ref, bf16[2048,256]{1,0:T(8,128)(2,1)S(1)} %fusion.1.basis_ref, ...), custom_call_target="tpu_custom_call" | custom-call | tf_op jit(solution)/shard_map/synthesis/pallas_call | solution.py:380
  (3 shorter events, 0.0 us)
Async XLA Ops:
  1.4 1.0 %copy-start.1 = (bf16[16,64,2,128]{3,2,1,0:T(2,128)(2,1)S(1)}, bf16[16,64,2,128]{3,2,1,0:T(2,128)(2,1)}, u32[]{:S(2)}) copy-start(bf16[16,64,2,128]{3,2,1,0:T(2,128)(2,1)} %param.7) | copy-start | bytes 1572868
  2.4 18.2 %copy-start = (bf16[16,2,2,6,16,128]{5,4,3,2,1,0:T(8,128)(2,1)S(1)}, bf16[16,2,2,6,16,128]{5,4,3,2,1,0:T(8,128)(2,1)}, u32[]{:S(2)}) copy-start(bf16[16,2,2,6,16,128]{5,4,3,2,1,0:T(8,128)(2,1)} %sgt_ref.1) | copy-start | bytes 4718596
  2.4 18.2 %copy-start.2 = (s32[128]{0:T(128)S(1)}, s32[128]{0:T(128)}, u32[]{:S(2)}) copy-start(s32[128]{0:T(128)} %point_ref.3) | copy-start | bytes 1540
  3.8 16.9 %all-to-all-start = ((bf16[8,144,128]{2,1,0:T(8,128)(2,1)}), bf16[8,144,128]{2,1,0:T(8,128)(2,1)S(1)}, u32[]{:S(2)}, u32[]{:S(2)}) async-start(bf16[8,144,128]{2,1,0:T(8,128)(2,1)} %pack_slip.1), calls=%async_computation | async-start | bytes 589824 | tf_op jit(solution)/shard_map/all_to_all | solution.py:343
  24.0 12.1 %all-to-all-start.1 = ((bf16[8,128,128]{2,1,0:T(8,128)(2,1)}), bf16[8,128,128]{2,1,0:T(8,128)(2,1)S(1)}, u32[]{:S(2)}, u32[]{:S(2)}) async-start(bf16[8,128,128]{2,1,0:T(8,128)(2,1)} %project.1), calls=%async_computation.1 | async-start | bytes 524288 | tf_op jit(solution)/shard_map/all_to_all | solution.py:358
  27.6 1.9 %collective-permute-start = (bf16[8,144,128]{2,1,0:T(8,128)(2,1)S(1)}, bf16[8,144,128]{2,1,0:T(8,128)(2,1)S(1)}, u32[]{:S(2)}, u32[]{:S(2)}) collective-permute-start(bf16[8,144,128]{2,1,0:T(8,128)(2,1)S(1)} %all-to-all-done.recv_ref.own_ref), channel_id=1, source_target_pairs={{0,1},{1,0},{2,3},{3,2},{4,5},{5,4},{6,7},{7,6},{8,9},{9,8},{10,11... | collective-permute-start | bytes 884744 | tf_op jit(solution)/shard_map/ppermute | solution.py:344
  27.7 8.4 %copy-start.3 = (s32[8]{0:T(128)S(1)}, s32[8]{0:T(128)}, u32[]{:S(2)}) copy-start(s32[8]{0:T(128)} %count_ref.1) | copy-start | bytes 100
  29.6 18.6 %copy-start.4 = (f32[2048,128]{1,0:T(8,128)S(1)}, f32[2048,128]{1,0:T(8,128)}, u32[]{:S(2)}) copy-start(f32[2048,128]{1,0:T(8,128)} %get-tuple-element.12) | copy-start | bytes 3145732
  44.4 12.1 %all-to-all-start.2 = ((f32[8,64,128]{2,1,0:T(8,128)}), f32[8,64,128]{2,1,0:T(8,128)S(1)}, u32[]{:S(2)}, u32[]{:S(2)}) async-start(f32[8,64,128]{2,1,0:T(8,128)} %contract.1), calls=%async_computation.2 | async-start | bytes 524288 | tf_op jit(solution)/shard_map/all_to_all | solution.py:374

commit v2 on v1

v2 whole, which is shorter than its diff:
```python
import functools
import math

import jax
import jax.numpy as jnp
from jax import lax
from jax.experimental import pallas as pl
from jax.experimental.pallas import tpu as pltpu
from jax.sharding import PartitionSpec as P

NT = 2048
PERIODS = 40

damping = 0.05
sample_step = 0.1

LANES = 128
STRAINS = 6
BLOCK = 4
GROUP = 16
BF16 = jnp.bfloat16
F32 = jnp.float32


def basis_angles(freq_count, sample_count, fine):
    freq_ids = jnp.arange(freq_count, dtype=jnp.int32)
    tables = []
    for time_ids in (jnp.arange(0, sample_count, fine), jnp.arange(fine)):
        angles = (time_ids.astype(jnp.int32)[:, None] * freq_ids[None, :] % sample_count).astype(
            F32
        ) * (2.0 * math.pi / sample_count)
        tables += [jnp.cos(angles), jnp.sin(angles)]
    return tables


def oscillator_gains(period_count, freq_count, sample_count):
    period_ids = jnp.arange(period_count, dtype=F32)
    periods = 2.0 * jnp.exp(period_ids * (math.log(5.0) / max(period_count - 1, 1)))
    natural = 2.0 * math.pi / periods
    omega_bins = jnp.arange(freq_count, dtype=F32) * (2.0 * math.pi / (sample_count * sample_step))
    squared_natural = (natural * natural)[:, None]
    real_part = squared_natural - (omega_bins * omega_bins)[None, :]
    imag_part = 2.0 * damping * natural[:, None] * omega_bins[None, :]
    magnitude = real_part * real_part + imag_part * imag_part
    return (-squared_natural * real_part / magnitude, squared_natural * imag_part / magnitude)


def swap_blocks(parts):
    count = len(parts)
    width = LANES // count
    parts = list(parts)
    group = lax.broadcasted_iota(jnp.int32, parts[0].shape, 1) // width
    step = 1
    while step < count:
        low_lanes = (group & step) == 0
        for x in range(count):
            if x & step:
                continue
            low, high = parts[x], parts[x | step]
            parts[x] = jnp.where(low_lanes, low, pltpu.roll(high, width * step, 1))
            parts[x | step] = jnp.where(low_lanes, pltpu.roll(low, LANES - width * step, 1), high)
        step *= 2
    return parts


def pack_slip_kernel(workers, slip_hbm, mech_ref, out_ref, narrow, wide, padded, done):
    core = lax.rem(lax.axis_index("site"), 2)
    stride = 2 * workers
    slots = mech_ref.shape[1]
    rows = out_ref.shape[1] - slots
    pieces = done.shape[0]
    height = rows // pieces
    copies = []
    for i in range(pieces):
        here = pl.ds(i * height * stride, height * stride)
        copies.append(pltpu.make_async_copy(slip_hbm.at[here, :], narrow.at[here, :], done.at[i]))
        copies[i].start()
    padded[...] = jnp.zeros_like(padded)
    padded[:STRAINS, :slots] = mech_ref[...]
    moments = padded[...].T[:slots, :]
    first = moments.astype(BF16).astype(F32)
    second = (moments - first).astype(BF16).astype(F32)
    third = moments - first - second
    coded = (
        first + pltpu.roll(second, STRAINS, 1) + pltpu.roll(third, 2 * STRAINS, 1)
    ).astype(BF16)
    for d in range(workers):
        out_ref[d, rows:, :] = coded
    chunk = 16
    for i in range(pieces):
        copies[i].wait()
        here = pl.ds(i * height * stride, height * stride)
        wide[here, :] = narrow[here, :].astype(F32)
        for start in range(i * height, (i + 1) * height, chunk):
            parts = [
                wide[pl.ds(start * stride + 2 * x + core, chunk, stride=stride), :]
                for x in range(workers)
            ]
            for d, part in enumerate(swap_blocks(parts)):
                out_ref[d, start : start + chunk, :] = part.astype(BF16)


def choose_kernel(point_ref, chosen_ref):
    points, total = chosen_ref.shape
    point_ids = lax.axis_index("sub") * points + lax.broadcasted_iota(
        jnp.int32, (points, total), 0
    )
    chosen_ref[...] = (point_ref[...] == point_ids).astype(F32).astype(BF16)


def project_kernel(workers, chosen_ref, recv_ref, sgt_ref, out_ref, moments, wide):
    points = sgt_ref.shape[0]
    sites = sgt_ref.shape[4]
    mech_start = recv_ref.shape[1] - chosen_ref.shape[1] // workers
    coded = jnp.concatenate([recv_ref[w, mech_start:, :] for w in range(workers)], axis=0)
    coded = jnp.dot(chosen_ref[...], coded, preferred_element_type=F32)
    moments[...] = (
        coded + pltpu.roll(coded, LANES - STRAINS, 1) + pltpu.roll(coded, LANES - 2 * STRAINS, 1)
    )
    height = 4 * sites

    def one_point(row):
        moment = moments[pl.ds(row, 1), :]
        weights = [
            jnp.broadcast_to(moment[:, m : m + 1], (sites, LANES)) for m in range(STRAINS)
        ]
        for p in range(2):
            for c in range(2):
                combined = weights[0] * sgt_ref[row, p, c, 0].astype(F32)
                for m in range(1, STRAINS):
                    combined = combined + weights[m] * sgt_ref[row, p, c, m].astype(F32)
                start = pl.multiple_of(row * height + (2 * p + c) * sites, sites)
                wide[pl.ds(start, sites), :] = combined.astype(BF16).astype(F32)

    group = 8

    def some_points(step, carry):
        for u in range(group):
            one_point(step * group + u)
        return carry

    lax.fori_loop(0, points // group, some_points, 0)
    rows = out_ref.shape[1]
    chunk = 16
    for start in range(0, rows, chunk):
        parts = [
            wide[pl.ds(start * workers + x, chunk, stride=workers), :] for x in range(workers)
        ]
        for d, part in enumerate(swap_blocks(parts)):
            out_ref[d, start : start + chunk, :] = part.astype(BF16)


def gather_kernel(
    workers,
    tall,
    high,
    point_ref,
    count_ref,
    own_ref,
    other_ref,
    start_ref,
    block_ref,
    spread_hbm,
    slip,
    line_ref,
    wide,
    spread_ref,
    done,
):
    core = lax.rem(lax.axis_index("site"), 2)
    total = point_ref.shape[0]
    slots = total // workers
    slip_rows = slots * tall
    height = workers * tall
    for w in range(workers):
        here = slice(w * slip_rows, (w + 1) * slip_rows)
        slip[core, here, :] = own_ref[w, :slip_rows, :].astype(F32)
        slip[1 - core, here, :] = other_ref[w, :slip_rows, :].astype(F32)

    def note_worker(w, filled):
        def note_slot(k, carry):
            j = w * slots + k
            start_ref[filled + k] = point_ref[j] * high
            line_ref[filled + k] = j * tall
            return carry

        count = count_ref[w]
        lax.fori_loop(0, count, note_slot, 0)
        return filled + count

    amount = lax.fori_loop(0, workers, note_worker, 0)
    blocks = (amount + 2 * BLOCK - 1) // (2 * BLOCK)
    for extra in range(GROUP):
        start_ref[amount + extra] = 0
        line_ref[amount + extra] = 0

    width = LANES // workers
    group = lax.broadcasted_iota(jnp.int32, (tall, LANES), 1) // width
    row_ids = lax.broadcasted_iota(jnp.int32, (LANES, LANES), 0)
    lane_ids = lax.broadcasted_iota(jnp.int32, (LANES, LANES), 1)
    repeat = (row_ids % width == lane_ids % width).astype(F32).astype(BF16)

    def spread_slots(step, carry):
        for i in range(GROUP):
            index = step * GROUP + i
            for p in range(2):
                packed = slip[p, pl.ds(pl.multiple_of(line_ref[index], tall), tall), :]
                for x in range(workers):
                    wide[i, p, x * tall : (x + 1) * tall, :] = jnp.where(
                        (group == x) & (index < amount), packed, 0.0
                    )
        for i in range(GROUP):
            start = pl.multiple_of((step * GROUP + i) * height, height)
            for p in range(2):
                spread_ref[p, pl.ds(start, height), :] = jnp.dot(
                    wide[i, p].astype(BF16), repeat, preferred_element_type=F32
                ).astype(BF16)
        return carry

    lax.fori_loop(0, (amount + GROUP - 1) // GROUP, spread_slots, 0)
    block_ref[0] = blocks
    copy = pltpu.make_async_copy(spread_ref, spread_hbm, done)
    copy.start()
    copy.wait()


def contract_kernel(
    workers, tall, start_ref, block_ref, spread_hbm, proj_ref, out_ref, proj, even, odd, total, ordered, spread_ref, done
):
    proj_rows = proj_ref.shape[1]
    high = ordered.shape[0] // (workers * tall)
    half = high // 2
    variations = workers * tall
    lines = min(2, half)
    early = 2 * 2 * BLOCK * variations
    copies = [
        pltpu.make_async_copy(spread_hbm.at[:, part, :], spread_ref.at[:, part, :], done.at[i])
        for i, part in enumerate((pl.ds(0, early), pl.ds(early, spread_ref.shape[1] - early)))
    ]
    for copy in copies:
        copy.start()
    for w in range(workers):
        proj[w * proj_rows : (w + 1) * proj_rows, :] = proj_ref[w].astype(F32)
    total[...] = jnp.zeros_like(total)

    def widen_block(first, spread):
        for i in range(BLOCK):
            here = pl.ds(pl.multiple_of((first + i) * variations, variations), variations)
            real = spread_ref[0, here, :].astype(F32)
            imag = spread_ref[1, here, :].astype(F32)
            spread[0, i] = real + imag
            spread[1, i] = imag
            spread[2, i] = real

    def add_block(first, spread):
        starts = [start_ref[first + i] for i in range(BLOCK)]
        for line in range(0, half, lines):
            green = []
            for i in range(BLOCK):
                for y in range(line, line + lines):
                    real = jnp.broadcast_to(proj[pl.ds(starts[i] + y, 1), :], (tall, LANES))
                    imag = jnp.broadcast_to(proj[pl.ds(starts[i] + half + y, 1), :], (tall, LANES))
                    green.append((real, real + imag, imag - real))
            for x in range(workers):
                sums = [
                    [total[kind, y, x] for kind in range(3)] for y in range(line, line + lines)
                ]
                for i in range(BLOCK):
                    factors = [spread[kind, i, x * tall : (x + 1) * tall, :] for kind in range(3)]
                    for y in range(lines):
                        for kind in range(3):
                            sums[y][kind] = (
                                sums[y][kind] + green[i * lines + y][kind] * factors[kind]
                            )
                for y in range(lines):
                    for kind in range(3):
                        total[kind, line + y, x] = sums[y][kind]

    def add_two_blocks(step, carry):
        first = step * (2 * BLOCK)
        widen_block(first, even)
        widen_block(first + BLOCK, odd)
        add_block(first, even)
        add_block(first + BLOCK, odd)
        return carry

    copies[0].wait()
    lax.fori_loop(0, jnp.minimum(2, block_ref[0]), add_two_blocks, 0)
    copies[1].wait()
    lax.fori_loop(2, block_ref[0], add_two_blocks, 0)
    for y in range(half):
        for x in range(workers):
            shared = total[0, y, x]
            at_real = (y * workers + x) * tall
            at_imag = ((half + y) * workers + x) * tall
            ordered[at_real : at_real + tall, :] = shared - total[1, y, x]
            ordered[at_imag : at_imag + tall, :] = shared + total[2, y, x]
    for d in range(workers):
        for v in range(tall):
            y, x = divmod(d * tall + v, workers)
            out_ref[d, v * high : (v + 1) * high, :] = ordered[
                pl.ds(x * tall + y, high, stride=variations), :
            ]


def dot_rows(a, b):
    return lax.dot_general(a, b, (((1,), (1,)), ((), ())), preferred_element_type=F32)


def tables_kernel(
    coarse_cos_ref, coarse_sin_ref, fine_cos_ref, fine_sin_ref, ready_hbm, basis_ref, rest_ref
):
    del ready_hbm
    fine, freqs = fine_cos_ref.shape
    norm_scale = 1.0 / math.sqrt(freqs)
    cosine = norm_scale * fine_cos_ref[...]
    sine = norm_scale * fine_sin_ref[...]
    for i in range(coarse_cos_ref.shape[0]):
        start_cos, start_sin = coarse_cos_ref[i : i + 1, :], coarse_sin_ref[i : i + 1, :]
        here = slice(i * fine, (i + 1) * fine)
        for part, values in enumerate(
            (start_cos * cosine - start_sin * sine, -(start_sin * cosine) - start_cos * sine)
        ):
            low = values.astype(BF16)
            basis_ref[here, part * freqs : (part + 1) * freqs] = low
            rest_ref[here, part * freqs : (part + 1) * freqs] = (
                values - low.astype(F32)
            ).astype(BF16)


def synthesis_kernel(
    workers,
    tall,
    recv_ref,
    gain_re_ref,
    gain_im_ref,
    basis_ref,
    rest_ref,
    motion_ref,
    peak_ref,
    natural,
    peaks,
):
    freqs = natural.shape[1]
    rows = recv_ref.shape[1]
    for x, part in enumerate(swap_blocks([recv_ref[w] for w in range(workers)])):
        natural[pl.ds(x, rows, stride=workers), :] = part
    width = natural.shape[0] // (2 * tall)
    real = jnp.concatenate(
        [natural[(2 * v) * width : (2 * v + 1) * width, :] for v in range(tall)], axis=0
    )
    imag = jnp.concatenate(
        [natural[(2 * v + 1) * width : (2 * v + 2) * width, :] for v in range(tall)], axis=0
    )
    real_main, imag_main = real.astype(BF16), imag.astype(BF16)
    main = jnp.concatenate([real_main, imag_main], axis=1)
    rest = jnp.concatenate(
        [
            (real - real_main.astype(F32)).astype(BF16),
            (imag - imag_main.astype(F32)).astype(BF16),
        ],
        axis=1,
    )
    samples = basis_ref.shape[0]
    tile = 256
    for t in range(0, samples, tile):
        motion = dot_rows(main, basis_ref[t : t + tile, :])
        motion = motion + dot_rows(rest, basis_ref[t : t + tile, :])
        motion = motion + dot_rows(main, rest_ref[t : t + tile, :])
        motion_ref[:, t : t + tile] = motion.astype(BF16)
    tile = 512

    def one_period(q):
        gain_re = gain_re_ref[pl.ds(q, 1), :]
        gain_im = gain_im_ref[pl.ds(q, 1), :]
        response = jnp.concatenate(
            [
                (gain_re * real - gain_im * imag).astype(BF16),
                (gain_re * imag + gain_im * real).astype(BF16),
            ],
            axis=1,
        )
        peak = None
        for t in range(0, samples, tile):
            wave = jnp.abs(dot_rows(basis_ref[t : t + tile, :], response))
            wave = jnp.max(wave.reshape(tile // 8, 8, wave.shape[1]), axis=0)
            peak = wave if peak is None else jnp.maximum(peak, wave)
        peaks[pl.ds(q, 1), :] = jnp.max(peak, axis=0, keepdims=True)

    periods = gain_re_ref.shape[0]
    group = 20

    def some_periods(i, carry):
        for u in range(group):
            one_period(i * group + u)
        return carry

    lax.fori_loop(0, periods // group, some_periods, 0)
    for q in range(periods - periods % group, periods):
        one_period(q)
    peak_ref[...] = peaks[...].T[:, :periods]


def vmem():
    return pl.BlockSpec(memory_space=pltpu.VMEM)


def hbm():
    return pl.BlockSpec(memory_space=pltpu.HBM)


def smem():
    return pl.BlockSpec(memory_space=pltpu.SMEM)


def params(mebibytes, held=0):
    return pltpu.CompilerParams(vmem_limit_bytes=mebibytes * 2**20 + held)


def beside(microseconds):
    return pl.CostEstimate(
        flops=microseconds * 10**9, bytes_accessed=microseconds * 3 * 10**6, transcendentals=0
    )


def per_device(sgt, mechanism, slip, point_list, subfault_counts):
    workers = lax.axis_size("sub")
    site_parts = lax.axis_size("site")
    slots, variations, _, freqs = slip.shape
    points, _, components, _, sites, _ = sgt.shape
    total = point_list.shape[0]
    tall = variations // workers
    high = 2 * components * sites // workers
    slip_rows = slots * tall
    proj_rows = points * high
    flat = slip.reshape(slots * variations * 2, freqs)
    packed = pl.pallas_call(
        functools.partial(pack_slip_kernel, workers),
        out_shape=jax.ShapeDtypeStruct((workers, slip_rows + slots, LANES), BF16),
        in_specs=[hbm(), vmem()],
        out_specs=vmem(),
        scratch_shapes=[
            pltpu.VMEM(flat.shape, BF16),
            pltpu.VMEM(flat.shape, F32),
            pltpu.VMEM((LANES, LANES), F32),
            pltpu.SemaphoreType.DMA((4,)),
        ],
        compiler_params=params(58),
        name="pack_slip",
    )(flat, mechanism.T)
    own = lax.all_to_all(packed, "sub", split_axis=0, concat_axis=0, tiled=True)
    other = lax.ppermute(own, "site", [(i, i ^ 1) for i in range(site_parts)])
    chosen = pl.pallas_call(
        choose_kernel,
        out_shape=jax.ShapeDtypeStruct((points, total), BF16),
        in_specs=[vmem()],
        out_specs=vmem(),
        cost_estimate=beside(10),
        name="choose",
    )(point_list.reshape(1, total))
    projected = pl.pallas_call(
        functools.partial(project_kernel, workers),
        out_shape=jax.ShapeDtypeStruct((workers, proj_rows, LANES), BF16),
        in_specs=[vmem(), vmem(), vmem()],
        out_specs=vmem(),
        scratch_shapes=[
            pltpu.VMEM((points, LANES), F32),
            pltpu.VMEM((proj_rows * workers, LANES), F32),
        ],
        compiler_params=params(24),
        name="project",
    )(chosen, own, sgt)
    chunks = lax.all_to_all(projected, "sub", split_axis=0, concat_axis=0, tiled=True)
    capacity = total // 2 + GROUP
    spread_bytes = 2 * capacity * variations * LANES * 2
    starts, blocks, spread = pl.pallas_call(
        functools.partial(gather_kernel, workers, tall, high),
        out_shape=(
            jax.ShapeDtypeStruct((total + GROUP,), jnp.int32),
            jax.ShapeDtypeStruct((1,), jnp.int32),
            jax.ShapeDtypeStruct((2, capacity * variations, LANES), BF16),
        ),
        in_specs=[smem(), smem(), vmem(), vmem()],
        out_specs=(smem(), smem(), hbm()),
        scratch_shapes=[
            pltpu.VMEM((2, workers * slip_rows, LANES), F32),
            pltpu.SMEM((total + GROUP,), jnp.int32),
            pltpu.VMEM((GROUP, 2, variations, LANES), F32),
            pltpu.VMEM((2, capacity * variations, LANES), BF16),
            pltpu.SemaphoreType.DMA,
        ],
        compiler_params=params(16, spread_bytes),
        name="gather",
    )(point_list, subfault_counts, own, other)
    partial_rows = tall * high
    spectrum = pl.pallas_call(
        functools.partial(contract_kernel, workers, tall),
        out_shape=jax.ShapeDtypeStruct((workers, partial_rows, LANES), F32),
        in_specs=[smem(), smem(), hbm(), vmem()],
        out_specs=vmem(),
        scratch_shapes=[
            pltpu.VMEM((workers * proj_rows, LANES), F32),
            pltpu.VMEM((3, BLOCK, variations, LANES), F32),
            pltpu.VMEM((3, BLOCK, variations, LANES), F32),
            pltpu.VMEM((3, high // 2, workers, tall, LANES), F32),
            pltpu.VMEM((high * variations, LANES), F32),
            pltpu.VMEM((2, capacity * variations, LANES), BF16),
            pltpu.SemaphoreType.DMA((2,)),
        ],
        compiler_params=params(12, spread_bytes),
        name="contract",
    )(starts, blocks, spread, chunks)
    basis, basis_rest = pl.pallas_call(
        tables_kernel,
        out_shape=(jax.ShapeDtypeStruct((NT, 2 * freqs), BF16),) * 2,
        in_specs=[vmem()] * 4 + [hbm()],
        out_specs=(vmem(), vmem()),
        compiler_params=params(16),
        name="tables",
    )(*basis_angles(freqs, NT, 64), spectrum)
    gains = oscillator_gains(PERIODS, freqs, NT)
    spectrum = lax.all_to_all(spectrum, "sub", split_axis=0, concat_axis=0, tiled=True)
    width = tall * components * sites
    motion, peaks = pl.pallas_call(
        functools.partial(synthesis_kernel, workers, tall),
        out_shape=(
            jax.ShapeDtypeStruct((width, NT), BF16),
            jax.ShapeDtypeStruct((width, PERIODS), F32),
        ),
        in_specs=[vmem()] * 5,
        out_specs=(vmem(), vmem()),
        scratch_shapes=[
            pltpu.VMEM((2 * width, freqs), F32),
            pltpu.VMEM((LANES, width), F32),
        ],
        compiler_params=params(32),
        name="synthesis",
    )(spectrum, *gains, basis, basis_rest)
    return (
        motion.reshape(tall, components, sites, NT),
        peaks.reshape(tall, components, sites, PERIODS),
    )


def solution(mesh):
    in_specs = (
        P("sub", None, None, None, "site", None),
        P("sub", None),
        P("sub", None, None, None),
        P(),
        P(),
    )
    out_specs = (P("sub", None, "site", None), P("sub", None, "site", None))
    return jax.shard_map(
        per_device, mesh=mesh, in_specs=in_specs, out_specs=out_specs, check_vma=False
    )
```

time: 71.3 us -> 67.4 us (0.945)
  other arithmetic: 8.38 us -> 0.43 us
  Pallas kernels: 27.2 us -> 30 us
  waiting for transfers between devices: 18.2 us -> 20.5 us
  local copies, waits for them, and re-layouts: 1.83 us -> 0.7 us
    mul x1, other arithmetic: 5.06 us -> 0.01 us  [basis_angles(): jnp.arange(0, sample_count, fine)]
    all_to_all x1, waiting for transfers between devices: 4.55 us -> 8.24 us  [per_device(): own = lax.all_to_all(packed, 'sub', split_axis=0, concat_axis=0, tiled=True)]
    all_to_all x1, waiting for transfers between devices: 6.59 us -> 3.22 us  [per_device(): lax.all_to_all(projected, 'sub', split_axis=0, concat_axis=0, tiled=True)]
    convert_element_type x2 -> x0, other arithmetic: 3.2 us -> none  [the longest x1 1.8 us: per_device(): basis_rest = (basis - lax.reduce_precision(basis, 8, 7)).astype(BF16)]
    pallas_call x1, Pallas kernels: 1.37 us -> 3.56 us  [per_device(): pl.pallas_call(functools.partial(pack_slip_kernel, workers), out_shape=ja...]
    pallas_call x1 -> x4, Pallas kernels: 8.27 us -> 10.2 us  [the longest x1 4.59 us: per_device(): pl.pallas_call(functools.partial(contract_kernel, workers, tall), out_sha...]
    ppermute x1, waiting for transfers between devices: 0.01 us -> 1.39 us  [per_device(): other = lax.ppermute(own, 'site', [(i, i ^ 1) for i in range(site_parts)])]
    pallas_call x1, Pallas kernels: 3.36 us -> 2.06 us  [per_device(): pl.pallas_call(functools.partial(project_kernel, workers), out_shape=jax....]
  transfers between devices with their start and end apart: 4 -> 4, of which waited for: 3 -> 4; matrix products, arithmetic and copies ran while one was open for 12% -> 1% of each run, Pallas kernels for 0% -> 8%
where the time goes in v2:
time: 67.4 us; the launch traced here: 66.9 us
  Pallas kernels  30 us (45%)
  waiting for transfers between devices  20.5 us (30%)
  starting transfers between devices  14.5 us (22%)
  between operations  0.71 us (1%)
  local copies, waits for them, and re-layouts  0.7 us (1%)
    pallas_call x1, Pallas kernels, per_device(): pl.pallas_call(functools.partial(synthesis_kernel, workers, tall), out_sh...  14.2 us
    all_to_all x1, waiting for transfers between devices, per_device(): own = lax.all_to_all(packed, 'sub', split_axis=0, concat_axis=0, tiled=True)  8.24 us
    all_to_all x1, waiting for transfers between devices, per_device(): lax.all_to_all(spectrum, 'sub', split_axis=0, concat_axis=0, tiled=True)  7.67 us
    all_to_all x1, starting transfers between devices, per_device(): own = lax.all_to_all(packed, 'sub', split_axis=0, concat_axis=0, tiled=True)  7.26 us
    pallas_call x1, Pallas kernels, per_device(): pl.pallas_call(functools.partial(contract_kernel, workers, tall), out_sha...  4.59 us
    pallas_call x1, Pallas kernels, per_device(): pl.pallas_call(functools.partial(gather_kernel, workers, tall, high), out...  3.64 us
    all_to_all x1, starting transfers between devices, per_device(): lax.all_to_all(spectrum, 'sub', split_axis=0, concat_axis=0, tiled=True)  3.6 us
    all_to_all x1, starting transfers between devices, per_device(): lax.all_to_all(projected, 'sub', split_axis=0, concat_axis=0, tiled=True)  3.59 us
  transfers between devices with their start and end apart: 4, of which 4 were waited for; matrix products, arithmetic and copies ran while one was open for 1% of the time, Pallas kernels for 8%

profile of v2, /device:TPU:0, one launch (start us, length us, event | category | flops | bytes accessed | tf_op | source)
XLA Modules:
  0.0 66.9 jit_solution(6837996628999222294)
XLA Ops:
  0.6 3.6 %pack_slip.1 = bf16[8,144,128]{2,1,0:T(8,128)(2,1)} custom-call(bf16[2048,128]{1,0:T(8,128)(2,1)} %bitcast.6, f32[6,16]{1,0:T(8,128)} %bitcast.7), custom_call_target="tpu_custom_call" | custom-call | tf_op jit(solution)/shard_map/pack_slip/pallas_call | solution.py:437
  4.2 7.3 %all-to-all-start = ((bf16[8,144,128]{2,1,0:T(8,128)(2,1)}), bf16[8,144,128]{2,1,0:T(8,128)(2,1)S(1)}, u32[]{:S(2)}, u32[]{:S(2)}) async-start(bf16[8,144,128]{2,1,0:T(8,128)(2,1)} %pack_slip.1), calls=%async_computation | async-start | bytes 589824 | tf_op jit(solution)/shard_map/all_to_all | solution.py:451
  11.5 0.0 copy-start
  11.5 1.4 %choose.1.chosen_ref = bf16[16,128]{1,0:T(8,128)(2,1)} custom-call(s32[1,128]{1,0:T(1,128)} %bitcast.5), custom_call_target="tpu_custom_call" | custom-call | flops 10000000000 | bytes 30000000 | tf_op jit(solution)/shard_map/choose/pallas_call | solution.py:453
  12.8 8.2 %all-to-all-done.own_ref.recv_ref = bf16[8,144,128]{2,1,0:T(8,128)(2,1)S(1)} async-done(((bf16[8,144,128]{2,1,0:T(8,128)(2,1)}), bf16[8,144,128]{2,1,0:T(8,128)(2,1)S(1)}, u32[]{:S(2)}, u32[]{:S(2)}) %all-to-all-start) | async-done | bytes 294944 | tf_op jit(solution)/shard_map/all_to_all | solution.py:451
  21.1 0.0 copy-done
  21.1 0.0 copy-start.1
  21.1 0.7 %copy-done.1 = bf16[16,128]{1,0:T(8,128)(2,1)S(1)} copy-done((bf16[16,128]{1,0:T(8,128)(2,1)S(1)}, bf16[16,128]{1,0:T(8,128)(2,1)}, u32[]{:S(2)}) %copy-start.1) | copy-done | bytes 4120
  21.8 0.0 copy-start.2
  21.8 0.0 copy-start.3
  21.8 2.1 %project.1 = bf16[8,128,128]{2,1,0:T(8,128)(2,1)} custom-call(bf16[16,128]{1,0:T(8,128)(2,1)S(1)} %copy-done.1, bf16[8,144,128]{2,1,0:T(8,128)(2,1)S(1)} %all-to-all-done.own_ref.recv_ref, bf16[16,2,2,6,16,128]{5,4,3,2,1,0:T(8,128)(2,1)S(1)} %copy-done), custom_call_target="tpu_custom_call" | custom-call | tf_op jit(solution)/shard_map/project/pallas_call | solution.py:461
  23.8 3.6 %all-to-all-start.1 = ((bf16[8,128,128]{2,1,0:T(8,128)(2,1)}), bf16[8,128,128]{2,1,0:T(8,128)(2,1)S(1)}, u32[]{:S(2)}, u32[]{:S(2)}) async-start(bf16[8,128,128]{2,1,0:T(8,128)(2,1)} %project.1), calls=%async_computation.1 | async-start | bytes 524288 | tf_op jit(solution)/shard_map/all_to_all | solution.py:473
  27.4 0.1 collective-permute-start
  27.5 0.1 fusion.12
  27.7 1.4 %collective-permute-done.other_ref = bf16[8,144,128]{2,1,0:T(8,128)(2,1)S(1)} collective-permute-done((bf16[8,144,128]{2,1,0:T(8,128)(2,1)S(1)}, bf16[8,144,128]{2,1,0:T(8,128)(2,1)S(1)}, u32[]{:S(2)}, u32[]{:S(2)}) %collective-permute-start) | collective-permute-done | bytes 294944 | tf_op jit(solution)/shard_map/ppermute | solution.py:452
  29.1 0.0 copy-done.2
  29.1 0.0 copy-done.3
  29.1 3.6 %gather.1 = (s32[144]{0:T(256)S(1)}, s32[1]{0:T(128)}, bf16[2,5120,128]{2,1,0:T(8,128)(2,1)S(1)}) custom-call(s32[128]{0:T(128)S(1)} %copy-done.2, s32[8]{0:T(128)S(1)} %copy-done.3, bf16[8,144,128]{2,1,0:T(8,128)(2,1)S(1)} %all-to-all-done.own_ref.recv_ref, bf16[8,144,128]{2,1,0:T(8,128)(2,1)S(1)} %collective-permute-done.other_ref), custom_call_target="tpu_custom_call" | custom-call | tf_op jit(solution)/shard_map/gather/pallas_call | solution.py:476
  32.7 3.2 %all-to-all-done.1.proj_ref = bf16[8,128,128]{2,1,0:T(8,128)(2,1)S(1)} async-done(((bf16[8,128,128]{2,1,0:T(8,128)(2,1)}), bf16[8,128,128]{2,1,0:T(8,128)(2,1)S(1)}, u32[]{:S(2)}, u32[]{:S(2)}) %all-to-all-start.1) | async-done | bytes 262176 | tf_op jit(solution)/shard_map/all_to_all | solution.py:473
  36.0 4.6 %contract.1.ready_hbm = f32[8,64,128]{2,1,0:T(8,128)} custom-call(s32[144]{0:T(256)S(1)} %get-tuple-element.9.start_ref, s32[1]{0:T(128)} %get-tuple-element.10.block_ref, bf16[2,5120,128]{2,1,0:T(8,128)(2,1)S(1)} %get-tuple-element.11.spread_hbm, bf16[8,128,128]{2,1,0:T(8,128)(2,1)S(1)} %all-to-all-done.1.proj_ref), custom_call_target="tpu_custom_call" | custom-call | tf_op jit(solution)/shard_map/contract/pallas_call | solution.py:496
  40.6 3.6 %all-to-all-start.2 = ((f32[8,64,128]{2,1,0:T(8,128)}), f32[8,64,128]{2,1,0:T(8,128)S(1)}, u32[]{:S(2)}, u32[]{:S(2)}) async-start(f32[8,64,128]{2,1,0:T(8,128)} %contract.1.ready_hbm), calls=%async_computation.2 | async-start | bytes 524288 | tf_op jit(solution)/shard_map/all_to_all | solution.py:522
  44.2 0.2 fusion.17
  44.3 0.1 fusion.8
  44.4 0.6 tables.1
  45.0 7.7 %all-to-all-done.2.recv_ref = f32[8,64,128]{2,1,0:T(8,128)S(1)} async-done(((f32[8,64,128]{2,1,0:T(8,128)}), f32[8,64,128]{2,1,0:T(8,128)S(1)}, u32[]{:S(2)}, u32[]{:S(2)}) %all-to-all-start.2) | async-done | bytes 262176 | tf_op jit(solution)/shard_map/all_to_all | solution.py:522
  52.7 14.2 %synthesis.1 = (bf16[256,2048]{1,0:T(8,128)(2,1)}, f32[256,40]{1,0:T(8,128)}) custom-call(f32[8,64,128]{2,1,0:T(8,128)S(1)} %all-to-all-done.2.recv_ref, f32[40,128]{1,0:T(8,128)S(1)} %get-tuple-element.17.gain_re_ref, f32[40,128]{1,0:T(8,128)S(1)} %get-tuple-element.16.gain_im_ref, bf16[2048,256]{1,0:T(8,128)(2,1)S(1)} %get-tuple-element.12.basis_ref, ...), custom_call_target="tpu_custom_call" | custom-call | tf_op jit(solution)/shard_map/synthesis/pallas_call | solution.py:524
  (4 shorter events, 0.0 us)
Async XLA Ops:
  4.2 16.9 %all-to-all-start = ((bf16[8,144,128]{2,1,0:T(8,128)(2,1)}), bf16[8,144,128]{2,1,0:T(8,128)(2,1)S(1)}, u32[]{:S(2)}, u32[]{:S(2)}) async-start(bf16[8,144,128]{2,1,0:T(8,128)(2,1)} %pack_slip.1), calls=%async_computation | async-start | bytes 589824 | tf_op jit(solution)/shard_map/all_to_all | solution.py:451
  11.5 9.6 %copy-start = (bf16[16,2,2,6,16,128]{5,4,3,2,1,0:T(8,128)(2,1)S(1)}, bf16[16,2,2,6,16,128]{5,4,3,2,1,0:T(8,128)(2,1)}, u32[]{:S(2)}) copy-start(bf16[16,2,2,6,16,128]{5,4,3,2,1,0:T(8,128)(2,1)} %sgt_ref.1) | copy-start | bytes 4718596
  21.1 0.7 %copy-start.1 = (bf16[16,128]{1,0:T(8,128)(2,1)S(1)}, bf16[16,128]{1,0:T(8,128)(2,1)}, u32[]{:S(2)}) copy-start(bf16[16,128]{1,0:T(8,128)(2,1)} %choose.1.chosen_ref) | copy-start | bytes 12292
  21.8 7.3 %copy-start.2 = (s32[128]{0:T(128)S(1)}, s32[128]{0:T(128)}, u32[]{:S(2)}) copy-start(s32[128]{0:T(128)} %point_ref.1) | copy-start | bytes 1540
  21.8 7.3 %copy-start.3 = (s32[8]{0:T(128)S(1)}, s32[8]{0:T(128)}, u32[]{:S(2)}) copy-start(s32[8]{0:T(128)} %count_ref.1) | copy-start | bytes 100
  23.8 12.1 %all-to-all-start.1 = ((bf16[8,128,128]{2,1,0:T(8,128)(2,1)}), bf16[8,128,128]{2,1,0:T(8,128)(2,1)S(1)}, u32[]{:S(2)}, u32[]{:S(2)}) async-start(bf16[8,128,128]{2,1,0:T(8,128)(2,1)} %project.1), calls=%async_computation.1 | async-start | bytes 524288 | tf_op jit(solution)/shard_map/all_to_all | solution.py:473
  27.4 1.6 %collective-permute-start = (bf16[8,144,128]{2,1,0:T(8,128)(2,1)S(1)}, bf16[8,144,128]{2,1,0:T(8,128)(2,1)S(1)}, u32[]{:S(2)}, u32[]{:S(2)}) collective-permute-start(bf16[8,144,128]{2,1,0:T(8,128)(2,1)S(1)} %all-to-all-done.own_ref.recv_ref), channel_id=1, source_target_pairs={{0,1},{1,0},{2,3},{3,2},{4,5},{5,4},{6,7},{7,6},{8,9},{9,8},{10,11... | collective-permute-start | bytes 884744 | tf_op jit(solution)/shard_map/ppermute | solution.py:452
  40.6 12.1 %all-to-all-start.2 = ((f32[8,64,128]{2,1,0:T(8,128)}), f32[8,64,128]{2,1,0:T(8,128)S(1)}, u32[]{:S(2)}, u32[]{:S(2)}) async-start(f32[8,64,128]{2,1,0:T(8,128)} %contract.1.ready_hbm), calls=%async_computation.2 | async-start | bytes 524288 | tf_op jit(solution)/shard_map/all_to_all | solution.py:522

commit v3 on v2

--- a/solution.py
+++ b/solution.py
@@ -63,7 +63,7 @@
     return parts
 
 
-def pack_slip_kernel(workers, slip_hbm, mech_ref, out_ref, narrow, wide, padded, done):
+def pack_slip_kernel(workers, slip_hbm, mech_hbm, out_hbm, narrow, mech_ref, out_ref, wide, padded, done, mech_done, sent):
     core = lax.rem(lax.axis_index("site"), 2)
     stride = 2 * workers
     slots = mech_ref.shape[1]
@@ -75,7 +75,10 @@
         here = pl.ds(i * height * stride, height * stride)
         copies.append(pltpu.make_async_copy(slip_hbm.at[here, :], narrow.at[here, :], done.at[i]))
         copies[i].start()
+    mech_copy = pltpu.make_async_copy(mech_hbm, mech_ref, mech_done)
+    mech_copy.start()
     padded[...] = jnp.zeros_like(padded)
+    mech_copy.wait()
     padded[:STRAINS, :slots] = mech_ref[...]
     moments = padded[...].T[:slots, :]
     first = moments.astype(BF16).astype(F32)
@@ -86,6 +89,13 @@
     ).astype(BF16)
     for d in range(workers):
         out_ref[d, rows:, :] = coded
+    sends = [
+        pltpu.make_async_copy(out_ref.at[:, part, :], out_hbm.at[:, part, :], sent.at[i])
+        for i, part in enumerate(
+            [pl.ds(i * height, height) for i in range(pieces)] + [pl.ds(rows, slots)]
+        )
+    ]
+    sends[pieces].start()
     chunk = 16
     for i in range(pieces):
         copies[i].wait()
@@ -98,6 +108,9 @@
             ]
             for d, part in enumerate(swap_blocks(parts)):
                 out_ref[d, start : start + chunk, :] = part.astype(BF16)
+        sends[i].start()
+    for send in sends:
+        send.wait()
 
 
 def choose_kernel(point_ref, chosen_ref):
@@ -105,7 +118,7 @@
     point_ids = lax.axis_index("sub") * points + lax.broadcasted_iota(
         jnp.int32, (points, total), 0
     )
-    chosen_ref[...] = (point_ref[...] == point_ids).astype(F32).astype(BF16)
+    chosen_ref[...] = (point_ref[...] == point_ids).astype(F32)
 
 
 def project_kernel(workers, chosen_ref, recv_ref, sgt_ref, out_ref, moments, wide):
@@ -225,20 +238,13 @@
 
 
 def contract_kernel(
-    workers, tall, start_ref, block_ref, spread_hbm, proj_ref, out_ref, proj, even, odd, total, ordered, spread_ref, done
+    workers, tall, start_ref, block_ref, spread_ref, proj_ref, out_ref, proj, even, odd, total, ordered, outgoing
 ):
     proj_rows = proj_ref.shape[1]
     high = ordered.shape[0] // (workers * tall)
     half = high // 2
     variations = workers * tall
     lines = min(2, half)
-    early = 2 * 2 * BLOCK * variations
-    copies = [
-        pltpu.make_async_copy(spread_hbm.at[:, part, :], spread_ref.at[:, part, :], done.at[i])
-        for i, part in enumerate((pl.ds(0, early), pl.ds(early, spread_ref.shape[1] - early)))
-    ]
-    for copy in copies:
-        copy.start()
     for w in range(workers):
         proj[w * proj_rows : (w + 1) * proj_rows, :] = proj_ref[w].astype(F32)
     total[...] = jnp.zeros_like(total)
@@ -284,10 +290,7 @@
         add_block(first + BLOCK, odd)
         return carry
 
-    copies[0].wait()
-    lax.fori_loop(0, jnp.minimum(2, block_ref[0]), add_two_blocks, 0)
-    copies[1].wait()
-    lax.fori_loop(2, block_ref[0], add_two_blocks, 0)
+    lax.fori_loop(0, block_ref[0], add_two_blocks, 0)
     for y in range(half):
         for x in range(workers):
             shared = total[0, y, x]
@@ -298,9 +301,10 @@
     for d in range(workers):
         for v in range(tall):
             y, x = divmod(d * tall + v, workers)
-            out_ref[d, v * high : (v + 1) * high, :] = ordered[
+            outgoing[(d * tall + v) * high : (d * tall + v + 1) * high, :] = ordered[
                 pl.ds(x * tall + y, high, stride=variations), :
             ]
+    out_ref[...] = outgoing[...].astype(BF16)
 
 
 def dot_rows(a, b):
@@ -336,14 +340,20 @@
     gain_im_ref,
     basis_ref,
     rest_ref,
-    motion_ref,
+    motion_hbm,
     peak_ref,
+    received,
     natural,
     peaks,
+    motion_ref,
+    done,
 ):
     freqs = natural.shape[1]
-    rows = recv_ref.shape[1]
-    for x, part in enumerate(swap_blocks([recv_ref[w] for w in range(workers)])):
+    rows = recv_ref.shape[0] // workers
+    received[...] = recv_ref[...].astype(F32)
+    for x, part in enumerate(
+        swap_blocks([received[w * rows : (w + 1) * rows, :] for w in range(workers)])
+    ):
         natural[pl.ds(x, rows, stride=workers), :] = part
     width = natural.shape[0] // (2 * tall)
     real = jnp.concatenate(
@@ -352,53 +362,49 @@
     imag = jnp.concatenate(
         [natural[(2 * v + 1) * width : (2 * v + 2) * width, :] for v in range(tall)], axis=0
     )
-    real_main, imag_main = real.astype(BF16), imag.astype(BF16)
-    main = jnp.concatenate([real_main, imag_main], axis=1)
-    rest = jnp.concatenate(
-        [
-            (real - real_main.astype(F32)).astype(BF16),
-            (imag - imag_main.astype(F32)).astype(BF16),
-        ],
-        axis=1,
-    )
+    spectrum = jnp.concatenate([real.astype(BF16), imag.astype(BF16)], axis=1)
     samples = basis_ref.shape[0]
-    tile = 256
-    for t in range(0, samples, tile):
-        motion = dot_rows(main, basis_ref[t : t + tile, :])
-        motion = motion + dot_rows(rest, basis_ref[t : t + tile, :])
-        motion = motion + dot_rows(main, rest_ref[t : t + tile, :])
-        motion_ref[:, t : t + tile] = motion.astype(BF16)
-    tile = 512
-
-    def one_period(q):
-        gain_re = gain_re_ref[pl.ds(q, 1), :]
-        gain_im = gain_im_ref[pl.ds(q, 1), :]
-        response = jnp.concatenate(
+    tile = samples // 4
+    copies = []
+    for i in range(4):
+        here = slice(i * tile, (i + 1) * tile)
+        motion = dot_rows(spectrum, basis_ref[here, :]) + dot_rows(spectrum, rest_ref[here, :])
+        motion_ref[:, here] = motion.astype(BF16)
+        copies.append(
+            pltpu.make_async_copy(motion_ref.at[:, here], motion_hbm.at[:, here], done.at[i])
+        )
+        copies[i].start()
+
+    def response_of(q):
+        gain_re = gain_re_ref[q : q + 1, :]
+        gain_im = gain_im_ref[q : q + 1, :]
+        return jnp.concatenate(
             [
                 (gain_re * real - gain_im * imag).astype(BF16),
                 (gain_re * imag + gain_im * real).astype(BF16),
             ],
             axis=1,
         )
+
+    def some_periods(first, number):
+        response = jnp.concatenate([response_of(first + i) for i in range(number)], axis=0)
         peak = None
         for t in range(0, samples, tile):
             wave = jnp.abs(dot_rows(basis_ref[t : t + tile, :], response))
             wave = jnp.max(wave.reshape(tile // 8, 8, wave.shape[1]), axis=0)
             peak = wave if peak is None else jnp.maximum(peak, wave)
-        peaks[pl.ds(q, 1), :] = jnp.max(peak, axis=0, keepdims=True)
+        top = jnp.max(peak, axis=0, keepdims=True)
+        columns = top.shape[1] // number
+        for i in range(number):
+            peaks[first + i : first + i + 1, :] = top[:, i * columns : (i + 1) * columns]
 
     periods = gain_re_ref.shape[0]
-    group = 20
-
-    def some_periods(i, carry):
-        for u in range(group):
-            one_period(i * group + u)
-        return carry
-
-    lax.fori_loop(0, periods // group, some_periods, 0)
-    for q in range(periods - periods % group, periods):
-        one_period(q)
+    together = 2
+    for first in range(0, periods, together):
+        some_periods(first, min(together, periods - first))
     peak_ref[...] = peaks[...].T[:, :periods]
+    for copy in copies:
+        copy.wait()
 
 
 def vmem():
@@ -437,13 +443,17 @@
     packed = pl.pallas_call(
         functools.partial(pack_slip_kernel, workers),
         out_shape=jax.ShapeDtypeStruct((workers, slip_rows + slots, LANES), BF16),
-        in_specs=[hbm(), vmem()],
-        out_specs=vmem(),
+        in_specs=[hbm(), hbm()],
+        out_specs=hbm(),
         scratch_shapes=[
             pltpu.VMEM(flat.shape, BF16),
+            pltpu.VMEM((STRAINS, slots), F32),
+            pltpu.VMEM((workers, slip_rows + slots, LANES), BF16),
             pltpu.VMEM(flat.shape, F32),
             pltpu.VMEM((LANES, LANES), F32),
             pltpu.SemaphoreType.DMA((4,)),
+            pltpu.SemaphoreType.DMA,
+            pltpu.SemaphoreType.DMA((5,)),
         ],
         compiler_params=params(58),
         name="pack_slip",
@@ -452,12 +462,12 @@
     other = lax.ppermute(own, "site", [(i, i ^ 1) for i in range(site_parts)])
     chosen = pl.pallas_call(
         choose_kernel,
-        out_shape=jax.ShapeDtypeStruct((points, total), BF16),
+        out_shape=jax.ShapeDtypeStruct((points, total), F32),
         in_specs=[vmem()],
         out_specs=vmem(),
         cost_estimate=beside(10),
         name="choose",
-    )(point_list.reshape(1, total))
+    )(point_list.reshape(1, total)).astype(BF16)
     projected = pl.pallas_call(
         functools.partial(project_kernel, workers),
         out_shape=jax.ShapeDtypeStruct((workers, proj_rows, LANES), BF16),
@@ -495,8 +505,8 @@
     partial_rows = tall * high
     spectrum = pl.pallas_call(
         functools.partial(contract_kernel, workers, tall),
-        out_shape=jax.ShapeDtypeStruct((workers, partial_rows, LANES), F32),
-        in_specs=[smem(), smem(), hbm(), vmem()],
+        out_shape=jax.ShapeDtypeStruct((workers * partial_rows, LANES), BF16),
+        in_specs=[smem(), smem(), vmem(), vmem()],
         out_specs=vmem(),
         scratch_shapes=[
             pltpu.VMEM((workers * proj_rows, LANES), F32),
@@ -504,8 +514,7 @@
             pltpu.VMEM((3, BLOCK, variations, LANES), F32),
             pltpu.VMEM((3, high // 2, workers, tall, LANES), F32),
             pltpu.VMEM((high * variations, LANES), F32),
-            pltpu.VMEM((2, capacity * variations, LANES), BF16),
-            pltpu.SemaphoreType.DMA((2,)),
+            pltpu.VMEM((high * variations, LANES), F32),
         ],
         compiler_params=params(12, spread_bytes),
         name="contract",
@@ -528,10 +537,13 @@
             jax.ShapeDtypeStruct((width, PERIODS), F32),
         ),
         in_specs=[vmem()] * 5,
-        out_specs=(vmem(), vmem()),
+        out_specs=(hbm(), vmem()),
         scratch_shapes=[
+            pltpu.VMEM(spectrum.shape, F32),
             pltpu.VMEM((2 * width, freqs), F32),
             pltpu.VMEM((LANES, width), F32),
+            pltpu.VMEM((width, NT), BF16),
+            pltpu.SemaphoreType.DMA((4,)),
         ],
         compiler_params=params(32),
         name="synthesis",

time: 67.4 us -> 63.3 us (0.939)
  Pallas kernels: 30 us -> 27.7 us
  waiting for transfers between devices: 20.5 us -> 18.6 us
  other arithmetic: 0.43 us -> 1.16 us
  local copies, waits for them, and re-layouts: 0.7 us -> 0.01 us
    pallas_call x1, Pallas kernels: 14.2 us -> 12.8 us  [per_device(): pl.pallas_call(functools.partial(synthesis_kernel, workers, tall), out_sh...]
    all_to_all x1, waiting for transfers between devices: 7.67 us -> 6.64 us  [per_device(): lax.all_to_all(spectrum, 'sub', split_axis=0, concat_axis=0, tiled=True)]
    all_to_all x1, waiting for transfers between devices: 8.24 us -> 7.5 us  [per_device(): own = lax.all_to_all(packed, 'sub', split_axis=0, concat_axis=0, tiled=True)]
    convert_element_type x0 -> x1, other arithmetic: none -> 0.73 us  [per_device(): chosen = pl.pallas_call(choose_kernel, out_shape=jax.ShapeDtypeStruct((po...]
    unnamed x8 -> x6, local copies, waits for them, and re-layouts: 0.7 us -> 0.01 us
  transfers between devices with their start and end apart: 4 -> 4, of which waited for: 4 -> 4; matrix products, arithmetic and copies ran while one was open for 1% -> 2% of each run, Pallas kernels for 8% -> 9%
where the time goes in v3:
time: 63.3 us; the launch traced here: 62.8 us
  Pallas kernels  27.7 us (44%)
  waiting for transfers between devices  18.6 us (29%)
  starting transfers between devices  14.5 us (23%)
  other arithmetic  1.16 us (2%)
  between operations  0.86 us (1%)
    pallas_call x1, Pallas kernels, per_device(): pl.pallas_call(functools.partial(synthesis_kernel, workers, tall), out_sh...  12.8 us
    all_to_all x1, waiting for transfers between devices, per_device(): own = lax.all_to_all(packed, 'sub', split_axis=0, concat_axis=0, tiled=True)  7.5 us
    all_to_all x1, starting transfers between devices, per_device(): own = lax.all_to_all(packed, 'sub', split_axis=0, concat_axis=0, tiled=True)  7.26 us
    all_to_all x1, waiting for transfers between devices, per_device(): lax.all_to_all(spectrum, 'sub', split_axis=0, concat_axis=0, tiled=True)  6.64 us
    pallas_call x1, Pallas kernels, per_device(): pl.pallas_call(functools.partial(contract_kernel, workers, tall), out_sha...  4.19 us
    pallas_call x1, Pallas kernels, per_device(): pl.pallas_call(functools.partial(gather_kernel, workers, tall, high), out...  3.65 us
    all_to_all x1, starting transfers between devices, per_device(): lax.all_to_all(projected, 'sub', split_axis=0, concat_axis=0, tiled=True)  3.59 us
    all_to_all x1, starting transfers between devices, per_device(): lax.all_to_all(spectrum, 'sub', split_axis=0, concat_axis=0, tiled=True)  3.58 us
  transfers between devices with their start and end apart: 4, of which 4 were waited for; matrix products, arithmetic and copies ran while one was open for 2% of the time, Pallas kernels for 9%

profile of v3, /device:TPU:0, one launch (start us, length us, event | category | flops | bytes accessed | tf_op | source)
XLA Modules:
  0.0 62.8 jit_solution(14046074693124783736)
XLA Ops:
  0.6 3.0 %pack_slip.1 = bf16[8,144,128]{2,1,0:T(8,128)(2,1)} custom-call(bf16[2048,128]{1,0:T(8,128)(2,1)} %bitcast.9, f32[6,16]{1,0:T(8,128)} %bitcast.10), custom_call_target="tpu_custom_call" | custom-call | tf_op jit(solution)/shard_map/pack_slip/pallas_call | solution.py:443
  3.7 7.3 %all-to-all-start = ((bf16[8,144,128]{2,1,0:T(8,128)(2,1)}), bf16[8,144,128]{2,1,0:T(8,128)(2,1)S(1)}, u32[]{:S(2)}, u32[]{:S(2)}) async-start(bf16[8,144,128]{2,1,0:T(8,128)(2,1)} %pack_slip.1), calls=%async_computation | async-start | bytes 589824 | tf_op jit(solution)/shard_map/all_to_all | solution.py:461
  10.9 0.0 copy-start
  10.9 1.4 %choose.1 = f32[16,128]{1,0:T(8,128)} custom-call(s32[1,128]{1,0:T(1,128)} %bitcast.8), custom_call_target="tpu_custom_call" | custom-call | flops 10000000000 | bytes 30000000 | tf_op jit(solution)/shard_map/choose/pallas_call | solution.py:463
  12.3 0.0 copy-start.1
  12.3 0.0 copy-start.2
  12.3 0.7 %convert_element_type.13.chosen_ref = bf16[16,128]{1,0:T(8,128)(2,1)S(1)} convert(f32[16,128]{1,0:T(8,128)} %choose.1) | non-fusion elementwise | flops 2048 | bytes 12288 | tf_op jit(solution)/shard_map/convert_element_type | solution.py:470
  13.1 7.5 %all-to-all-done.own_ref.recv_ref = bf16[8,144,128]{2,1,0:T(8,128)(2,1)S(1)} async-done(((bf16[8,144,128]{2,1,0:T(8,128)(2,1)}), bf16[8,144,128]{2,1,0:T(8,128)(2,1)S(1)}, u32[]{:S(2)}, u32[]{:S(2)}) %all-to-all-start) | async-done | bytes 294944 | tf_op jit(solution)/shard_map/all_to_all | solution.py:461
  20.6 0.0 copy-done
  20.6 2.1 %project.1 = bf16[8,128,128]{2,1,0:T(8,128)(2,1)} custom-call(bf16[16,128]{1,0:T(8,128)(2,1)S(1)} %convert_element_type.13.chosen_ref, bf16[8,144,128]{2,1,0:T(8,128)(2,1)S(1)} %all-to-all-done.own_ref.recv_ref, bf16[16,2,2,6,16,128]{5,4,3,2,1,0:T(8,128)(2,1)S(1)} %copy-done), custom_call_target="tpu_custom_call" | custom-call | tf_op jit(solution)/shard_map/project/pallas_call | solution.py:471
  22.6 3.6 %all-to-all-start.1 = ((bf16[8,128,128]{2,1,0:T(8,128)(2,1)}), bf16[8,128,128]{2,1,0:T(8,128)(2,1)S(1)}, u32[]{:S(2)}, u32[]{:S(2)}) async-start(bf16[8,128,128]{2,1,0:T(8,128)(2,1)} %project.1), calls=%async_computation.1 | async-start | bytes 524288 | tf_op jit(solution)/shard_map/all_to_all | solution.py:483
  26.2 0.1 fusion.12
  26.4 0.1 collective-permute-start
  26.5 0.2 fusion.17
  26.6 1.4 %collective-permute-done.other_ref = bf16[8,144,128]{2,1,0:T(8,128)(2,1)S(1)} collective-permute-done((bf16[8,144,128]{2,1,0:T(8,128)(2,1)S(1)}, bf16[8,144,128]{2,1,0:T(8,128)(2,1)S(1)}, u32[]{:S(2)}, u32[]{:S(2)}) %collective-permute-start) | collective-permute-done | bytes 294944 | tf_op jit(solution)/shard_map/ppermute | solution.py:462
  28.0 0.0 copy-done.1
  28.0 0.0 copy-done.2
  28.0 3.6 %gather.1 = (s32[144]{0:T(256)S(1)}, s32[1]{0:T(128)}, bf16[2,5120,128]{2,1,0:T(8,128)(2,1)S(1)}) custom-call(s32[128]{0:T(128)S(1)} %copy-done.1, s32[8]{0:T(128)S(1)} %copy-done.2, bf16[8,144,128]{2,1,0:T(8,128)(2,1)S(1)} %all-to-all-done.own_ref.recv_ref, bf16[8,144,128]{2,1,0:T(8,128)(2,1)S(1)} %collective-permute-done.other_ref), custom_call_target="tpu_custom_call" | custom-call | tf_op jit(solution)/shard_map/gather/pallas_call | solution.py:486
  31.7 3.0 %all-to-all-done.1.proj_ref = bf16[8,128,128]{2,1,0:T(8,128)(2,1)S(1)} async-done(((bf16[8,128,128]{2,1,0:T(8,128)(2,1)}), bf16[8,128,128]{2,1,0:T(8,128)(2,1)S(1)}, u32[]{:S(2)}, u32[]{:S(2)}) %all-to-all-start.1) | async-done | bytes 262176 | tf_op jit(solution)/shard_map/all_to_all | solution.py:483
  34.7 4.2 %contract.1.ready_hbm = bf16[512,128]{1,0:T(8,128)(2,1)} custom-call(s32[144]{0:T(256)S(1)} %get-tuple-element.9.start_ref, s32[1]{0:T(128)} %get-tuple-element.10.block_ref, bf16[2,5120,128]{2,1,0:T(8,128)(2,1)S(1)} %get-tuple-element.11.spread_ref, bf16[8,128,128]{2,1,0:T(8,128)(2,1)S(1)} %all-to-all-done.1.proj_ref), custom_call_target="tpu_custom_call" | custom-call | tf_op jit(solution)/shard_map/contract/pallas_call | solution.py:506
  38.9 3.6 %all-to-all-start.2 = ((bf16[8,64,128]{2,1,0:T(8,128)(2,1)}), bf16[8,64,128]{2,1,0:T(8,128)(2,1)S(1)}, u32[]{:S(2)}, u32[]{:S(2)}) async-start(bf16[8,64,128]{2,1,0:T(8,128)(2,1)} %bitcast.3), calls=%async_computation.2 | async-start | bytes 262144 | tf_op jit(solution)/shard_map/all_to_all | solution.py:531
  42.5 0.1 fusion.8
  42.6 0.6 tables.1
  43.2 6.6 %all-to-all-done.2 = bf16[8,64,128]{2,1,0:T(8,128)(2,1)S(1)} async-done(((bf16[8,64,128]{2,1,0:T(8,128)(2,1)}), bf16[8,64,128]{2,1,0:T(8,128)(2,1)S(1)}, u32[]{:S(2)}, u32[]{:S(2)}) %all-to-all-start.2) | async-done | bytes 131104 | tf_op jit(solution)/shard_map/all_to_all | solution.py:531
  49.9 12.8 %synthesis.1 = (bf16[256,2048]{1,0:T(8,128)(2,1)}, f32[256,40]{1,0:T(8,128)}) custom-call(bf16[512,128]{1,0:T(8,128)(2,1)S(1)} %bitcast.7, f32[40,128]{1,0:T(8,128)S(1)} %get-tuple-element.17.gain_re_ref, f32[40,128]{1,0:T(8,128)S(1)} %get-tuple-element.16.gain_im_ref, bf16[2048,256]{1,0:T(8,128)(2,1)S(1)} %get-tuple-element.12.basis_ref, ...), custom_call_target="tpu_custom_call" | custom-call | tf_op jit(solution)/shard_map/synthesis/pallas_call | solution.py:533
  (4 shorter events, 0.0 us)
Async XLA Ops:
  3.7 16.9 %all-to-all-start = ((bf16[8,144,128]{2,1,0:T(8,128)(2,1)}), bf16[8,144,128]{2,1,0:T(8,128)(2,1)S(1)}, u32[]{:S(2)}, u32[]{:S(2)}) async-start(bf16[8,144,128]{2,1,0:T(8,128)(2,1)} %pack_slip.1), calls=%async_computation | async-start | bytes 589824 | tf_op jit(solution)/shard_map/all_to_all | solution.py:461
  10.9 9.6 %copy-start = (bf16[16,2,2,6,16,128]{5,4,3,2,1,0:T(8,128)(2,1)S(1)}, bf16[16,2,2,6,16,128]{5,4,3,2,1,0:T(8,128)(2,1)}, u32[]{:S(2)}) copy-start(bf16[16,2,2,6,16,128]{5,4,3,2,1,0:T(8,128)(2,1)} %sgt_ref.1) | copy-start | bytes 4718596
  12.3 15.7 %copy-start.1 = (s32[128]{0:T(128)S(1)}, s32[128]{0:T(128)}, u32[]{:S(2)}) copy-start(s32[128]{0:T(128)} %point_ref.1) | copy-start | bytes 1540
  12.3 15.7 %copy-start.2 = (s32[8]{0:T(128)S(1)}, s32[8]{0:T(128)}, u32[]{:S(2)}) copy-start(s32[8]{0:T(128)} %count_ref.1) | copy-start | bytes 100
  22.6 12.1 %all-to-all-start.1 = ((bf16[8,128,128]{2,1,0:T(8,128)(2,1)}), bf16[8,128,128]{2,1,0:T(8,128)(2,1)S(1)}, u32[]{:S(2)}, u32[]{:S(2)}) async-start(bf16[8,128,128]{2,1,0:T(8,128)(2,1)} %project.1), calls=%async_computation.1 | async-start | bytes 524288 | tf_op jit(solution)/shard_map/all_to_all | solution.py:483
  26.4 1.6 %collective-permute-start = (bf16[8,144,128]{2,1,0:T(8,128)(2,1)S(1)}, bf16[8,144,128]{2,1,0:T(8,128)(2,1)S(1)}, u32[]{:S(2)}, u32[]{:S(2)}) collective-permute-start(bf16[8,144,128]{2,1,0:T(8,128)(2,1)S(1)} %all-to-all-done.own_ref.recv_ref), channel_id=1, source_target_pairs={{0,1},{1,0},{2,3},{3,2},{4,5},{5,4},{6,7},{7,6},{8,9},{9,8},{10,11... | collective-permute-start | bytes 884744 | tf_op jit(solution)/shard_map/ppermute | solution.py:462
  38.9 10.9 %all-to-all-start.2 = ((bf16[8,64,128]{2,1,0:T(8,128)(2,1)}), bf16[8,64,128]{2,1,0:T(8,128)(2,1)S(1)}, u32[]{:S(2)}, u32[]{:S(2)}) async-start(bf16[8,64,128]{2,1,0:T(8,128)(2,1)} %bitcast.3), calls=%async_computation.2 | async-start | bytes 262144 | tf_op jit(solution)/shard_map/all_to_all | solution.py:531

commit v4 on v3

--- a/solution.py
+++ b/solution.py
@@ -45,22 +45,20 @@
     return (-squared_natural * real_part / magnitude, squared_natural * imag_part / magnitude)
 
 
+def roll_groups(array, groups, count):
+    shift = (groups % count) * (LANES // count)
+    return pltpu.roll(array, shift, 1) if shift else array
+
+
 def swap_blocks(parts):
     count = len(parts)
-    width = LANES // count
-    parts = list(parts)
-    group = lax.broadcasted_iota(jnp.int32, parts[0].shape, 1) // width
+    group = lax.broadcasted_iota(jnp.int32, parts[0].shape, 1) // (LANES // count)
     step = 1
     while step < count:
-        low_lanes = (group & step) == 0
-        for x in range(count):
-            if x & step:
-                continue
-            low, high = parts[x], parts[x | step]
-            parts[x] = jnp.where(low_lanes, low, pltpu.roll(high, width * step, 1))
-            parts[x | step] = jnp.where(low_lanes, pltpu.roll(low, LANES - width * step, 1), high)
+        own = (group & step) == 0
+        parts = [jnp.where(own, parts[i], parts[(i + step) % count]) for i in range(count)]
         step *= 2
-    return parts
+    return [parts[-d % count] for d in range(count)]
 
 
 def pack_slip_kernel(workers, slip_hbm, mech_hbm, out_hbm, narrow, mech_ref, out_ref, wide, padded, done, mech_done, sent):
@@ -103,11 +101,17 @@
         wide[here, :] = narrow[here, :].astype(F32)
         for start in range(i * height, (i + 1) * height, chunk):
             parts = [
-                wide[pl.ds(start * stride + 2 * x + core, chunk, stride=stride), :]
+                roll_groups(
+                    wide[pl.ds(start * stride + 2 * x + core, chunk, stride=stride), :].astype(
+                        BF16
+                    ),
+                    x,
+                    workers,
+                )
                 for x in range(workers)
             ]
             for d, part in enumerate(swap_blocks(parts)):
-                out_ref[d, start : start + chunk, :] = part.astype(BF16)
+                out_ref[d, start : start + chunk, :] = part
         sends[i].start()
     for send in sends:
         send.wait()
@@ -157,10 +161,13 @@
     chunk = 16
     for start in range(0, rows, chunk):
         parts = [
-            wide[pl.ds(start * workers + x, chunk, stride=workers), :] for x in range(workers)
+            roll_groups(
+                wide[pl.ds(start * workers + x, chunk, stride=workers), :].astype(BF16), x, workers
+            )
+            for x in range(workers)
         ]
         for d, part in enumerate(swap_blocks(parts)):
-            out_ref[d, start : start + chunk, :] = part.astype(BF16)
+            out_ref[d, start : start + chunk, :] = part
 
 
 def gather_kernel(
@@ -208,6 +215,7 @@
         line_ref[amount + extra] = 0
 
     width = LANES // workers
+    me = lax.axis_index("sub")
     group = lax.broadcasted_iota(jnp.int32, (tall, LANES), 1) // width
     row_ids = lax.broadcasted_iota(jnp.int32, (LANES, LANES), 0)
     lane_ids = lax.broadcasted_iota(jnp.int32, (LANES, LANES), 1)
@@ -220,7 +228,7 @@
                 packed = slip[p, pl.ds(pl.multiple_of(line_ref[index], tall), tall), :]
                 for x in range(workers):
                     wide[i, p, x * tall : (x + 1) * tall, :] = jnp.where(
-                        (group == x) & (index < amount), packed, 0.0
+                        (group == lax.rem(x + me, workers)) & (index < amount), packed, 0.0
                     )
         for i in range(GROUP):
             start = pl.multiple_of((step * GROUP + i) * height, height)
@@ -350,11 +358,13 @@
 ):
     freqs = natural.shape[1]
     rows = recv_ref.shape[0] // workers
-    received[...] = recv_ref[...].astype(F32)
-    for x, part in enumerate(
-        swap_blocks([received[w * rows : (w + 1) * rows, :] for w in range(workers)])
-    ):
-        natural[pl.ds(x, rows, stride=workers), :] = part
+    if rows % 16:
+        received[...] = recv_ref[...].astype(F32)
+        parts = [received[w * rows : (w + 1) * rows, :] for w in range(workers)]
+    else:
+        parts = [recv_ref[w * rows : (w + 1) * rows, :] for w in range(workers)]
+    for x, part in enumerate(swap_blocks(parts)):
+        natural[pl.ds(x, rows, stride=workers), :] = roll_groups(part, -x, workers).astype(F32)
     width = natural.shape[0] // (2 * tall)
     real = jnp.concatenate(
         [natural[(2 * v) * width : (2 * v + 1) * width, :] for v in range(tall)], axis=0

time: 63.3 us -> 62.1 us (0.981)
  Pallas kernels: 27.7 us -> 26.4 us
where the time goes in v4:
time: 62.1 us; the launch traced here: 61.6 us
  Pallas kernels  26.4 us (43%)
  waiting for transfers between devices  18.6 us (30%)
  starting transfers between devices  14.5 us (23%)
  other arithmetic  1.16 us (2%)
  between operations  0.86 us (1%)
    pallas_call x1, Pallas kernels, per_device(): pl.pallas_call(functools.partial(synthesis_kernel, workers, tall), out_sh...  12.6 us
    all_to_all x1, waiting for transfers between devices, per_device(): own = lax.all_to_all(packed, 'sub', split_axis=0, concat_axis=0, tiled=True)  7.5 us
    all_to_all x1, starting transfers between devices, per_device(): own = lax.all_to_all(packed, 'sub', split_axis=0, concat_axis=0, tiled=True)  7.26 us
    all_to_all x1, waiting for transfers between devices, per_device(): lax.all_to_all(spectrum, 'sub', split_axis=0, concat_axis=0, tiled=True)  6.64 us
    pallas_call x1, Pallas kernels, per_device(): pl.pallas_call(functools.partial(contract_kernel, workers, tall), out_sha...  4.2 us
    pallas_call x1, Pallas kernels, per_device(): pl.pallas_call(functools.partial(gather_kernel, workers, tall, high), out...  3.65 us
    all_to_all x1, starting transfers between devices, per_device(): lax.all_to_all(projected, 'sub', split_axis=0, concat_axis=0, tiled=True)  3.59 us
    all_to_all x1, starting transfers between devices, per_device(): lax.all_to_all(spectrum, 'sub', split_axis=0, concat_axis=0, tiled=True)  3.58 us
  transfers between devices with their start and end apart: 4, of which 4 were waited for; matrix products, arithmetic and copies ran while one was open for 2% of the time, Pallas kernels for 9%

profile of v4, /device:TPU:0, one launch (start us, length us, event | category | flops | bytes accessed | tf_op | source)
XLA Modules:
  0.0 61.6 jit_solution(4832487276970592091)
XLA Ops:
  0.6 2.4 %pack_slip.1 = bf16[8,144,128]{2,1,0:T(8,128)(2,1)} custom-call(bf16[2048,128]{1,0:T(8,128)(2,1)} %bitcast.9, f32[6,16]{1,0:T(8,128)} %bitcast.10), custom_call_target="tpu_custom_call" | custom-call | tf_op jit(solution)/shard_map/pack_slip/pallas_call | solution.py:453
  3.1 7.3 %all-to-all-start = ((bf16[8,144,128]{2,1,0:T(8,128)(2,1)}), bf16[8,144,128]{2,1,0:T(8,128)(2,1)S(1)}, u32[]{:S(2)}, u32[]{:S(2)}) async-start(bf16[8,144,128]{2,1,0:T(8,128)(2,1)} %pack_slip.1), calls=%async_computation | async-start | bytes 589824 | tf_op jit(solution)/shard_map/all_to_all | solution.py:471
  10.3 0.0 copy-start
  10.4 1.4 %choose.1 = f32[16,128]{1,0:T(8,128)} custom-call(s32[1,128]{1,0:T(1,128)} %bitcast.8), custom_call_target="tpu_custom_call" | custom-call | flops 10000000000 | bytes 30000000 | tf_op jit(solution)/shard_map/choose/pallas_call | solution.py:473
  11.7 0.0 copy-start.1
  11.7 0.0 copy-start.2
  11.7 0.7 %convert_element_type.13.chosen_ref = bf16[16,128]{1,0:T(8,128)(2,1)S(1)} convert(f32[16,128]{1,0:T(8,128)} %choose.1) | non-fusion elementwise | flops 2048 | bytes 12288 | tf_op jit(solution)/shard_map/convert_element_type | solution.py:480
  12.5 7.5 %all-to-all-done.own_ref.recv_ref = bf16[8,144,128]{2,1,0:T(8,128)(2,1)S(1)} async-done(((bf16[8,144,128]{2,1,0:T(8,128)(2,1)}), bf16[8,144,128]{2,1,0:T(8,128)(2,1)S(1)}, u32[]{:S(2)}, u32[]{:S(2)}) %all-to-all-start) | async-done | bytes 294944 | tf_op jit(solution)/shard_map/all_to_all | solution.py:471
  20.0 0.0 copy-done
  20.0 1.6 %project.1 = bf16[8,128,128]{2,1,0:T(8,128)(2,1)} custom-call(bf16[16,128]{1,0:T(8,128)(2,1)S(1)} %convert_element_type.13.chosen_ref, bf16[8,144,128]{2,1,0:T(8,128)(2,1)S(1)} %all-to-all-done.own_ref.recv_ref, bf16[16,2,2,6,16,128]{5,4,3,2,1,0:T(8,128)(2,1)S(1)} %copy-done), custom_call_target="tpu_custom_call" | custom-call | tf_op jit(solution)/shard_map/project/pallas_call | solution.py:481
  21.6 3.6 %all-to-all-start.1 = ((bf16[8,128,128]{2,1,0:T(8,128)(2,1)}), bf16[8,128,128]{2,1,0:T(8,128)(2,1)S(1)}, u32[]{:S(2)}, u32[]{:S(2)}) async-start(bf16[8,128,128]{2,1,0:T(8,128)(2,1)} %project.1), calls=%async_computation.1 | async-start | bytes 524288 | tf_op jit(solution)/shard_map/all_to_all | solution.py:493
  25.2 0.1 fusion.12
  25.3 0.1 collective-permute-start
  25.4 0.2 fusion.17
  25.6 1.4 %collective-permute-done.other_ref = bf16[8,144,128]{2,1,0:T(8,128)(2,1)S(1)} collective-permute-done((bf16[8,144,128]{2,1,0:T(8,128)(2,1)S(1)}, bf16[8,144,128]{2,1,0:T(8,128)(2,1)S(1)}, u32[]{:S(2)}, u32[]{:S(2)}) %collective-permute-start) | collective-permute-done | bytes 294944 | tf_op jit(solution)/shard_map/ppermute | solution.py:472
  27.0 0.0 copy-done.1
  27.0 0.0 copy-done.2
  27.0 3.6 %gather.1 = (s32[144]{0:T(256)S(1)}, s32[1]{0:T(128)}, bf16[2,5120,128]{2,1,0:T(8,128)(2,1)S(1)}) custom-call(s32[128]{0:T(128)S(1)} %copy-done.1, s32[8]{0:T(128)S(1)} %copy-done.2, bf16[8,144,128]{2,1,0:T(8,128)(2,1)S(1)} %all-to-all-done.own_ref.recv_ref, bf16[8,144,128]{2,1,0:T(8,128)(2,1)S(1)} %collective-permute-done.other_ref), custom_call_target="tpu_custom_call" | custom-call | tf_op jit(solution)/shard_map/gather/pallas_call | solution.py:496
  30.6 3.0 %all-to-all-done.1.proj_ref = bf16[8,128,128]{2,1,0:T(8,128)(2,1)S(1)} async-done(((bf16[8,128,128]{2,1,0:T(8,128)(2,1)}), bf16[8,128,128]{2,1,0:T(8,128)(2,1)S(1)}, u32[]{:S(2)}, u32[]{:S(2)}) %all-to-all-start.1) | async-done | bytes 262176 | tf_op jit(solution)/shard_map/all_to_all | solution.py:493
  33.7 4.2 %contract.1.ready_hbm = bf16[512,128]{1,0:T(8,128)(2,1)} custom-call(s32[144]{0:T(256)S(1)} %get-tuple-element.9.start_ref, s32[1]{0:T(128)} %get-tuple-element.10.block_ref, bf16[2,5120,128]{2,1,0:T(8,128)(2,1)S(1)} %get-tuple-element.11.spread_ref, bf16[8,128,128]{2,1,0:T(8,128)(2,1)S(1)} %all-to-all-done.1.proj_ref), custom_call_target="tpu_custom_call" | custom-call | tf_op jit(solution)/shard_map/contract/pallas_call | solution.py:516
  37.9 3.6 %all-to-all-start.2 = ((bf16[8,64,128]{2,1,0:T(8,128)(2,1)}), bf16[8,64,128]{2,1,0:T(8,128)(2,1)S(1)}, u32[]{:S(2)}, u32[]{:S(2)}) async-start(bf16[8,64,128]{2,1,0:T(8,128)(2,1)} %bitcast.3), calls=%async_computation.2 | async-start | bytes 262144 | tf_op jit(solution)/shard_map/all_to_all | solution.py:541
  41.5 0.1 fusion.8
  41.6 0.6 tables.1
  42.2 6.6 %all-to-all-done.2 = bf16[8,64,128]{2,1,0:T(8,128)(2,1)S(1)} async-done(((bf16[8,64,128]{2,1,0:T(8,128)(2,1)}), bf16[8,64,128]{2,1,0:T(8,128)(2,1)S(1)}, u32[]{:S(2)}, u32[]{:S(2)}) %all-to-all-start.2) | async-done | bytes 131104 | tf_op jit(solution)/shard_map/all_to_all | solution.py:541
  48.8 12.6 %synthesis.1 = (bf16[256,2048]{1,0:T(8,128)(2,1)}, f32[256,40]{1,0:T(8,128)}) custom-call(bf16[512,128]{1,0:T(8,128)(2,1)S(1)} %bitcast.7, f32[40,128]{1,0:T(8,128)S(1)} %get-tuple-element.17.gain_re_ref, f32[40,128]{1,0:T(8,128)S(1)} %get-tuple-element.16.gain_im_ref, bf16[2048,256]{1,0:T(8,128)(2,1)S(1)} %get-tuple-element.12.basis_ref, ...), custom_call_target="tpu_custom_call" | custom-call | tf_op jit(solution)/shard_map/synthesis/pallas_call | solution.py:543
  (4 shorter events, 0.0 us)
Async XLA Ops:
  3.1 16.9 %all-to-all-start = ((bf16[8,144,128]{2,1,0:T(8,128)(2,1)}), bf16[8,144,128]{2,1,0:T(8,128)(2,1)S(1)}, u32[]{:S(2)}, u32[]{:S(2)}) async-start(bf16[8,144,128]{2,1,0:T(8,128)(2,1)} %pack_slip.1), calls=%async_computation | async-start | bytes 589824 | tf_op jit(solution)/shard_map/all_to_all | solution.py:471
  10.3 9.6 %copy-start = (bf16[16,2,2,6,16,128]{5,4,3,2,1,0:T(8,128)(2,1)S(1)}, bf16[16,2,2,6,16,128]{5,4,3,2,1,0:T(8,128)(2,1)}, u32[]{:S(2)}) copy-start(bf16[16,2,2,6,16,128]{5,4,3,2,1,0:T(8,128)(2,1)} %sgt_ref.1) | copy-start | bytes 4718596
  11.7 15.2 %copy-start.1 = (s32[128]{0:T(128)S(1)}, s32[128]{0:T(128)}, u32[]{:S(2)}) copy-start(s32[128]{0:T(128)} %point_ref.1) | copy-start | bytes 1540
  11.7 15.2 %copy-start.2 = (s32[8]{0:T(128)S(1)}, s32[8]{0:T(128)}, u32[]{:S(2)}) copy-start(s32[8]{0:T(128)} %count_ref.1) | copy-start | bytes 100
  21.6 12.1 %all-to-all-start.1 = ((bf16[8,128,128]{2,1,0:T(8,128)(2,1)}), bf16[8,128,128]{2,1,0:T(8,128)(2,1)S(1)}, u32[]{:S(2)}, u32[]{:S(2)}) async-start(bf16[8,128,128]{2,1,0:T(8,128)(2,1)} %project.1), calls=%async_computation.1 | async-start | bytes 524288 | tf_op jit(solution)/shard_map/all_to_all | solution.py:493
  25.3 1.6 %collective-permute-start = (bf16[8,144,128]{2,1,0:T(8,128)(2,1)S(1)}, bf16[8,144,128]{2,1,0:T(8,128)(2,1)S(1)}, u32[]{:S(2)}, u32[]{:S(2)}) collective-permute-start(bf16[8,144,128]{2,1,0:T(8,128)(2,1)S(1)} %all-to-all-done.own_ref.recv_ref), channel_id=1, source_target_pairs={{0,1},{1,0},{2,3},{3,2},{4,5},{5,4},{6,7},{7,6},{8,9},{9,8},{10,11... | collective-permute-start | bytes 884744 | tf_op jit(solution)/shard_map/ppermute | solution.py:472
  37.9 10.9 %all-to-all-start.2 = ((bf16[8,64,128]{2,1,0:T(8,128)(2,1)}), bf16[8,64,128]{2,1,0:T(8,128)(2,1)S(1)}, u32[]{:S(2)}, u32[]{:S(2)}) async-start(bf16[8,64,128]{2,1,0:T(8,128)(2,1)} %bitcast.3), calls=%async_computation.2 | async-start | bytes 262144 | tf_op jit(solution)/shard_map/all_to_all | solution.py:541

commit v5 on v4

--- a/solution.py
+++ b/solution.py
@@ -117,12 +117,33 @@
         send.wait()
 
 
-def choose_kernel(point_ref, chosen_ref):
+def choose_kernel(
+    workers, tall, high, point_ref, slots_ref, count_ref, chosen_ref, start_ref, line_ref
+):
     points, total = chosen_ref.shape
+    slots = total // workers
     point_ids = lax.axis_index("sub") * points + lax.broadcasted_iota(
         jnp.int32, (points, total), 0
     )
     chosen_ref[...] = (point_ref[...] == point_ids).astype(F32)
+
+    def note_worker(w, filled):
+        def note_slot(k, carry):
+            j = w * slots + k
+            start_ref[filled + k] = slots_ref[j] * high
+            line_ref[filled + k] = j * tall
+            return carry
+
+        count = count_ref[w]
+        lax.fori_loop(0, count, note_slot, 0)
+        return filled + count
+
+    amount = lax.fori_loop(0, workers, note_worker, 0)
+    for extra in range(GROUP):
+        start_ref[amount + extra] = 0
+        line_ref[amount + extra] = 0
+    start_ref[total + GROUP] = (amount + 2 * BLOCK - 1) // (2 * BLOCK)
+    line_ref[total + GROUP] = amount
 
 
 def project_kernel(workers, chosen_ref, recv_ref, sgt_ref, out_ref, moments, wide):
@@ -170,50 +191,16 @@
             out_ref[d, start : start + chunk, :] = part
 
 
-def gather_kernel(
-    workers,
-    tall,
-    high,
-    point_ref,
-    count_ref,
-    own_ref,
-    other_ref,
-    start_ref,
-    block_ref,
-    spread_hbm,
-    slip,
-    line_ref,
-    wide,
-    spread_ref,
-    done,
-):
+def gather_kernel(workers, tall, line_ref, own_ref, other_ref, spread_ref, slip, wide):
     core = lax.rem(lax.axis_index("site"), 2)
-    total = point_ref.shape[0]
-    slots = total // workers
-    slip_rows = slots * tall
+    total = line_ref.shape[0] - GROUP - 1
+    amount = line_ref[total + GROUP]
+    slip_rows = total // workers * tall
     height = workers * tall
     for w in range(workers):
         here = slice(w * slip_rows, (w + 1) * slip_rows)
         slip[core, here, :] = own_ref[w, :slip_rows, :].astype(F32)
         slip[1 - core, here, :] = other_ref[w, :slip_rows, :].astype(F32)
-
-    def note_worker(w, filled):
-        def note_slot(k, carry):
-            j = w * slots + k
-            start_ref[filled + k] = point_ref[j] * high
-            line_ref[filled + k] = j * tall
-            return carry
-
-        count = count_ref[w]
-        lax.fori_loop(0, count, note_slot, 0)
-        return filled + count
-
-    amount = lax.fori_loop(0, workers, note_worker, 0)
-    blocks = (amount + 2 * BLOCK - 1) // (2 * BLOCK)
-    for extra in range(GROUP):
-        start_ref[amount + extra] = 0
-        line_ref[amount + extra] = 0
-
     width = LANES // workers
     me = lax.axis_index("sub")
     group = lax.broadcasted_iota(jnp.int32, (tall, LANES), 1) // width
@@ -239,14 +226,10 @@
         return carry
 
     lax.fori_loop(0, (amount + GROUP - 1) // GROUP, spread_slots, 0)
-    block_ref[0] = blocks
-    copy = pltpu.make_async_copy(spread_ref, spread_hbm, done)
-    copy.start()
-    copy.wait()
 
 
 def contract_kernel(
-    workers, tall, start_ref, block_ref, spread_ref, proj_ref, out_ref, proj, even, odd, total, ordered, outgoing
+    workers, tall, start_ref, spread_ref, proj_ref, out_ref, proj, even, odd, total, ordered, outgoing
 ):
     proj_rows = proj_ref.shape[1]
     high = ordered.shape[0] // (workers * tall)
@@ -298,7 +281,7 @@
         add_block(first + BLOCK, odd)
         return carry
 
-    lax.fori_loop(0, block_ref[0], add_two_blocks, 0)
+    lax.fori_loop(0, start_ref[start_ref.shape[0] - 1], add_two_blocks, 0)
     for y in range(half):
         for x in range(workers):
             shared = total[0, y, x]
@@ -470,14 +453,19 @@
     )(flat, mechanism.T)
     own = lax.all_to_all(packed, "sub", split_axis=0, concat_axis=0, tiled=True)
     other = lax.ppermute(own, "site", [(i, i ^ 1) for i in range(site_parts)])
-    chosen = pl.pallas_call(
-        choose_kernel,
-        out_shape=jax.ShapeDtypeStruct((points, total), F32),
-        in_specs=[vmem()],
-        out_specs=vmem(),
+    chosen, starts, lines = pl.pallas_call(
+        functools.partial(choose_kernel, workers, tall, high),
+        out_shape=(
+            jax.ShapeDtypeStruct((points, total), F32),
+            jax.ShapeDtypeStruct((total + GROUP + 1,), jnp.int32),
+            jax.ShapeDtypeStruct((total + GROUP + 1,), jnp.int32),
+        ),
+        in_specs=[vmem(), smem(), smem()],
+        out_specs=(vmem(), smem(), smem()),
         cost_estimate=beside(10),
         name="choose",
-    )(point_list.reshape(1, total)).astype(BF16)
+    )(point_list.reshape(1, total), point_list, subfault_counts)
+    chosen = chosen.astype(BF16)
     projected = pl.pallas_call(
         functools.partial(project_kernel, workers),
         out_shape=jax.ShapeDtypeStruct((workers, proj_rows, LANES), BF16),
@@ -493,30 +481,23 @@
     chunks = lax.all_to_all(projected, "sub", split_axis=0, concat_axis=0, tiled=True)
     capacity = total // 2 + GROUP
     spread_bytes = 2 * capacity * variations * LANES * 2
-    starts, blocks, spread = pl.pallas_call(
-        functools.partial(gather_kernel, workers, tall, high),
-        out_shape=(
-            jax.ShapeDtypeStruct((total + GROUP,), jnp.int32),
-            jax.ShapeDtypeStruct((1,), jnp.int32),
-            jax.ShapeDtypeStruct((2, capacity * variations, LANES), BF16),
-        ),
-        in_specs=[smem(), smem(), vmem(), vmem()],
-        out_specs=(smem(), smem(), hbm()),
+    spread = pl.pallas_call(
+        functools.partial(gather_kernel, workers, tall),
+        out_shape=jax.ShapeDtypeStruct((2, capacity * variations, LANES), BF16),
+        in_specs=[smem(), vmem(), vmem()],
+        out_specs=vmem(),
         scratch_shapes=[
             pltpu.VMEM((2, workers * slip_rows, LANES), F32),
-            pltpu.SMEM((total + GROUP,), jnp.int32),
             pltpu.VMEM((GROUP, 2, variations, LANES), F32),
-            pltpu.VMEM((2, capacity * variations, LANES), BF16),
-            pltpu.SemaphoreType.DMA,
         ],
         compiler_params=params(16, spread_bytes),
         name="gather",
-    )(point_list, subfault_counts, own, other)
+    )(lines, own, other)
     partial_rows = tall * high
     spectrum = pl.pallas_call(
         functools.partial(contract_kernel, workers, tall),
         out_shape=jax.ShapeDtypeStruct((workers * partial_rows, LANES), BF16),
-        in_specs=[smem(), smem(), vmem(), vmem()],
+        in_specs=[smem(), vmem(), vmem()],
         out_specs=vmem(),
         scratch_shapes=[
             pltpu.VMEM((workers * proj_rows, LANES), F32),
@@ -528,7 +509,7 @@
         ],
         compiler_params=params(12, spread_bytes),
         name="contract",
-    )(starts, blocks, spread, chunks)
+    )(starts, spread, chunks)
     basis, basis_rest = pl.pallas_call(
         tables_kernel,
         out_shape=(jax.ShapeDtypeStruct((NT, 2 * freqs), BF16),) * 2,

time: 62.1 us -> 61.5 us (level)
  Pallas kernels: 26.4 us -> 25.1 us
  waiting for transfers between devices: 18.6 us -> 19.4 us
    all_to_all x1, waiting for transfers between devices: 3.05 us -> 4.43 us  [per_device(): lax.all_to_all(projected, 'sub', split_axis=0, concat_axis=0, tiled=True)]
    pallas_call x2, Pallas kernels: 5.02 us -> 4.25 us  [the longest x1 2.26 us: per_device(): pl.pallas_call(functools.partial(gather_kernel, workers, tall), out_shape...]
  transfers between devices with their start and end apart: 4 -> 4, of which waited for: 4 -> 4; matrix products, arithmetic and copies ran while one was open for 2% -> 2% of each run, Pallas kernels for 9% -> 8%
where the time goes in v5:
time: 61.5 us; the launch traced here: 61 us
  Pallas kernels  25.1 us (41%)
  waiting for transfers between devices  19.4 us (32%)
  starting transfers between devices  14.5 us (24%)
  other arithmetic  1.14 us (2%)
  between operations  0.87 us (1%)
    pallas_call x1, Pallas kernels, per_device(): pl.pallas_call(functools.partial(synthesis_kernel, workers, tall), out_sh...  12.6 us
    all_to_all x1, starting transfers between devices, per_device(): own = lax.all_to_all(packed, 'sub', split_axis=0, concat_axis=0, tiled=True)  7.26 us
    all_to_all x1, waiting for transfers between devices, per_device(): own = lax.all_to_all(packed, 'sub', split_axis=0, concat_axis=0, tiled=True)  6.9 us
    all_to_all x1, waiting for transfers between devices, per_device(): lax.all_to_all(spectrum, 'sub', split_axis=0, concat_axis=0, tiled=True)  6.64 us
    all_to_all x1, waiting for transfers between devices, per_device(): lax.all_to_all(projected, 'sub', split_axis=0, concat_axis=0, tiled=True)  4.43 us
    pallas_call x1, Pallas kernels, per_device(): pl.pallas_call(functools.partial(contract_kernel, workers, tall), out_sha...  3.66 us
    all_to_all x1, starting transfers between devices, per_device(): lax.all_to_all(projected, 'sub', split_axis=0, concat_axis=0, tiled=True)  3.59 us
    all_to_all x1, starting transfers between devices, per_device(): lax.all_to_all(spectrum, 'sub', split_axis=0, concat_axis=0, tiled=True)  3.58 us
  transfers between devices with their start and end apart: 4, of which 4 were waited for; matrix products, arithmetic and copies ran while one was open for 2% of the time, Pallas kernels for 8%

profile of v5, /device:TPU:0, one launch (start us, length us, event | category | flops | bytes accessed | tf_op | source)
XLA Modules:
  0.0 61.0 jit_solution(5247378895711179243)
XLA Ops:
  0.6 2.4 %pack_slip.1 = bf16[8,144,128]{2,1,0:T(8,128)(2,1)} custom-call(bf16[2048,128]{1,0:T(8,128)(2,1)} %bitcast.8, f32[6,16]{1,0:T(8,128)} %bitcast.9), custom_call_target="tpu_custom_call" | custom-call | tf_op jit(solution)/shard_map/pack_slip/pallas_call | solution.py:436
  3.1 7.3 %all-to-all-start = ((bf16[8,144,128]{2,1,0:T(8,128)(2,1)}), bf16[8,144,128]{2,1,0:T(8,128)(2,1)S(1)}, u32[]{:S(2)}, u32[]{:S(2)}) async-start(bf16[8,144,128]{2,1,0:T(8,128)(2,1)} %pack_slip.1), calls=%async_computation | async-start | bytes 589824 | tf_op jit(solution)/shard_map/all_to_all | solution.py:454
  10.3 0.0 copy-start
  10.4 2.0 %choose.1 = (f32[16,128]{1,0:T(8,128)}, s32[145]{0:T(256)}, s32[145]{0:T(256)}) custom-call(s32[1,128]{1,0:T(1,128)} %bitcast.12, s32[128]{0:T(128)} %slots_ref.1, s32[8]{0:T(128)} %count_ref.1), custom_call_target="tpu_custom_call" | custom-call | flops 10000000000 | bytes 30000000 | tf_op jit(solution)/shard_map/choose/pallas_call | solution.py:456
  12.3 0.0 copy-start.2
  12.4 0.7 %convert_element_type.13.chosen_ref = bf16[16,128]{1,0:T(8,128)(2,1)S(1)} convert(f32[16,128]{1,0:T(8,128)} %get-tuple-element.11) | non-fusion elementwise | flops 2048 | bytes 12288 | tf_op jit(solution)/shard_map/convert_element_type | solution.py:468
  13.1 0.0 copy-start.1
  13.1 6.9 %all-to-all-done.own_ref.recv_ref = bf16[8,144,128]{2,1,0:T(8,128)(2,1)S(1)} async-done(((bf16[8,144,128]{2,1,0:T(8,128)(2,1)}), bf16[8,144,128]{2,1,0:T(8,128)(2,1)S(1)}, u32[]{:S(2)}, u32[]{:S(2)}) %all-to-all-start) | async-done | bytes 294944 | tf_op jit(solution)/shard_map/all_to_all | solution.py:454
  20.0 0.0 copy-done
  20.0 1.6 %project.1 = bf16[8,128,128]{2,1,0:T(8,128)(2,1)} custom-call(bf16[16,128]{1,0:T(8,128)(2,1)S(1)} %convert_element_type.13.chosen_ref, bf16[8,144,128]{2,1,0:T(8,128)(2,1)S(1)} %all-to-all-done.own_ref.recv_ref, bf16[16,2,2,6,16,128]{5,4,3,2,1,0:T(8,128)(2,1)S(1)} %copy-done), custom_call_target="tpu_custom_call" | custom-call | tf_op jit(solution)/shard_map/project/pallas_call | solution.py:469
  21.6 3.6 %all-to-all-start.1 = ((bf16[8,128,128]{2,1,0:T(8,128)(2,1)}), bf16[8,128,128]{2,1,0:T(8,128)(2,1)S(1)}, u32[]{:S(2)}, u32[]{:S(2)}) async-start(bf16[8,128,128]{2,1,0:T(8,128)(2,1)} %project.1), calls=%async_computation.1 | async-start | bytes 524288 | tf_op jit(solution)/shard_map/all_to_all | solution.py:481
  25.2 0.1 fusion.12
  25.3 0.1 collective-permute-start
  25.4 0.2 fusion.17
  25.6 1.4 %collective-permute-done.other_ref = bf16[8,144,128]{2,1,0:T(8,128)(2,1)S(1)} collective-permute-done((bf16[8,144,128]{2,1,0:T(8,128)(2,1)S(1)}, bf16[8,144,128]{2,1,0:T(8,128)(2,1)S(1)}, u32[]{:S(2)}, u32[]{:S(2)}) %collective-permute-start) | collective-permute-done | bytes 294944 | tf_op jit(solution)/shard_map/ppermute | solution.py:455
  27.0 0.0 copy-done.2
  27.0 2.3 %gather.1.spread_ref = bf16[2,5120,128]{2,1,0:T(8,128)(2,1)S(1)} custom-call(s32[145]{0:T(256)S(1)} %copy-done.2, bf16[8,144,128]{2,1,0:T(8,128)(2,1)S(1)} %all-to-all-done.own_ref.recv_ref, bf16[8,144,128]{2,1,0:T(8,128)(2,1)S(1)} %collective-permute-done.other_ref), custom_call_target="tpu_custom_call" | custom-call | tf_op jit(solution)/shard_map/gather/pallas_call | solution.py:484
  29.2 4.4 %all-to-all-done.1.proj_ref = bf16[8,128,128]{2,1,0:T(8,128)(2,1)S(1)} async-done(((bf16[8,128,128]{2,1,0:T(8,128)(2,1)}), bf16[8,128,128]{2,1,0:T(8,128)(2,1)S(1)}, u32[]{:S(2)}, u32[]{:S(2)}) %all-to-all-start.1) | async-done | bytes 262176 | tf_op jit(solution)/shard_map/all_to_all | solution.py:481
  33.7 0.0 copy-done.1
  33.7 3.7 %contract.1.ready_hbm = bf16[512,128]{1,0:T(8,128)(2,1)} custom-call(s32[145]{0:T(256)S(1)} %copy-done.1, bf16[2,5120,128]{2,1,0:T(8,128)(2,1)S(1)} %gather.1.spread_ref, bf16[8,128,128]{2,1,0:T(8,128)(2,1)S(1)} %all-to-all-done.1.proj_ref), custom_call_target="tpu_custom_call" | custom-call | tf_op jit(solution)/shard_map/contract/pallas_call | solution.py:497
  37.3 3.6 %all-to-all-start.2 = ((bf16[8,64,128]{2,1,0:T(8,128)(2,1)}), bf16[8,64,128]{2,1,0:T(8,128)(2,1)S(1)}, u32[]{:S(2)}, u32[]{:S(2)}) async-start(bf16[8,64,128]{2,1,0:T(8,128)(2,1)} %bitcast.3), calls=%async_computation.2 | async-start | bytes 262144 | tf_op jit(solution)/shard_map/all_to_all | solution.py:522
  40.9 0.1 fusion.8
  41.0 0.6 tables.1
  41.6 6.6 %all-to-all-done.2 = bf16[8,64,128]{2,1,0:T(8,128)(2,1)S(1)} async-done(((bf16[8,64,128]{2,1,0:T(8,128)(2,1)}), bf16[8,64,128]{2,1,0:T(8,128)(2,1)S(1)}, u32[]{:S(2)}, u32[]{:S(2)}) %all-to-all-start.2) | async-done | bytes 131104 | tf_op jit(solution)/shard_map/all_to_all | solution.py:522
  48.3 12.6 %synthesis.1 = (bf16[256,2048]{1,0:T(8,128)(2,1)}, f32[256,40]{1,0:T(8,128)}) custom-call(bf16[512,128]{1,0:T(8,128)(2,1)S(1)} %bitcast.7, f32[40,128]{1,0:T(8,128)S(1)} %get-tuple-element.17.gain_re_ref, f32[40,128]{1,0:T(8,128)S(1)} %get-tuple-element.16.gain_im_ref, bf16[2048,256]{1,0:T(8,128)(2,1)S(1)} %get-tuple-element.12.basis_ref, ...), custom_call_target="tpu_custom_call" | custom-call | tf_op jit(solution)/shard_map/synthesis/pallas_call | solution.py:524
  (4 shorter events, 0.0 us)
Async XLA Ops:
  3.1 16.9 %all-to-all-start = ((bf16[8,144,128]{2,1,0:T(8,128)(2,1)}), bf16[8,144,128]{2,1,0:T(8,128)(2,1)S(1)}, u32[]{:S(2)}, u32[]{:S(2)}) async-start(bf16[8,144,128]{2,1,0:T(8,128)(2,1)} %pack_slip.1), calls=%async_computation | async-start | bytes 589824 | tf_op jit(solution)/shard_map/all_to_all | solution.py:454
  10.3 9.6 %copy-start = (bf16[16,2,2,6,16,128]{5,4,3,2,1,0:T(8,128)(2,1)S(1)}, bf16[16,2,2,6,16,128]{5,4,3,2,1,0:T(8,128)(2,1)}, u32[]{:S(2)}) copy-start(bf16[16,2,2,6,16,128]{5,4,3,2,1,0:T(8,128)(2,1)} %sgt_ref.1) | copy-start | bytes 4718596
  12.3 14.6 %copy-start.2 = (s32[145]{0:T(256)S(1)}, s32[145]{0:T(256)}, u32[]{:S(2)}) copy-start(s32[145]{0:T(256)} %get-tuple-element.10.line_ref) | copy-start | bytes 1744
  13.1 20.6 %copy-start.1 = (s32[145]{0:T(256)S(1)}, s32[145]{0:T(256)}, u32[]{:S(2)}) copy-start(s32[145]{0:T(256)} %get-tuple-element.9.start_ref) | copy-start | bytes 1744
  21.6 12.1 %all-to-all-start.1 = ((bf16[8,128,128]{2,1,0:T(8,128)(2,1)}), bf16[8,128,128]{2,1,0:T(8,128)(2,1)S(1)}, u32[]{:S(2)}, u32[]{:S(2)}) async-start(bf16[8,128,128]{2,1,0:T(8,128)(2,1)} %project.1), calls=%async_computation.1 | async-start | bytes 524288 | tf_op jit(solution)/shard_map/all_to_all | solution.py:481
  25.3 1.6 %collective-permute-start = (bf16[8,144,128]{2,1,0:T(8,128)(2,1)S(1)}, bf16[8,144,128]{2,1,0:T(8,128)(2,1)S(1)}, u32[]{:S(2)}, u32[]{:S(2)}) collective-permute-start(bf16[8,144,128]{2,1,0:T(8,128)(2,1)S(1)} %all-to-all-done.own_ref.recv_ref), channel_id=1, source_target_pairs={{0,1},{1,0},{2,3},{3,2},{4,5},{5,4},{6,7},{7,6},{8,9},{9,8},{10,11... | collective-permute-start | bytes 884744 | tf_op jit(solution)/shard_map/ppermute | solution.py:455
  37.3 10.9 %all-to-all-start.2 = ((bf16[8,64,128]{2,1,0:T(8,128)(2,1)}), bf16[8,64,128]{2,1,0:T(8,128)(2,1)S(1)}, u32[]{:S(2)}, u32[]{:S(2)}) async-start(bf16[8,64,128]{2,1,0:T(8,128)(2,1)} %bitcast.3), calls=%async_computation.2 | async-start | bytes 262144 | tf_op jit(solution)/shard_map/all_to_all | solution.py:522

commit v6 on v5

--- a/solution.py
+++ b/solution.py
@@ -66,6 +66,8 @@
     stride = 2 * workers
     slots = mech_ref.shape[1]
     rows = out_ref.shape[1] - slots
+    tall = rows // slots
+    block = slip_hbm.shape[0] // slots
     pieces = done.shape[0]
     height = rows // pieces
     copies = []
@@ -100,16 +102,16 @@
         here = pl.ds(i * height * stride, height * stride)
         wide[here, :] = narrow[here, :].astype(F32)
         for start in range(i * height, (i + 1) * height, chunk):
-            parts = [
-                roll_groups(
-                    wide[pl.ds(start * stride + 2 * x + core, chunk, stride=stride), :].astype(
-                        BF16
-                    ),
-                    x,
-                    workers,
+            first = start // tall
+            parts = []
+            for x in range(workers):
+                lines = [
+                    wide[pl.ds(j * block + 2 * x * tall + core, tall, stride=2), :]
+                    for j in range(first, first + chunk // tall)
+                ]
+                parts.append(
+                    roll_groups(jnp.concatenate(lines, axis=0).astype(BF16), x, workers)
                 )
-                for x in range(workers)
-            ]
             for d, part in enumerate(swap_blocks(parts)):
                 out_ref[d, start : start + chunk, :] = part
         sends[i].start()
@@ -146,7 +148,9 @@
     line_ref[total + GROUP] = amount
 
 
-def project_kernel(workers, chosen_ref, recv_ref, sgt_ref, out_ref, moments, wide):
+def project_kernel(
+    workers, chosen_ref, recv_ref, sgt_ref, out_hbm, out_ref, moments, wide, sent
+):
     points = sgt_ref.shape[0]
     sites = sgt_ref.shape[4]
     mech_start = recv_ref.shape[1] - chosen_ref.shape[1] // workers
@@ -170,25 +174,41 @@
                 start = pl.multiple_of(row * height + (2 * p + c) * sites, sites)
                 wide[pl.ds(start, sites), :] = combined.astype(BF16).astype(F32)
 
-    group = 8
+    rows = out_ref.shape[1]
+    pieces = sent.shape[0]
+    group = 4
+    chunk = 16
 
     def some_points(step, carry):
         for u in range(group):
             one_point(step * group + u)
         return carry
 
-    lax.fori_loop(0, points // group, some_points, 0)
-    rows = out_ref.shape[1]
-    chunk = 16
-    for start in range(0, rows, chunk):
-        parts = [
-            roll_groups(
-                wide[pl.ds(start * workers + x, chunk, stride=workers), :].astype(BF16), x, workers
-            )
-            for x in range(workers)
-        ]
-        for d, part in enumerate(swap_blocks(parts)):
-            out_ref[d, start : start + chunk, :] = part
+    sends = []
+    for i in range(pieces):
+        steps = points // pieces // group
+        if steps == 1:
+            some_points(i, 0)
+        else:
+            lax.fori_loop(i * steps, (i + 1) * steps, some_points, 0)
+        for start in range(i * rows // pieces, (i + 1) * rows // pieces, chunk):
+            parts = [
+                roll_groups(
+                    wide[pl.ds(start * workers + x, chunk, stride=workers), :].astype(BF16),
+                    x,
+                    workers,
+                )
+                for x in range(workers)
+            ]
+            for d, part in enumerate(swap_blocks(parts)):
+                out_ref[d, start : start + chunk, :] = part
+        here = pl.ds(i * rows // pieces, rows // pieces)
+        sends.append(
+            pltpu.make_async_copy(out_ref.at[:, here, :], out_hbm.at[:, here, :], sent.at[i])
+        )
+        sends[i].start()
+    for send in sends:
+        send.wait()
 
 
 def gather_kernel(workers, tall, line_ref, own_ref, other_ref, spread_ref, slip, wide):
@@ -229,10 +249,10 @@
 
 
 def contract_kernel(
-    workers, tall, start_ref, spread_ref, proj_ref, out_ref, proj, even, odd, total, ordered, outgoing
+    workers, tall, start_ref, spread_ref, proj_ref, out_ref, proj, even, odd, total, outgoing
 ):
     proj_rows = proj_ref.shape[1]
-    high = ordered.shape[0] // (workers * tall)
+    high = outgoing.shape[0] // (workers * tall)
     half = high // 2
     variations = workers * tall
     lines = min(2, half)
@@ -285,16 +305,10 @@
     for y in range(half):
         for x in range(workers):
             shared = total[0, y, x]
-            at_real = (y * workers + x) * tall
-            at_imag = ((half + y) * workers + x) * tall
-            ordered[at_real : at_real + tall, :] = shared - total[1, y, x]
-            ordered[at_imag : at_imag + tall, :] = shared + total[2, y, x]
-    for d in range(workers):
-        for v in range(tall):
-            y, x = divmod(d * tall + v, workers)
-            outgoing[(d * tall + v) * high : (d * tall + v + 1) * high, :] = ordered[
-                pl.ds(x * tall + y, high, stride=variations), :
-            ]
+            at_real = (x * high + y) * tall
+            at_imag = (x * high + half + y) * tall
+            outgoing[at_real : at_real + tall, :] = shared - total[1, y, x]
+            outgoing[at_imag : at_imag + tall, :] = shared + total[2, y, x]
     out_ref[...] = outgoing[...].astype(BF16)
 
 
@@ -341,20 +355,28 @@
 ):
     freqs = natural.shape[1]
     rows = recv_ref.shape[0] // workers
+    high = rows // tall
     if rows % 16:
         received[...] = recv_ref[...].astype(F32)
         parts = [received[w * rows : (w + 1) * rows, :] for w in range(workers)]
     else:
         parts = [recv_ref[w * rows : (w + 1) * rows, :] for w in range(workers)]
     for x, part in enumerate(swap_blocks(parts)):
-        natural[pl.ds(x, rows, stride=workers), :] = roll_groups(part, -x, workers).astype(F32)
-    width = natural.shape[0] // (2 * tall)
-    real = jnp.concatenate(
-        [natural[(2 * v) * width : (2 * v + 1) * width, :] for v in range(tall)], axis=0
-    )
-    imag = jnp.concatenate(
-        [natural[(2 * v + 1) * width : (2 * v + 2) * width, :] for v in range(tall)], axis=0
-    )
+        part = roll_groups(part, -x, workers).astype(F32)
+        for r in range(high):
+            start = (r * workers + x) * tall
+            natural[start : start + tall, :] = part[r * tall : (r + 1) * tall, :]
+    real, imag = [
+        jnp.concatenate(
+            [
+                natural[pl.ds(r * workers * tall + v, workers, stride=tall), :]
+                for v in range(tall)
+                for r in range(first, first + high // 2)
+            ],
+            axis=0,
+        )
+        for first in (0, high // 2)
+    ]
     spectrum = jnp.concatenate([real.astype(BF16), imag.astype(BF16)], axis=1)
     samples = basis_ref.shape[0]
     tile = samples // 4
@@ -470,10 +492,12 @@
         functools.partial(project_kernel, workers),
         out_shape=jax.ShapeDtypeStruct((workers, proj_rows, LANES), BF16),
         in_specs=[vmem(), vmem(), vmem()],
-        out_specs=vmem(),
+        out_specs=hbm(),
         scratch_shapes=[
+            pltpu.VMEM((workers, proj_rows, LANES), BF16),
             pltpu.VMEM((points, LANES), F32),
             pltpu.VMEM((proj_rows * workers, LANES), F32),
+            pltpu.SemaphoreType.DMA((4,)),
         ],
         compiler_params=params(24),
         name="project",
@@ -504,7 +528,6 @@
             pltpu.VMEM((3, BLOCK, variations, LANES), F32),
             pltpu.VMEM((3, BLOCK, variations, LANES), F32),
             pltpu.VMEM((3, high // 2, workers, tall, LANES), F32),
-            pltpu.VMEM((high * variations, LANES), F32),
             pltpu.VMEM((high * variations, LANES), F32),
         ],
         compiler_params=params(12, spread_bytes),

time: 61.5 us -> 61 us (level)
  no operation moved by 1% of the time
where the time goes in v6:
time: 61 us; the launch traced here: 60.5 us
  Pallas kernels  24.6 us (40%)
  waiting for transfers between devices  19.4 us (32%)
  starting transfers between devices  14.5 us (24%)
  other arithmetic  1.14 us (2%)
  between operations  0.88 us (1%)
    pallas_call x1, Pallas kernels, per_device(): pl.pallas_call(functools.partial(synthesis_kernel, workers, tall), out_sh...  12.6 us
    all_to_all x1, starting transfers between devices, per_device(): own = lax.all_to_all(packed, 'sub', split_axis=0, concat_axis=0, tiled=True)  7.26 us
    all_to_all x1, waiting for transfers between devices, per_device(): own = lax.all_to_all(packed, 'sub', split_axis=0, concat_axis=0, tiled=True)  6.9 us
    all_to_all x1, waiting for transfers between devices, per_device(): lax.all_to_all(spectrum, 'sub', split_axis=0, concat_axis=0, tiled=True)  6.64 us
    all_to_all x1, waiting for transfers between devices, per_device(): lax.all_to_all(projected, 'sub', split_axis=0, concat_axis=0, tiled=True)  4.43 us
    all_to_all x1, starting transfers between devices, per_device(): lax.all_to_all(projected, 'sub', split_axis=0, concat_axis=0, tiled=True)  3.6 us
    all_to_all x1, starting transfers between devices, per_device(): lax.all_to_all(spectrum, 'sub', split_axis=0, concat_axis=0, tiled=True)  3.58 us
    pallas_call x1, Pallas kernels, per_device(): pl.pallas_call(functools.partial(contract_kernel, workers, tall), out_sha...  3.45 us
  transfers between devices with their start and end apart: 4, of which 4 were waited for; matrix products, arithmetic and copies ran while one was open for 2% of the time, Pallas kernels for 8%

profile of v6, /device:TPU:0, one launch (start us, length us, event | category | flops | bytes accessed | tf_op | source)
XLA Modules:
  0.0 60.5 jit_solution(17920689678487073290)
XLA Ops:
  0.6 2.3 %pack_slip.1 = bf16[8,144,128]{2,1,0:T(8,128)(2,1)} custom-call(bf16[2048,128]{1,0:T(8,128)(2,1)} %bitcast.8, f32[6,16]{1,0:T(8,128)} %bitcast.9), custom_call_target="tpu_custom_call" | custom-call | tf_op jit(solution)/shard_map/pack_slip/pallas_call | solution.py:458
  2.9 7.3 %all-to-all-start = ((bf16[8,144,128]{2,1,0:T(8,128)(2,1)}), bf16[8,144,128]{2,1,0:T(8,128)(2,1)S(1)}, u32[]{:S(2)}, u32[]{:S(2)}) async-start(bf16[8,144,128]{2,1,0:T(8,128)(2,1)} %pack_slip.1), calls=%async_computation | async-start | bytes 589824 | tf_op jit(solution)/shard_map/all_to_all | solution.py:476
  10.2 0.0 copy-start
  10.2 2.0 %choose.1 = (f32[16,128]{1,0:T(8,128)}, s32[145]{0:T(256)}, s32[145]{0:T(256)}) custom-call(s32[1,128]{1,0:T(1,128)} %bitcast.12, s32[128]{0:T(128)} %slots_ref.1, s32[8]{0:T(128)} %count_ref.1), custom_call_target="tpu_custom_call" | custom-call | flops 10000000000 | bytes 30000000 | tf_op jit(solution)/shard_map/choose/pallas_call | solution.py:478
  12.2 0.0 copy-start.2
  12.2 0.7 %convert_element_type.13.chosen_ref = bf16[16,128]{1,0:T(8,128)(2,1)S(1)} convert(f32[16,128]{1,0:T(8,128)} %get-tuple-element.11) | non-fusion elementwise | flops 2048 | bytes 12288 | tf_op jit(solution)/shard_map/convert_element_type | solution.py:490
  12.9 0.0 copy-start.1
  12.9 6.9 %all-to-all-done.own_ref.recv_ref = bf16[8,144,128]{2,1,0:T(8,128)(2,1)S(1)} async-done(((bf16[8,144,128]{2,1,0:T(8,128)(2,1)}), bf16[8,144,128]{2,1,0:T(8,128)(2,1)S(1)}, u32[]{:S(2)}, u32[]{:S(2)}) %all-to-all-start) | async-done | bytes 294944 | tf_op jit(solution)/shard_map/all_to_all | solution.py:476
  19.8 0.0 copy-done
  19.8 1.4 %project.1 = bf16[8,128,128]{2,1,0:T(8,128)(2,1)} custom-call(bf16[16,128]{1,0:T(8,128)(2,1)S(1)} %convert_element_type.13.chosen_ref, bf16[8,144,128]{2,1,0:T(8,128)(2,1)S(1)} %all-to-all-done.own_ref.recv_ref, bf16[16,2,2,6,16,128]{5,4,3,2,1,0:T(8,128)(2,1)S(1)} %copy-done), custom_call_target="tpu_custom_call" | custom-call | tf_op jit(solution)/shard_map/project/pallas_call | solution.py:491
  21.2 3.6 %all-to-all-start.1 = ((bf16[8,128,128]{2,1,0:T(8,128)(2,1)}), bf16[8,128,128]{2,1,0:T(8,128)(2,1)S(1)}, u32[]{:S(2)}, u32[]{:S(2)}) async-start(bf16[8,128,128]{2,1,0:T(8,128)(2,1)} %project.1), calls=%async_computation.1 | async-start | bytes 524288 | tf_op jit(solution)/shard_map/all_to_all | solution.py:505
  24.8 0.1 fusion.12
  25.0 0.1 collective-permute-start
  25.1 0.2 fusion.17
  25.2 1.4 %collective-permute-done.other_ref = bf16[8,144,128]{2,1,0:T(8,128)(2,1)S(1)} collective-permute-done((bf16[8,144,128]{2,1,0:T(8,128)(2,1)S(1)}, bf16[8,144,128]{2,1,0:T(8,128)(2,1)S(1)}, u32[]{:S(2)}, u32[]{:S(2)}) %collective-permute-start) | collective-permute-done | bytes 294944 | tf_op jit(solution)/shard_map/ppermute | solution.py:477
  26.6 0.0 copy-done.2
  26.6 2.3 %gather.1.spread_ref = bf16[2,5120,128]{2,1,0:T(8,128)(2,1)S(1)} custom-call(s32[145]{0:T(256)S(1)} %copy-done.2, bf16[8,144,128]{2,1,0:T(8,128)(2,1)S(1)} %all-to-all-done.own_ref.recv_ref, bf16[8,144,128]{2,1,0:T(8,128)(2,1)S(1)} %collective-permute-done.other_ref), custom_call_target="tpu_custom_call" | custom-call | tf_op jit(solution)/shard_map/gather/pallas_call | solution.py:508
  28.9 4.4 %all-to-all-done.1.proj_ref = bf16[8,128,128]{2,1,0:T(8,128)(2,1)S(1)} async-done(((bf16[8,128,128]{2,1,0:T(8,128)(2,1)}), bf16[8,128,128]{2,1,0:T(8,128)(2,1)S(1)}, u32[]{:S(2)}, u32[]{:S(2)}) %all-to-all-start.1) | async-done | bytes 262176 | tf_op jit(solution)/shard_map/all_to_all | solution.py:505
  33.4 0.0 copy-done.1
  33.4 3.4 %contract.1.ready_hbm = bf16[512,128]{1,0:T(8,128)(2,1)} custom-call(s32[145]{0:T(256)S(1)} %copy-done.1, bf16[2,5120,128]{2,1,0:T(8,128)(2,1)S(1)} %gather.1.spread_ref, bf16[8,128,128]{2,1,0:T(8,128)(2,1)S(1)} %all-to-all-done.1.proj_ref), custom_call_target="tpu_custom_call" | custom-call | tf_op jit(solution)/shard_map/contract/pallas_call | solution.py:521
  36.8 3.6 %all-to-all-start.2 = ((bf16[8,64,128]{2,1,0:T(8,128)(2,1)}), bf16[8,64,128]{2,1,0:T(8,128)(2,1)S(1)}, u32[]{:S(2)}, u32[]{:S(2)}) async-start(bf16[8,64,128]{2,1,0:T(8,128)(2,1)} %bitcast.3), calls=%async_computation.2 | async-start | bytes 262144 | tf_op jit(solution)/shard_map/all_to_all | solution.py:545
  40.4 0.1 fusion.8
  40.5 0.6 tables.1
  41.1 6.6 %all-to-all-done.2 = bf16[8,64,128]{2,1,0:T(8,128)(2,1)S(1)} async-done(((bf16[8,64,128]{2,1,0:T(8,128)(2,1)}), bf16[8,64,128]{2,1,0:T(8,128)(2,1)S(1)}, u32[]{:S(2)}, u32[]{:S(2)}) %all-to-all-start.2) | async-done | bytes 131104 | tf_op jit(solution)/shard_map/all_to_all | solution.py:545
  47.7 12.6 %synthesis.1 = (bf16[256,2048]{1,0:T(8,128)(2,1)}, f32[256,40]{1,0:T(8,128)}) custom-call(bf16[512,128]{1,0:T(8,128)(2,1)S(1)} %bitcast.7, f32[40,128]{1,0:T(8,128)S(1)} %get-tuple-element.17.gain_re_ref, f32[40,128]{1,0:T(8,128)S(1)} %get-tuple-element.16.gain_im_ref, bf16[2048,256]{1,0:T(8,128)(2,1)S(1)} %get-tuple-element.12.basis_ref, ...), custom_call_target="tpu_custom_call" | custom-call | tf_op jit(solution)/shard_map/synthesis/pallas_call | solution.py:547
  (4 shorter events, 0.0 us)
Async XLA Ops:
  2.9 16.9 %all-to-all-start = ((bf16[8,144,128]{2,1,0:T(8,128)(2,1)}), bf16[8,144,128]{2,1,0:T(8,128)(2,1)S(1)}, u32[]{:S(2)}, u32[]{:S(2)}) async-start(bf16[8,144,128]{2,1,0:T(8,128)(2,1)} %pack_slip.1), calls=%async_computation | async-start | bytes 589824 | tf_op jit(solution)/shard_map/all_to_all | solution.py:476
  10.2 9.6 %copy-start = (bf16[16,2,2,6,16,128]{5,4,3,2,1,0:T(8,128)(2,1)S(1)}, bf16[16,2,2,6,16,128]{5,4,3,2,1,0:T(8,128)(2,1)}, u32[]{:S(2)}) copy-start(bf16[16,2,2,6,16,128]{5,4,3,2,1,0:T(8,128)(2,1)} %sgt_ref.1) | copy-start | bytes 4718596
  12.2 14.5 %copy-start.2 = (s32[145]{0:T(256)S(1)}, s32[145]{0:T(256)}, u32[]{:S(2)}) copy-start(s32[145]{0:T(256)} %get-tuple-element.10.line_ref) | copy-start | bytes 1744
  12.9 20.5 %copy-start.1 = (s32[145]{0:T(256)S(1)}, s32[145]{0:T(256)}, u32[]{:S(2)}) copy-start(s32[145]{0:T(256)} %get-tuple-element.9.start_ref) | copy-start | bytes 1744
  21.2 12.1 %all-to-all-start.1 = ((bf16[8,128,128]{2,1,0:T(8,128)(2,1)}), bf16[8,128,128]{2,1,0:T(8,128)(2,1)S(1)}, u32[]{:S(2)}, u32[]{:S(2)}) async-start(bf16[8,128,128]{2,1,0:T(8,128)(2,1)} %project.1), calls=%async_computation.1 | async-start | bytes 524288 | tf_op jit(solution)/shard_map/all_to_all | solution.py:505
  25.0 1.6 %collective-permute-start = (bf16[8,144,128]{2,1,0:T(8,128)(2,1)S(1)}, bf16[8,144,128]{2,1,0:T(8,128)(2,1)S(1)}, u32[]{:S(2)}, u32[]{:S(2)}) collective-permute-start(bf16[8,144,128]{2,1,0:T(8,128)(2,1)S(1)} %all-to-all-done.own_ref.recv_ref), channel_id=1, source_target_pairs={{0,1},{1,0},{2,3},{3,2},{4,5},{5,4},{6,7},{7,6},{8,9},{9,8},{10,11... | collective-permute-start | bytes 884744 | tf_op jit(solution)/shard_map/ppermute | solution.py:477
  36.8 10.9 %all-to-all-start.2 = ((bf16[8,64,128]{2,1,0:T(8,128)(2,1)}), bf16[8,64,128]{2,1,0:T(8,128)(2,1)S(1)}, u32[]{:S(2)}, u32[]{:S(2)}) async-start(bf16[8,64,128]{2,1,0:T(8,128)(2,1)} %bitcast.3), calls=%async_computation.2 | async-start | bytes 262144 | tf_op jit(solution)/shard_map/all_to_all | solution.py:545

commit v7 on v6

--- a/solution.py
+++ b/solution.py
@@ -464,7 +464,7 @@
             pltpu.VMEM(flat.shape, BF16),
             pltpu.VMEM((STRAINS, slots), F32),
             pltpu.VMEM((workers, slip_rows + slots, LANES), BF16),
-            pltpu.VMEM(flat.shape, F32),
+            pltpu.VMEM((flat.shape[0] + 2 * tall, freqs), F32),
             pltpu.VMEM((LANES, LANES), F32),
             pltpu.SemaphoreType.DMA((4,)),
             pltpu.SemaphoreType.DMA,
@@ -496,7 +496,7 @@
         scratch_shapes=[
             pltpu.VMEM((workers, proj_rows, LANES), BF16),
             pltpu.VMEM((points, LANES), F32),
-            pltpu.VMEM((proj_rows * workers, LANES), F32),
+            pltpu.VMEM((proj_rows * workers + workers, LANES), F32),
             pltpu.SemaphoreType.DMA((4,)),
         ],
         compiler_params=params(24),
@@ -554,7 +554,7 @@
         out_specs=(hbm(), vmem()),
         scratch_shapes=[
             pltpu.VMEM(spectrum.shape, F32),
-            pltpu.VMEM((2 * width, freqs), F32),
+            pltpu.VMEM((2 * width + workers, freqs), F32),
             pltpu.VMEM((LANES, width), F32),
             pltpu.VMEM((width, NT), BF16),
             pltpu.SemaphoreType.DMA((4,)),

time: 61 us -> 61 us (level)
  no operation moved by 1% of the time
where the time goes in v7:
time: 61 us; the launch traced here: 60.5 us
  Pallas kernels  24.6 us (40%)
  waiting for transfers between devices  19.4 us (32%)
  starting transfers between devices  14.5 us (24%)
  other arithmetic  1.14 us (2%)
  between operations  0.88 us (1%)
    pallas_call x1, Pallas kernels, per_device(): pl.pallas_call(functools.partial(synthesis_kernel, workers, tall), out_sh...  12.6 us
    all_to_all x1, starting transfers between devices, per_device(): own = lax.all_to_all(packed, 'sub', split_axis=0, concat_axis=0, tiled=True)  7.26 us
    all_to_all x1, waiting for transfers between devices, per_device(): own = lax.all_to_all(packed, 'sub', split_axis=0, concat_axis=0, tiled=True)  6.9 us
    all_to_all x1, waiting for transfers between devices, per_device(): lax.all_to_all(spectrum, 'sub', split_axis=0, concat_axis=0, tiled=True)  6.64 us
    all_to_all x1, waiting for transfers between devices, per_device(): lax.all_to_all(projected, 'sub', split_axis=0, concat_axis=0, tiled=True)  4.43 us
    all_to_all x1, starting transfers between devices, per_device(): lax.all_to_all(projected, 'sub', split_axis=0, concat_axis=0, tiled=True)  3.6 us
    all_to_all x1, starting transfers between devices, per_device(): lax.all_to_all(spectrum, 'sub', split_axis=0, concat_axis=0, tiled=True)  3.58 us
    pallas_call x1, Pallas kernels, per_device(): pl.pallas_call(functools.partial(contract_kernel, workers, tall), out_sha...  3.45 us
  transfers between devices with their start and end apart: 4, of which 4 were waited for; matrix products, arithmetic and copies ran while one was open for 2% of the time, Pallas kernels for 8%

profile of v7, /device:TPU:0, one launch (start us, length us, event | category | flops | bytes accessed | tf_op | source)
XLA Modules:
  0.0 60.5 jit_solution(1656098075899098417)
XLA Ops:
  0.6 2.3 %pack_slip.1 = bf16[8,144,128]{2,1,0:T(8,128)(2,1)} custom-call(bf16[2048,128]{1,0:T(8,128)(2,1)} %bitcast.8, f32[6,16]{1,0:T(8,128)} %bitcast.9), custom_call_target="tpu_custom_call" | custom-call | tf_op jit(solution)/shard_map/pack_slip/pallas_call | solution.py:458
  2.9 7.3 %all-to-all-start = ((bf16[8,144,128]{2,1,0:T(8,128)(2,1)}), bf16[8,144,128]{2,1,0:T(8,128)(2,1)S(1)}, u32[]{:S(2)}, u32[]{:S(2)}) async-start(bf16[8,144,128]{2,1,0:T(8,128)(2,1)} %pack_slip.1), calls=%async_computation | async-start | bytes 589824 | tf_op jit(solution)/shard_map/all_to_all | solution.py:476
  10.2 0.0 copy-start
  10.2 2.0 %choose.1 = (f32[16,128]{1,0:T(8,128)}, s32[145]{0:T(256)}, s32[145]{0:T(256)}) custom-call(s32[1,128]{1,0:T(1,128)} %bitcast.12, s32[128]{0:T(128)} %slots_ref.1, s32[8]{0:T(128)} %count_ref.1), custom_call_target="tpu_custom_call" | custom-call | flops 10000000000 | bytes 30000000 | tf_op jit(solution)/shard_map/choose/pallas_call | solution.py:478
  12.2 0.0 copy-start.2
  12.2 0.7 %convert_element_type.13.chosen_ref = bf16[16,128]{1,0:T(8,128)(2,1)S(1)} convert(f32[16,128]{1,0:T(8,128)} %get-tuple-element.11) | non-fusion elementwise | flops 2048 | bytes 12288 | tf_op jit(solution)/shard_map/convert_element_type | solution.py:490
  12.9 0.0 copy-start.1
  12.9 6.9 %all-to-all-done.own_ref.recv_ref = bf16[8,144,128]{2,1,0:T(8,128)(2,1)S(1)} async-done(((bf16[8,144,128]{2,1,0:T(8,128)(2,1)}), bf16[8,144,128]{2,1,0:T(8,128)(2,1)S(1)}, u32[]{:S(2)}, u32[]{:S(2)}) %all-to-all-start) | async-done | bytes 294944 | tf_op jit(solution)/shard_map/all_to_all | solution.py:476
  19.8 0.0 copy-done
  19.8 1.4 %project.1 = bf16[8,128,128]{2,1,0:T(8,128)(2,1)} custom-call(bf16[16,128]{1,0:T(8,128)(2,1)S(1)} %convert_element_type.13.chosen_ref, bf16[8,144,128]{2,1,0:T(8,128)(2,1)S(1)} %all-to-all-done.own_ref.recv_ref, bf16[16,2,2,6,16,128]{5,4,3,2,1,0:T(8,128)(2,1)S(1)} %copy-done), custom_call_target="tpu_custom_call" | custom-call | tf_op jit(solution)/shard_map/project/pallas_call | solution.py:491
  21.2 3.6 %all-to-all-start.1 = ((bf16[8,128,128]{2,1,0:T(8,128)(2,1)}), bf16[8,128,128]{2,1,0:T(8,128)(2,1)S(1)}, u32[]{:S(2)}, u32[]{:S(2)}) async-start(bf16[8,128,128]{2,1,0:T(8,128)(2,1)} %project.1), calls=%async_computation.1 | async-start | bytes 524288 | tf_op jit(solution)/shard_map/all_to_all | solution.py:505
  24.8 0.1 fusion.12
  25.0 0.1 collective-permute-start
  25.1 0.2 fusion.17
  25.2 1.4 %collective-permute-done.other_ref = bf16[8,144,128]{2,1,0:T(8,128)(2,1)S(1)} collective-permute-done((bf16[8,144,128]{2,1,0:T(8,128)(2,1)S(1)}, bf16[8,144,128]{2,1,0:T(8,128)(2,1)S(1)}, u32[]{:S(2)}, u32[]{:S(2)}) %collective-permute-start) | collective-permute-done | bytes 294944 | tf_op jit(solution)/shard_map/ppermute | solution.py:477
  26.6 0.0 copy-done.2
  26.6 2.3 %gather.1.spread_ref = bf16[2,5120,128]{2,1,0:T(8,128)(2,1)S(1)} custom-call(s32[145]{0:T(256)S(1)} %copy-done.2, bf16[8,144,128]{2,1,0:T(8,128)(2,1)S(1)} %all-to-all-done.own_ref.recv_ref, bf16[8,144,128]{2,1,0:T(8,128)(2,1)S(1)} %collective-permute-done.other_ref), custom_call_target="tpu_custom_call" | custom-call | tf_op jit(solution)/shard_map/gather/pallas_call | solution.py:508
  28.9 4.4 %all-to-all-done.1.proj_ref = bf16[8,128,128]{2,1,0:T(8,128)(2,1)S(1)} async-done(((bf16[8,128,128]{2,1,0:T(8,128)(2,1)}), bf16[8,128,128]{2,1,0:T(8,128)(2,1)S(1)}, u32[]{:S(2)}, u32[]{:S(2)}) %all-to-all-start.1) | async-done | bytes 262176 | tf_op jit(solution)/shard_map/all_to_all | solution.py:505
  33.4 0.0 copy-done.1
  33.4 3.4 %contract.1.ready_hbm = bf16[512,128]{1,0:T(8,128)(2,1)} custom-call(s32[145]{0:T(256)S(1)} %copy-done.1, bf16[2,5120,128]{2,1,0:T(8,128)(2,1)S(1)} %gather.1.spread_ref, bf16[8,128,128]{2,1,0:T(8,128)(2,1)S(1)} %all-to-all-done.1.proj_ref), custom_call_target="tpu_custom_call" | custom-call | tf_op jit(solution)/shard_map/contract/pallas_call | solution.py:521
  36.8 3.6 %all-to-all-start.2 = ((bf16[8,64,128]{2,1,0:T(8,128)(2,1)}), bf16[8,64,128]{2,1,0:T(8,128)(2,1)S(1)}, u32[]{:S(2)}, u32[]{:S(2)}) async-start(bf16[8,64,128]{2,1,0:T(8,128)(2,1)} %bitcast.3), calls=%async_computation.2 | async-start | bytes 262144 | tf_op jit(solution)/shard_map/all_to_all | solution.py:545
  40.4 0.1 fusion.8
  40.5 0.6 tables.1
  41.1 6.6 %all-to-all-done.2 = bf16[8,64,128]{2,1,0:T(8,128)(2,1)S(1)} async-done(((bf16[8,64,128]{2,1,0:T(8,128)(2,1)}), bf16[8,64,128]{2,1,0:T(8,128)(2,1)S(1)}, u32[]{:S(2)}, u32[]{:S(2)}) %all-to-all-start.2) | async-done | bytes 131104 | tf_op jit(solution)/shard_map/all_to_all | solution.py:545
  47.7 12.6 %synthesis.1 = (bf16[256,2048]{1,0:T(8,128)(2,1)}, f32[256,40]{1,0:T(8,128)}) custom-call(bf16[512,128]{1,0:T(8,128)(2,1)S(1)} %bitcast.7, f32[40,128]{1,0:T(8,128)S(1)} %get-tuple-element.17.gain_re_ref, f32[40,128]{1,0:T(8,128)S(1)} %get-tuple-element.16.gain_im_ref, bf16[2048,256]{1,0:T(8,128)(2,1)S(1)} %get-tuple-element.12.basis_ref, ...), custom_call_target="tpu_custom_call" | custom-call | tf_op jit(solution)/shard_map/synthesis/pallas_call | solution.py:547
  (4 shorter events, 0.0 us)
Async XLA Ops:
  2.9 16.9 %all-to-all-start = ((bf16[8,144,128]{2,1,0:T(8,128)(2,1)}), bf16[8,144,128]{2,1,0:T(8,128)(2,1)S(1)}, u32[]{:S(2)}, u32[]{:S(2)}) async-start(bf16[8,144,128]{2,1,0:T(8,128)(2,1)} %pack_slip.1), calls=%async_computation | async-start | bytes 589824 | tf_op jit(solution)/shard_map/all_to_all | solution.py:476
  10.2 9.6 %copy-start = (bf16[16,2,2,6,16,128]{5,4,3,2,1,0:T(8,128)(2,1)S(1)}, bf16[16,2,2,6,16,128]{5,4,3,2,1,0:T(8,128)(2,1)}, u32[]{:S(2)}) copy-start(bf16[16,2,2,6,16,128]{5,4,3,2,1,0:T(8,128)(2,1)} %sgt_ref.1) | copy-start | bytes 4718596
  12.2 14.5 %copy-start.2 = (s32[145]{0:T(256)S(1)}, s32[145]{0:T(256)}, u32[]{:S(2)}) copy-start(s32[145]{0:T(256)} %get-tuple-element.10.line_ref) | copy-start | bytes 1744
  12.9 20.5 %copy-start.1 = (s32[145]{0:T(256)S(1)}, s32[145]{0:T(256)}, u32[]{:S(2)}) copy-start(s32[145]{0:T(256)} %get-tuple-element.9.start_ref) | copy-start | bytes 1744
  21.2 12.1 %all-to-all-start.1 = ((bf16[8,128,128]{2,1,0:T(8,128)(2,1)}), bf16[8,128,128]{2,1,0:T(8,128)(2,1)S(1)}, u32[]{:S(2)}, u32[]{:S(2)}) async-start(bf16[8,128,128]{2,1,0:T(8,128)(2,1)} %project.1), calls=%async_computation.1 | async-start | bytes 524288 | tf_op jit(solution)/shard_map/all_to_all | solution.py:505
  25.0 1.6 %collective-permute-start = (bf16[8,144,128]{2,1,0:T(8,128)(2,1)S(1)}, bf16[8,144,128]{2,1,0:T(8,128)(2,1)S(1)}, u32[]{:S(2)}, u32[]{:S(2)}) collective-permute-start(bf16[8,144,128]{2,1,0:T(8,128)(2,1)S(1)} %all-to-all-done.own_ref.recv_ref), channel_id=1, source_target_pairs={{0,1},{1,0},{2,3},{3,2},{4,5},{5,4},{6,7},{7,6},{8,9},{9,8},{10,11... | collective-permute-start | bytes 884744 | tf_op jit(solution)/shard_map/ppermute | solution.py:477
  36.8 10.9 %all-to-all-start.2 = ((bf16[8,64,128]{2,1,0:T(8,128)(2,1)}), bf16[8,64,128]{2,1,0:T(8,128)(2,1)S(1)}, u32[]{:S(2)}, u32[]{:S(2)}) async-start(bf16[8,64,128]{2,1,0:T(8,128)(2,1)} %bitcast.3), calls=%async_computation.2 | async-start | bytes 262144 | tf_op jit(solution)/shard_map/all_to_all | solution.py:545

commit v8 on v7

--- a/solution.py
+++ b/solution.py
@@ -466,9 +466,9 @@
             pltpu.VMEM((workers, slip_rows + slots, LANES), BF16),
             pltpu.VMEM((flat.shape[0] + 2 * tall, freqs), F32),
             pltpu.VMEM((LANES, LANES), F32),
-            pltpu.SemaphoreType.DMA((4,)),
+            pltpu.SemaphoreType.DMA((8,)),
             pltpu.SemaphoreType.DMA,
-            pltpu.SemaphoreType.DMA((5,)),
+            pltpu.SemaphoreType.DMA((9,)),
         ],
         compiler_params=params(58),
         name="pack_slip",

time: 61 us -> 61.4 us (level)
  no operation moved by 1% of the time
where the time goes in v8:
time: 61.4 us; the launch traced here: 60.9 us
  Pallas kernels  25 us (41%)
  waiting for transfers between devices  19.4 us (32%)
  starting transfers between devices  14.5 us (24%)
  other arithmetic  1.14 us (2%)
  between operations  0.88 us (1%)
    pallas_call x1, Pallas kernels, per_device(): pl.pallas_call(functools.partial(synthesis_kernel, workers, tall), out_sh...  12.6 us
    all_to_all x1, starting transfers between devices, per_device(): own = lax.all_to_all(packed, 'sub', split_axis=0, concat_axis=0, tiled=True)  7.26 us
    all_to_all x1, waiting for transfers between devices, per_device(): own = lax.all_to_all(packed, 'sub', split_axis=0, concat_axis=0, tiled=True)  6.9 us
    all_to_all x1, waiting for transfers between devices, per_device(): lax.all_to_all(spectrum, 'sub', split_axis=0, concat_axis=0, tiled=True)  6.64 us
    all_to_all x1, waiting for transfers between devices, per_device(): lax.all_to_all(projected, 'sub', split_axis=0, concat_axis=0, tiled=True)  4.43 us
    all_to_all x1, starting transfers between devices, per_device(): lax.all_to_all(projected, 'sub', split_axis=0, concat_axis=0, tiled=True)  3.6 us
    all_to_all x1, starting transfers between devices, per_device(): lax.all_to_all(spectrum, 'sub', split_axis=0, concat_axis=0, tiled=True)  3.58 us
    pallas_call x1, Pallas kernels, per_device(): pl.pallas_call(functools.partial(contract_kernel, workers, tall), out_sha...  3.45 us
  transfers between devices with their start and end apart: 4, of which 4 were waited for; matrix products, arithmetic and copies ran while one was open for 2% of the time, Pallas kernels for 8%

profile of v8, /device:TPU:0, one launch (start us, length us, event | category | flops | bytes accessed | tf_op | source)
XLA Modules:
  0.0 60.9 jit_solution(16122062202897438063)
XLA Ops:
  0.6 2.6 %pack_slip.1 = bf16[8,144,128]{2,1,0:T(8,128)(2,1)} custom-call(bf16[2048,128]{1,0:T(8,128)(2,1)} %bitcast.8, f32[6,16]{1,0:T(8,128)} %bitcast.9), custom_call_target="tpu_custom_call" | custom-call | tf_op jit(solution)/shard_map/pack_slip/pallas_call | solution.py:458
  3.3 7.3 %all-to-all-start = ((bf16[8,144,128]{2,1,0:T(8,128)(2,1)}), bf16[8,144,128]{2,1,0:T(8,128)(2,1)S(1)}, u32[]{:S(2)}, u32[]{:S(2)}) async-start(bf16[8,144,128]{2,1,0:T(8,128)(2,1)} %pack_slip.1), calls=%async_computation | async-start | bytes 589824 | tf_op jit(solution)/shard_map/all_to_all | solution.py:476
  10.6 0.0 copy-start
  10.6 2.0 %choose.1 = (f32[16,128]{1,0:T(8,128)}, s32[145]{0:T(256)}, s32[145]{0:T(256)}) custom-call(s32[1,128]{1,0:T(1,128)} %bitcast.12, s32[128]{0:T(128)} %slots_ref.1, s32[8]{0:T(128)} %count_ref.1), custom_call_target="tpu_custom_call" | custom-call | flops 10000000000 | bytes 30000000 | tf_op jit(solution)/shard_map/choose/pallas_call | solution.py:478
  12.5 0.0 copy-start.2
  12.6 0.7 %convert_element_type.13.chosen_ref = bf16[16,128]{1,0:T(8,128)(2,1)S(1)} convert(f32[16,128]{1,0:T(8,128)} %get-tuple-element.11) | non-fusion elementwise | flops 2048 | bytes 12288 | tf_op jit(solution)/shard_map/convert_element_type | solution.py:490
  13.3 0.0 copy-start.1
  13.3 6.9 %all-to-all-done.own_ref.recv_ref = bf16[8,144,128]{2,1,0:T(8,128)(2,1)S(1)} async-done(((bf16[8,144,128]{2,1,0:T(8,128)(2,1)}), bf16[8,144,128]{2,1,0:T(8,128)(2,1)S(1)}, u32[]{:S(2)}, u32[]{:S(2)}) %all-to-all-start) | async-done | bytes 294944 | tf_op jit(solution)/shard_map/all_to_all | solution.py:476
  20.2 0.0 copy-done
  20.2 1.4 %project.1 = bf16[8,128,128]{2,1,0:T(8,128)(2,1)} custom-call(bf16[16,128]{1,0:T(8,128)(2,1)S(1)} %convert_element_type.13.chosen_ref, bf16[8,144,128]{2,1,0:T(8,128)(2,1)S(1)} %all-to-all-done.own_ref.recv_ref, bf16[16,2,2,6,16,128]{5,4,3,2,1,0:T(8,128)(2,1)S(1)} %copy-done), custom_call_target="tpu_custom_call" | custom-call | tf_op jit(solution)/shard_map/project/pallas_call | solution.py:491
  21.6 3.6 %all-to-all-start.1 = ((bf16[8,128,128]{2,1,0:T(8,128)(2,1)}), bf16[8,128,128]{2,1,0:T(8,128)(2,1)S(1)}, u32[]{:S(2)}, u32[]{:S(2)}) async-start(bf16[8,128,128]{2,1,0:T(8,128)(2,1)} %project.1), calls=%async_computation.1 | async-start | bytes 524288 | tf_op jit(solution)/shard_map/all_to_all | solution.py:505
  25.2 0.1 fusion.12
  25.4 0.1 collective-permute-start
  25.5 0.2 fusion.17
  25.6 1.4 %collective-permute-done.other_ref = bf16[8,144,128]{2,1,0:T(8,128)(2,1)S(1)} collective-permute-done((bf16[8,144,128]{2,1,0:T(8,128)(2,1)S(1)}, bf16[8,144,128]{2,1,0:T(8,128)(2,1)S(1)}, u32[]{:S(2)}, u32[]{:S(2)}) %collective-permute-start) | collective-permute-done | bytes 294944 | tf_op jit(solution)/shard_map/ppermute | solution.py:477
  27.0 0.0 copy-done.2
  27.0 2.3 %gather.1.spread_ref = bf16[2,5120,128]{2,1,0:T(8,128)(2,1)S(1)} custom-call(s32[145]{0:T(256)S(1)} %copy-done.2, bf16[8,144,128]{2,1,0:T(8,128)(2,1)S(1)} %all-to-all-done.own_ref.recv_ref, bf16[8,144,128]{2,1,0:T(8,128)(2,1)S(1)} %collective-permute-done.other_ref), custom_call_target="tpu_custom_call" | custom-call | tf_op jit(solution)/shard_map/gather/pallas_call | solution.py:508
  29.3 4.4 %all-to-all-done.1.proj_ref = bf16[8,128,128]{2,1,0:T(8,128)(2,1)S(1)} async-done(((bf16[8,128,128]{2,1,0:T(8,128)(2,1)}), bf16[8,128,128]{2,1,0:T(8,128)(2,1)S(1)}, u32[]{:S(2)}, u32[]{:S(2)}) %all-to-all-start.1) | async-done | bytes 262176 | tf_op jit(solution)/shard_map/all_to_all | solution.py:505
  33.7 0.0 copy-done.1
  33.7 3.4 %contract.1.ready_hbm = bf16[512,128]{1,0:T(8,128)(2,1)} custom-call(s32[145]{0:T(256)S(1)} %copy-done.1, bf16[2,5120,128]{2,1,0:T(8,128)(2,1)S(1)} %gather.1.spread_ref, bf16[8,128,128]{2,1,0:T(8,128)(2,1)S(1)} %all-to-all-done.1.proj_ref), custom_call_target="tpu_custom_call" | custom-call | tf_op jit(solution)/shard_map/contract/pallas_call | solution.py:521
  37.2 3.6 %all-to-all-start.2 = ((bf16[8,64,128]{2,1,0:T(8,128)(2,1)}), bf16[8,64,128]{2,1,0:T(8,128)(2,1)S(1)}, u32[]{:S(2)}, u32[]{:S(2)}) async-start(bf16[8,64,128]{2,1,0:T(8,128)(2,1)} %bitcast.3), calls=%async_computation.2 | async-start | bytes 262144 | tf_op jit(solution)/shard_map/all_to_all | solution.py:545
  40.8 0.1 fusion.8
  40.9 0.6 tables.1
  41.5 6.6 %all-to-all-done.2 = bf16[8,64,128]{2,1,0:T(8,128)(2,1)S(1)} async-done(((bf16[8,64,128]{2,1,0:T(8,128)(2,1)}), bf16[8,64,128]{2,1,0:T(8,128)(2,1)S(1)}, u32[]{:S(2)}, u32[]{:S(2)}) %all-to-all-start.2) | async-done | bytes 131104 | tf_op jit(solution)/shard_map/all_to_all | solution.py:545
  48.1 12.6 %synthesis.1 = (bf16[256,2048]{1,0:T(8,128)(2,1)}, f32[256,40]{1,0:T(8,128)}) custom-call(bf16[512,128]{1,0:T(8,128)(2,1)S(1)} %bitcast.7, f32[40,128]{1,0:T(8,128)S(1)} %get-tuple-element.17.gain_re_ref, f32[40,128]{1,0:T(8,128)S(1)} %get-tuple-element.16.gain_im_ref, bf16[2048,256]{1,0:T(8,128)(2,1)S(1)} %get-tuple-element.12.basis_ref, ...), custom_call_target="tpu_custom_call" | custom-call | tf_op jit(solution)/shard_map/synthesis/pallas_call | solution.py:547
  (4 shorter events, 0.0 us)
Async XLA Ops:
  3.3 16.9 %all-to-all-start = ((bf16[8,144,128]{2,1,0:T(8,128)(2,1)}), bf16[8,144,128]{2,1,0:T(8,128)(2,1)S(1)}, u32[]{:S(2)}, u32[]{:S(2)}) async-start(bf16[8,144,128]{2,1,0:T(8,128)(2,1)} %pack_slip.1), calls=%async_computation | async-start | bytes 589824 | tf_op jit(solution)/shard_map/all_to_all | solution.py:476
  10.6 9.6 %copy-start = (bf16[16,2,2,6,16,128]{5,4,3,2,1,0:T(8,128)(2,1)S(1)}, bf16[16,2,2,6,16,128]{5,4,3,2,1,0:T(8,128)(2,1)}, u32[]{:S(2)}) copy-start(bf16[16,2,2,6,16,128]{5,4,3,2,1,0:T(8,128)(2,1)} %sgt_ref.1) | copy-start | bytes 4718596
  12.5 14.5 %copy-start.2 = (s32[145]{0:T(256)S(1)}, s32[145]{0:T(256)}, u32[]{:S(2)}) copy-start(s32[145]{0:T(256)} %get-tuple-element.10.line_ref) | copy-start | bytes 1744
  13.3 20.5 %copy-start.1 = (s32[145]{0:T(256)S(1)}, s32[145]{0:T(256)}, u32[]{:S(2)}) copy-start(s32[145]{0:T(256)} %get-tuple-element.9.start_ref) | copy-start | bytes 1744
  21.6 12.1 %all-to-all-start.1 = ((bf16[8,128,128]{2,1,0:T(8,128)(2,1)}), bf16[8,128,128]{2,1,0:T(8,128)(2,1)S(1)}, u32[]{:S(2)}, u32[]{:S(2)}) async-start(bf16[8,128,128]{2,1,0:T(8,128)(2,1)} %project.1), calls=%async_computation.1 | async-start | bytes 524288 | tf_op jit(solution)/shard_map/all_to_all | solution.py:505
  25.4 1.6 %collective-permute-start = (bf16[8,144,128]{2,1,0:T(8,128)(2,1)S(1)}, bf16[8,144,128]{2,1,0:T(8,128)(2,1)S(1)}, u32[]{:S(2)}, u32[]{:S(2)}) collective-permute-start(bf16[8,144,128]{2,1,0:T(8,128)(2,1)S(1)} %all-to-all-done.own_ref.recv_ref), channel_id=1, source_target_pairs={{0,1},{1,0},{2,3},{3,2},{4,5},{5,4},{6,7},{7,6},{8,9},{9,8},{10,11... | collective-permute-start | bytes 884744 | tf_op jit(solution)/shard_map/ppermute | solution.py:477
  37.2 10.9 %all-to-all-start.2 = ((bf16[8,64,128]{2,1,0:T(8,128)(2,1)}), bf16[8,64,128]{2,1,0:T(8,128)(2,1)S(1)}, u32[]{:S(2)}, u32[]{:S(2)}) async-start(bf16[8,64,128]{2,1,0:T(8,128)(2,1)} %bitcast.3), calls=%async_computation.2 | async-start | bytes 262144 | tf_op jit(solution)/shard_map/all_to_all | solution.py:545
